TPU v7x, 128 devices: a whole 4x4x4 slice. The times are simulated.
128 devices in a mesh: ctx: 16 (over y_lo, z, core), fsdp: 8 (over x, y_hi).
Axes of the slice: x: 4, y: 4 (y_hi: 2, y_lo: 2; y = y_hi * 2 + y_lo), z: 4, core: 2. Of those that a mesh axis runs over, the one named last changes fastest.
Arguments:
- tokens: bfloat16 [2, 8, 2048, 1024], P(None, 'fsdp', 'ctx')
- cotangent: bfloat16 [2, 8, 2048, 1024], P(None, 'fsdp', 'ctx')
- dest: int32 [2, 8, 2048], P(None, 'fsdp', 'ctx'), may hold values from 0 to 2047, as said below
- lengths: int32 [2, 8, 8], P(None, 'fsdp'), may hold values from 1 to 1024, as said below
- attn_weight: float32 [1024, 4096], P('fsdp')
- attn_first: float32 [1024, 4096], P('fsdp'), may hold values from -0.00048828125 to 0.00048828125
- attn_second: float32 [1024, 4096], P('fsdp'), may hold values from 7.9395324e-11 to 3.175813e-10
- ffn_weight: float32 [1024, 8192], P('fsdp')
- ffn_first: float32 [1024, 8192], P('fsdp'), may hold values from -0.00048828125 to 0.00048828125
- ffn_second: float32 [1024, 8192], P('fsdp'), may hold values from 7.9395324e-11 to 3.175813e-10
- vectors: float32 [12, 1024], P(None, 'fsdp')
- vec_first: float32 [12, 1024], P(None, 'fsdp'), may hold values from -0.0048828125 to 0.0048828125
- vec_second: float32 [12, 1024], P(None, 'fsdp'), may hold values from 2.3818598e-09 to 9.527439e-09
Outputs:
- layer_output: bfloat16 [2, 8, 2048, 1024], P(None, 'fsdp', 'ctx')
- input_grad: bfloat16 [2, 8, 2048, 1024], P(None, 'fsdp', 'ctx')
- grad_norm: float32 [], replicated
- attn_new: float32 [1024, 4096], P('fsdp')
- attn_first_new: float32 [1024, 4096], P('fsdp')
- attn_second_new: float32 [1024, 4096], P('fsdp')
- ffn_new: float32 [1024, 8192], P('fsdp')
- ffn_first_new: float32 [1024, 8192], P('fsdp')
- ffn_second_new: float32 [1024, 8192], P('fsdp')
- vec_new: float32 [12, 1024], P(None, 'fsdp')
- vec_first_new: float32 [12, 1024], P(None, 'fsdp')
- vec_second_new: float32 [12, 1024], P(None, 'fsdp')
- attn_copy: bfloat16 [1024, 4096], P('fsdp')
- ffn_copy: bfloat16 [1024, 8192], P('fsdp')
- output_bias_grad: float32 [1024], P('fsdp')
Inputs may be any that keep to these rules, and one draw needn't show every extreme that they name: Within each micro-batch and fsdp index, dest is a permutation of the pack's slots; slot s lies on ctx device s // 128, and each ctx device's given tokens go exactly 8 to each ctx device. The lengths of a pack sum to at most 2048; one of them is exactly 1024; sequences fill the packed slots in order and the rest is padding.
All inputs are finite; a program needn't handle non-finite values.
Results may differ from a plain program's by a relative error of at most 0.03.
Values may be sent and summed in bfloat16 or wider, within the bound.
A program may use at most 320 MiB of HBM per device.

v0:
```python
from functools import partial

import jax
import jax.numpy as jnp
from jax import lax
from jax.sharding import PartitionSpec as P

HEADS = 16
STEP = 10


NORM_EPS = 1e-05
CLIP_NORM = 1.0
BETA_FIRST = 0.9
BETA_SECOND = 0.999
ADAM_EPS = 1e-08
WEIGHT_DECAY = 0.01
RATE_VECTOR = 0.3
ATTN_RATE_SCALE = 3.0
NEG_LARGE = -1e30
CONTRACT_ROWS = (((0,), (0,)), ((), ()))
CONTRACT_COLS = (((1,), (1,)), ((), ()))


def in_one_piece(arrays, axis, split_dim, concat_dim, along):
    both = jnp.concatenate(arrays, axis=along)
    whole, at, outs = (
        lax.all_to_all(both, axis, split_axis=split_dim, concat_axis=concat_dim, tiled=True),
        0,
        [],
    )
    for a in arrays:
        outs.append(lax.slice_in_dim(whole, at, at + a.shape[along], axis=along))
        at += a.shape[along]
    return tuple(outs)


def in_one_piece_2(arrays, axis, dim, along):
    both = jnp.concatenate(arrays, axis=along)
    whole, at, outs = (lax.all_gather(both, axis, axis=dim, tiled=True), 0, [])
    for a in arrays:
        outs.append(lax.slice_in_dim(whole, at, at + a.shape[along], axis=along))
        at += a.shape[along]
    return tuple(outs)


def sent_to_all(value, axis):
    devices = lax.axis_size(axis)
    return lax.all_to_all(
        jnp.broadcast_to(value[None], (devices, *value.shape)), axis, 0, 0, tiled=True
    )


def taken_together(value, axis):
    everything = sent_to_all(value, axis)
    return jnp.sum(everything, axis=0)


def layer_stats(values, gain_row, shift_row):
    center = values - jnp.mean(values, axis=-1, keepdims=True)
    inverse = lax.rsqrt(jnp.mean(center * center, axis=-1, keepdims=True) + NORM_EPS)
    normal = center * inverse
    return (normal * gain_row + shift_row, normal, inverse)


def layer_back(grad_value, normal, inverse, gain_row):
    scaled = grad_value * gain_row
    return inverse * (
        scaled
        - jnp.mean(scaled, axis=-1, keepdims=True)
        - normal * jnp.mean(scaled * normal, axis=-1, keepdims=True)
    )


def seg_of_pack(lengths_row, pack_len):
    ends = jnp.cumsum(lengths_row)
    slots = jnp.arange(pack_len, dtype=jnp.int32)
    return jnp.sum((slots[:, None] >= ends[None, :]).astype(jnp.int32), axis=1)


def column_sum(values):
    return jnp.sum(values.astype(jnp.float32), axis=0)


def adamw(weight, grad_value, first, second, rate, decay):
    first_new = BETA_FIRST * first + (1.0 - BETA_FIRST) * grad_value
    second_new = BETA_SECOND * second + (1.0 - BETA_SECOND) * grad_value * grad_value
    first_hat = first_new / (1.0 - BETA_FIRST**STEP)
    second_hat = second_new / (1.0 - BETA_SECOND**STEP)
    weight_new = weight - rate * (first_hat / (jnp.sqrt(second_hat) + ADAM_EPS) + decay * weight)
    return (weight_new, first_new, second_new)


def shards(
    tokens,
    cotangent,
    dest,
    lengths,
    attn_weight,
    attn_first,
    attn_second,
    ffn_weight,
    ffn_first,
    ffn_second,
    vectors,
    vec_first,
    vec_second,
):
    micro_count = tokens.shape[0]
    row_count = tokens.shape[2]
    model_width = tokens.shape[3]
    hidden_units = ffn_weight.shape[1] // 2
    seq_slots = lengths.shape[2]
    head_size = model_width // HEADS
    groups = lax.axis_size("ctx")
    place_index = lax.axis_index("ctx")
    pack_len = row_count * groups
    scale_factor = head_size ** (-0.5)
    send_attn = attn_weight.astype(jnp.bfloat16)
    send_ffn = ffn_weight.astype(jnp.bfloat16)
    send_vec = vectors.astype(jnp.bfloat16)
    acc_attn = jnp.zeros((model_width, 4 * model_width), jnp.float32)
    acc_ffn = jnp.zeros((model_width, 2 * hidden_units), jnp.float32)
    acc_vec = jnp.zeros((vectors.shape[0], model_width), jnp.float32)
    outs_output = []
    outs_grad = []
    for micro_index in range(micro_count):
        full_attn, full_ffn, full_vec = (
            lax.all_gather(send_attn, "fsdp", axis=0, tiled=True),
            lax.all_gather(send_ffn, "fsdp", axis=0, tiled=True),
            lax.all_gather(send_vec, "fsdp", axis=1, tiled=True),
        )
        small_rows = full_vec.astype(jnp.float32)
        dest_rows = dest[micro_index, 0]
        send_order = jnp.argsort(dest_rows)
        sent_tokens = tokens[micro_index, 0][send_order]
        sent_cot = cotangent[micro_index, 0][send_order]
        sent_dest = dest_rows[send_order]
        recv_tokens, recv_cot, recv_dest = (
            *in_one_piece((sent_tokens, sent_cot), "ctx", 0, 0, 1),
            lax.all_to_all(sent_dest, "ctx", split_axis=0, concat_axis=0, tiled=True),
        )
        local_slot = recv_dest - place_index * row_count
        placing = jnp.argsort(local_slot)
        token_rows = recv_tokens[placing]
        cot_rows = recv_cot[placing].astype(jnp.float32)
        seg_all = seg_of_pack(lengths[micro_index, 0], pack_len)
        seg_own = lax.dynamic_slice_in_dim(seg_all, place_index * row_count, row_count)
        keep_rows = (seg_own < seq_slots).astype(jnp.float32)[:, None]
        same_segment = (seg_own[:, None] == seg_all[None, :])[None]
        projected = jnp.dot(
            token_rows, full_attn[:, : 3 * model_width], preferred_element_type=jnp.float32
        )
        queries = (projected[:, :model_width] + small_rows[0]).astype(jnp.bfloat16)
        key_rows = projected[:, model_width : 2 * model_width].astype(jnp.bfloat16)
        value_rows = (projected[:, 2 * model_width :] + small_rows[1]).astype(jnp.bfloat16)
        all_keys, all_values = in_one_piece_2((key_rows, value_rows), "ctx", 0, 1)
        query_heads = queries.reshape(row_count, HEADS, head_size)
        key_heads = all_keys.reshape(pack_len, HEADS, head_size)
        value_heads = all_values.reshape(pack_len, HEADS, head_size)
        scores = (
            jnp.einsum("qhd,khd->hqk", query_heads, key_heads, preferred_element_type=jnp.float32)
            * scale_factor
        )
        masked = jnp.where(same_segment, scores, NEG_LARGE)
        row_max = jnp.max(masked, axis=-1, keepdims=True)
        exp_scores = jnp.exp(masked - row_max)
        exp_total = jnp.sum(exp_scores, axis=-1, keepdims=True)
        log_total = row_max + jnp.log(exp_total)
        prob_low = (exp_scores / exp_total).astype(jnp.bfloat16)
        mixed = (
            jnp.einsum("hqk,khd->qhd", prob_low, value_heads, preferred_element_type=jnp.float32)
            .reshape(row_count, model_width)
            .astype(jnp.bfloat16)
        )
        branch = (
            jnp.dot(mixed, full_attn[:, 3 * model_width :], preferred_element_type=jnp.float32)
            + small_rows[2]
        )
        normed_one, normal_one, inverse_one = layer_stats(
            token_rows.astype(jnp.float32) + branch, small_rows[4], small_rows[5]
        )
        normed_low = normed_one.astype(jnp.bfloat16)
        hidden_pre = jnp.dot(
            normed_low, full_ffn[:, :hidden_units], preferred_element_type=jnp.float32
        ) + small_rows[8:].reshape(hidden_units)
        activ, gelu_back = jax.vjp(partial(jax.nn.gelu, approximate=False), hidden_pre)
        activ_low = activ.astype(jnp.bfloat16)
        ffn_out = (
            lax.dot_general(
                activ_low,
                full_ffn[:, hidden_units:],
                CONTRACT_COLS,
                preferred_element_type=jnp.float32,
            )
            + small_rows[3]
        )
        output, normal_two, inverse_two = layer_stats(
            normed_one + ffn_out, small_rows[6], small_rows[7]
        )
        output = output * keep_rows
        grad_out = cot_rows * keep_rows
        grad_two = layer_back(grad_out, normal_two, inverse_two, small_rows[6])
        ffn_grad_low = grad_two.astype(jnp.bfloat16)
        grad_activ = jnp.dot(
            ffn_grad_low, full_ffn[:, hidden_units:], preferred_element_type=jnp.float32
        )
        grad_hidden = gelu_back(grad_activ)[0].astype(jnp.bfloat16)
        grad_normed = (
            lax.dot_general(
                grad_hidden,
                full_ffn[:, :hidden_units],
                CONTRACT_COLS,
                preferred_element_type=jnp.float32,
            )
            + grad_two
        )
        grad_one = layer_back(grad_normed, normal_one, inverse_one, small_rows[4])
        branch_grad_low = grad_one.astype(jnp.bfloat16)
        grad_mixed = lax.dot_general(
            branch_grad_low,
            full_attn[:, 3 * model_width :],
            CONTRACT_COLS,
            preferred_element_type=jnp.float32,
        ).astype(jnp.bfloat16)
        grad_mixed_heads = grad_mixed.reshape(row_count, HEADS, head_size)
        scores_again = (
            jnp.einsum("qhd,khd->hqk", query_heads, key_heads, preferred_element_type=jnp.float32)
            * scale_factor
        )
        attn_prob = jnp.exp(jnp.where(same_segment, scores_again, NEG_LARGE) - log_total)
        grad_prob = jnp.einsum(
            "qhd,khd->hqk", grad_mixed_heads, value_heads, preferred_element_type=jnp.float32
        )
        delta_rows = jnp.sum(attn_prob * grad_prob, axis=-1)
        grad_scores = attn_prob * (grad_prob - delta_rows[:, :, None])
        score_grad_low = grad_scores.astype(jnp.bfloat16)
        grad_queries = (
            (
                jnp.einsum(
                    "hqk,khd->qhd", score_grad_low, key_heads, preferred_element_type=jnp.float32
                )
                * scale_factor
            )
            .reshape(row_count, model_width)
            .astype(jnp.bfloat16)
        )
        prob_again = attn_prob.astype(jnp.bfloat16)
        key_term = (
            jnp.einsum(
                "hqk,qhd->khd", score_grad_low, query_heads, preferred_element_type=jnp.float32
            )
            * scale_factor
        )
        value_term = jnp.einsum(
            "hqk,qhd->khd", prob_again, grad_mixed_heads, preferred_element_type=jnp.float32
        )
        kv_sums = lax.psum_scatter(
            jnp.concatenate(
                [
                    key_term.reshape(row_count * lax.axis_size("ctx"), model_width),
                    value_term.reshape(row_count * lax.axis_size("ctx"), model_width),
                ],
                axis=1,
            ).astype(jnp.bfloat16),
            "ctx",
            scatter_dimension=0,
            tiled=True,
        ).astype(jnp.float32)
        grad_keys = kv_sums[:, :model_width].astype(jnp.bfloat16)
        grad_values = kv_sums[:, model_width:].astype(jnp.bfloat16)
        grad_qkv = jnp.concatenate([grad_queries, grad_keys, grad_values], axis=1)
        grad_tokens = grad_one + lax.dot_general(
            grad_qkv,
            full_attn[:, : 3 * model_width],
            CONTRACT_COLS,
            preferred_element_type=jnp.float32,
        )
        grad_in_proj = lax.dot_general(
            token_rows, grad_qkv, CONTRACT_ROWS, preferred_element_type=jnp.float32
        )
        grad_out_proj = lax.dot_general(
            mixed, branch_grad_low, CONTRACT_ROWS, preferred_element_type=jnp.float32
        )
        grad_first_proj = lax.dot_general(
            normed_low, grad_hidden, CONTRACT_ROWS, preferred_element_type=jnp.float32
        )
        grad_second_proj = lax.dot_general(
            ffn_grad_low, activ_low, CONTRACT_ROWS, preferred_element_type=jnp.float32
        )
        vector_rows = jnp.stack(
            [
                column_sum(grad_queries),
                column_sum(grad_values),
                column_sum(branch_grad_low),
                column_sum(ffn_grad_low),
                jnp.sum(grad_normed * normal_one, axis=0),
                jnp.sum(grad_normed, axis=0),
                jnp.sum(grad_out * normal_two, axis=0),
                jnp.sum(grad_out, axis=0),
            ]
        )
        step_vec = jnp.concatenate(
            [vector_rows, column_sum(grad_hidden).reshape(4, model_width)], axis=0
        )
        step_attn = jnp.concatenate([grad_in_proj, grad_out_proj], axis=1)
        step_ffn = jnp.concatenate([grad_first_proj, grad_second_proj], axis=1)
        acc_attn = acc_attn + step_attn
        acc_ffn = acc_ffn + step_ffn
        acc_vec = acc_vec + step_vec
        back_output = output.astype(jnp.bfloat16)[local_slot]
        back_grad = grad_tokens.astype(jnp.bfloat16)[local_slot]
        ret_output, ret_grad = (
            lax.all_to_all(back_output, "ctx", split_axis=0, concat_axis=0, tiled=True),
            lax.all_to_all(back_grad, "ctx", split_axis=0, concat_axis=0, tiled=True),
        )
        restore = jnp.argsort(send_order)
        outs_output.append(ret_output[restore])
        outs_grad.append(ret_grad[restore])
    shares = (
        lax.psum_scatter(
            acc_attn.astype(jnp.bfloat16), "fsdp", scatter_dimension=0, tiled=True
        ).astype(jnp.float32),
        lax.psum_scatter(
            acc_ffn.astype(jnp.bfloat16), "fsdp", scatter_dimension=0, tiled=True
        ).astype(jnp.float32),
        lax.psum_scatter(
            acc_vec.astype(jnp.bfloat16), "fsdp", scatter_dimension=1, tiled=True
        ).astype(jnp.float32),
    )
    total_attn, total_ffn, total_vec = (
        lax.psum(shares[0].astype(jnp.bfloat16), "ctx").astype(jnp.float32),
        lax.psum(shares[1].astype(jnp.bfloat16), "ctx").astype(jnp.float32),
        lax.psum(shares[2].astype(jnp.bfloat16), "ctx").astype(jnp.float32),
    )
    local_square = (
        jnp.sum(total_attn * total_attn)
        + jnp.sum(total_ffn * total_ffn)
        + jnp.sum(total_vec * total_vec)
    )
    grad_norm = jnp.sqrt(taken_together(local_square, "fsdp"))
    factor = jnp.minimum(1.0, CLIP_NORM / (grad_norm + 1e-06))
    rate_matrix = model_width ** (-0.5)
    attn_new, attn_first_new, attn_second_new = adamw(
        attn_weight,
        total_attn * factor,
        attn_first,
        attn_second,
        ATTN_RATE_SCALE * rate_matrix,
        WEIGHT_DECAY,
    )
    ffn_new, ffn_first_new, ffn_second_new = adamw(
        ffn_weight, total_ffn * factor, ffn_first, ffn_second, rate_matrix, WEIGHT_DECAY
    )
    vec_new, vec_first_new, vec_second_new = adamw(
        vectors, total_vec * factor, vec_first, vec_second, RATE_VECTOR, 0.0
    )
    output_bias_grad = total_vec[2] * factor
    layer_output = jnp.stack(outs_output)[:, None]
    input_grad = jnp.stack(outs_grad)[:, None]
    return (
        layer_output,
        input_grad,
        grad_norm,
        attn_new,
        attn_first_new,
        attn_second_new,
        ffn_new,
        ffn_first_new,
        ffn_second_new,
        vec_new,
        vec_first_new,
        vec_second_new,
        attn_new.astype(jnp.bfloat16),
        ffn_new.astype(jnp.bfloat16),
        output_bias_grad,
    )


def solution(mesh):
    return jax.shard_map(
        shards,
        mesh=mesh,
        in_specs=(
            P(None, "fsdp", "ctx", None),
            P(None, "fsdp", "ctx", None),
            P(None, "fsdp", "ctx"),
            P(None, "fsdp", None),
            P("fsdp", None),
            P("fsdp", None),
            P("fsdp", None),
            P("fsdp", None),
            P("fsdp", None),
            P("fsdp", None),
            P(None, "fsdp"),
            P(None, "fsdp"),
            P(None, "fsdp"),
        ),
        out_specs=(
            P(None, "fsdp", "ctx", None),
            P(None, "fsdp", "ctx", None),
            P(),
            P("fsdp", None),
            P("fsdp", None),
            P("fsdp", None),
            P("fsdp", None),
            P("fsdp", None),
            P("fsdp", None),
            P(None, "fsdp"),
            P(None, "fsdp"),
            P(None, "fsdp"),
            P("fsdp", None),
            P("fsdp", None),
            P("fsdp"),
        ),
        check_vma=False,
    )
```

profile of v0, /device:TPU:1, one launch (start us, length us, event | category | flops | bytes accessed | tf_op | source)
XLA Modules:
  0.0 1316.5 jit_solution(4969138439860393196)
XLA Ops:
  14.5 7.8 all-to-all-start.1
  32.6 5.7 all-to-all-start.4
  38.4 25.3 %all_gather.19 = bf16[12,1024]{1,0:T(8,128)(2,1)S(1)} all-gather(bf16[12,128]{1,0:T(8,128)(2,1)S(1)} %convert_element_type.231), channel_id=1, replica_groups=mesh['ctx'=16,'fsdp'=8] {'fsdp'}, dimensions={1}, use_global_device_ids=true | all-gather | bytes 27648 | tf_op jit(solution)/shard_map/all_gather | solution.py:131
  63.6 10.6 all-to-all-start.3
  81.9 8.4 all-to-all-done.3
  90.3 4.2 all-to-all-start
  95.5 15.2 %all-to-all-done = bf16[16,8,2048]{2,1,0:T(8,128)(2,1)S(1)} async-done(((bf16[16,8,2048]{2,1,0:T(8,128)(2,1)}), bf16[16,8,2048]{2,1,0:T(8,128)(2,1)S(1)}, u32[]{:S(2)}, u32[]{:S(2)}) %all-to-all-start) | async-done | bytes 524320 | tf_op jit(solution)/shard_map/all_to_all | solution.py:28
  111.5 22.5 %all-gather.5.cloned.1.call-done = bf16[1024,4096]{1,0:T(8,128)(2,1)} async-done(((bf16[128,4096]{1,0:T(8,128)(2,1)}), bf16[1024,4096]{1,0:T(8,128)(2,1)}) %all-gather.5.cloned.1.call-update) | async-done | bytes 8388624 | tf_op jit(solution)/shard_map/all_gather | solution.py:129
  150.7 42.5 %all-gather.7.cloned.1.call-done = bf16[2048,2048]{1,0:T(8,128)(2,1)} async-done(((bf16[128,2048]{1,0:T(8,128)(2,1)}), bf16[2048,2048]{1,0:T(8,128)(2,1)}) %all-gather.7.cloned.1.call-update) | async-done | bytes 8388624 | tf_op jit(solution)/shard_map/all_gather | solution.py:40
  193.2 6.2 fusion.183
  199.4 6.4 copy.89
  205.8 6.8 copy.91
  212.6 10.9 fusion.188
  223.5 8.2 fusion.2
  231.8 10.5 fusion.133
  244.8 137.4 %all-gather.9.cloned.1.call-done = bf16[1024,8192]{1,0:T(8,128)(2,1)} async-done(((bf16[128,8192]{1,0:T(8,128)(2,1)}), bf16[1024,8192]{1,0:T(8,128)(2,1)}) %all-gather.9.cloned.1.call-update) | async-done | bytes 16777232 | tf_op jit(solution)/shard_map/all_gather | solution.py:130
  382.2 4.7 fusion.31
  387.0 9.4 fusion.190
  396.6 38.7 %all-gather.11.cloned.1.call-done = bf16[2048,2048]{1,0:T(8,128)(2,1)} async-done(((bf16[128,2048]{1,0:T(8,128)(2,1)}), bf16[2048,2048]{1,0:T(8,128)(2,1)}) %all-gather.11.cloned.1.call-update) | async-done | bytes 8388624 | tf_op jit(solution)/shard_map/all_gather | solution.py:40
  435.3 6.0 fusion.184
  441.3 6.5 copy.93
  447.8 6.7 copy.95
  454.5 10.9 fusion.191
  465.4 8.1 fusion.3
  473.6 10.2 fusion.132
  486.3 4.9 fusion.34
  491.2 10.4 fusion.193
  505.0 6.9 convert_reduce_fusion.1
  515.6 6.9 convert_reduce_fusion
  529.5 11.0 fusion.48
  540.6 10.9 multiply_reduce_fusion.1
  551.5 11.8 multiply_convert_fusion.1
  567.8 8.3 pad_maximum_fusion
  576.2 12.3 copy.105
  592.8 14.0 %multiply_reduce_fusion = (f32[16,128]{1,0:T(8,128)S(1)}, f32[16,128,2048]{2,1,0:T(8,128)}) fusion(f32[16,128,2048]{2,1,0:T(8,128)} %get-tuple-element.197, f32[16,128]{1,0:T(8,128)S(1)} %log_add_fusion, bf16[128,16,64]{0,2,1:T(8,128)(2,1)S(1)} %bitcast.175, bf16[2048,16,64]{0,2,1:T(8,128)(2,1)} %bitcast.168), kind=kOutput, calls=%fused_computation.23 | convolution fusion | flops 549451776 | bytes 38027264 | tf_op jit(solution)/shard_map/qhd,khd->hqk/dot_general | solution.py:232
  606.9 12.8 multiply_convert_fusion
  619.7 4.3 copy-done.1
  627.3 5.6 fusion.51
  632.9 8.5 pad_maximum_fusion.1
  641.4 12.3 copy.107
  660.4 6.6 convert_reduce_fusion.5
  671.6 6.4 fusion.145
  678.0 57.8 %reduce-scatter.18.cloned.1.call-done = bf16[128,2048]{1,0:T(8,128)(2,1)} async-done(((bf16[2048,2048]{1,0:T(8,128)(2,1)}), bf16[128,2048]{1,0:T(8,128)(2,1)}) %reduce-scatter.18.cloned.1.call-update) | async-done | bytes 524304
  737.2 8.1 fusion.144
  746.0 10.7 fusion.1
  760.4 8.7 fusion.168
  769.2 9.0 fusion.165
  778.2 9.0 fusion.159
  787.2 23.8 %fusion = bf16[1024,8192]{1,0:T(8,128)(2,1)} fusion(f32[1024,4096]{1,0:T(8,128)} %fusion.165, f32[1024,4096]{1,0:T(8,128)S(1)} %fusion.171, f32[1024,4096]{1,0:T(8,128)} %fusion.159, f32[1024,4096]{1,0:T(8,128)} %fusion.168), kind=kLoop, calls=%fused_computation.19 | loop fusion | flops 33554432 | bytes 83886080 | tf_op jit(solution)/shard_map/convert_element_type | solution.py:325
  813.6 59.5 %reduce-scatter.12.cloned.1.call-done = bf16[128,4096]{1,0:T(8,128)(2,1)} async-done(((bf16[1024,4096]{1,0:T(8,128)(2,1)}), bf16[128,4096]{1,0:T(8,128)(2,1)}) %reduce-scatter.12.cloned.1.call-update) | async-done | bytes 1048592 | tf_op jit(solution)/shard_map/reduce_scatter | solution.py:321
  873.1 192.2 %reduce-scatter.14.cloned.1.call-done = bf16[128,8192]{1,0:T(8,128)(2,1)} async-done(((bf16[1024,8192]{1,0:T(8,128)(2,1)}), bf16[128,8192]{1,0:T(8,128)(2,1)}) %reduce-scatter.14.cloned.1.call-update) | async-done | bytes 2097168 | tf_op jit(solution)/shard_map/reduce_scatter | solution.py:324
  1072.2 8.9 all-to-all-start.5
  1082.7 5.7 all-to-all-done.5
  1088.4 4.3 all-to-all-start.2
  1092.7 5.0 fusion.120
  1100.0 5.1 all-to-all-start.7
  1105.2 5.0 fusion.123
  1112.4 5.1 all-to-all-start.6
  1120.1 20.1 %reduce-scatter.20.cloned.1.call-done = bf16[128,12]{1,0:T(8,128)(2,1)} async-done(((bf16[1024,12]{1,0:T(8,128)(2,1)}), bf16[128,12]{1,0:T(8,128)(2,1)}) %reduce-scatter.20.cloned.1.call-update) | async-done | bytes 3088
  1141.0 29.1 %psum.23 = bf16[12,128]{1,0:T(8,128)(2,1)S(1)} all-reduce(bf16[12,128]{1,0:T(8,128)(2,1)S(1)} %copy.110), channel_id=1, replica_groups=mesh['ctx'=16,'fsdp'=8] {'ctx'}, use_global_device_ids=true, to_apply=%region_59.60 | all-reduce | flops 1536 | bytes 6144 | tf_op jit(solution)/shard_map/psum | solution.py:334
  1173.3 96.6 %all-reduce.3.cloned.1.call-done = (bf16[128,4096]{1,0:T(8,128)(2,1)}, bf16[128,8192]{1,0:T(8,128)(2,1)}) async-done(((bf16[128,4096]{1,0:T(8,128)(2,1)}, bf16[128,8192]{1,0:T(8,128)(2,1)}), (bf16[128,4096]{1,0:T(8,128)(2,1)}, bf16[128,8192]{1,0:T(8,128)(2,1)})) %all-reduce.3.cloned.1.call-update) | async-done | bytes 3145744 | tf_op jit(solution)/shard_map/psum | solution.py:332
  1277.6 12.7 all_to_all.96
  1292.2 6.8 fusion.177
  1301.3 6.4 fusion.174
  (389 shorter events, 123.2 us)
Async XLA Ops:
  7.2 15.2 %copy-start.43 = (bf16[2,1,128,1024]{3,2,1,0:T(8,128)(2,1)S(1)}, bf16[2,1,128,1024]{3,2,1,0:T(8,128)(2,1)}, u32[]{:S(2)}) copy-start(bf16[2,1,128,1024]{3,2,1,0:T(8,128)(2,1)} %param.14) | copy-start | bytes 1572868
  7.2 126.9 %all-gather.5.cloned.1.call-start = ((), (), s32[]{:S(2)}) async-start(), calls=%async_computation.14 | async-start | bytes 9437184 | tf_op jit(solution)/shard_map/all_gather | solution.py:129
  10.0 13.3 %copy-start.44 = (bf16[2,1,128,1024]{3,2,1,0:T(8,128)(2,1)S(1)}, bf16[2,1,128,1024]{3,2,1,0:T(8,128)(2,1)}, u32[]{:S(2)}) copy-start(bf16[2,1,128,1024]{3,2,1,0:T(8,128)(2,1)} %param.13) | copy-start | bytes 1572868
  14.5 18.1 %all-to-all-start.1 = ((s32[16,8,1]{1,2,0:T(1,128)}), s32[16,8,1]{1,2,0:T(1,128)S(1)}, u32[]{:S(2)}, u32[]{:S(2)}) async-start(s32[16,8,1]{1,2,0:T(1,128)} %bitcast.5), calls=%async_computation.1 | async-start | bytes 16384 | tf_op jit(solution)/shard_map/all_to_all | solution.py:141
  32.6 31.0 %all-to-all-start.4 = ((s32[16,8,1]{1,2,0:T(1,128)}), s32[16,8,1]{1,2,0:T(1,128)S(1)}, u32[]{:S(2)}, u32[]{:S(2)}) async-start(s32[16,8,1]{1,2,0:T(1,128)} %bitcast.30), calls=%async_computation.4 | async-start | bytes 16384 | tf_op jit(solution)/shard_map/all_to_all | solution.py:141
  63.6 26.6 %all-to-all-start.3 = ((bf16[16,8,2048]{2,1,0:T(8,128)(2,1)}), bf16[16,8,2048]{2,1,0:T(8,128)(2,1)S(1)}, u32[]{:S(2)}, u32[]{:S(2)}) async-start(bf16[16,8,2048]{2,1,0:T(8,128)(2,1)} %maximum_bitcast_fusion.1), calls=%async_computation.3 | async-start | bytes 1048576 | tf_op jit(solution)/shard_map/all_to_all | solution.py:28
  74.8 416.3 %copy-start.49 = (f32[1,1024]{1,0:T(1,128)}, f32[1,1024]{1,0:T(1,128)S(1)}, u32[]{:S(2)}) copy-start(f32[1,1024]{1,0:T(1,128)S(1)} %get-tuple-element.168) | copy-start | bytes 12292
  90.3 20.3 %all-to-all-start = ((bf16[16,8,2048]{2,1,0:T(8,128)(2,1)}), bf16[16,8,2048]{2,1,0:T(8,128)(2,1)S(1)}, u32[]{:S(2)}, u32[]{:S(2)}) async-start(bf16[16,8,2048]{2,1,0:T(8,128)(2,1)} %maximum_bitcast_fusion), calls=%async_computation | async-start | bytes 1048576 | tf_op jit(solution)/shard_map/all_to_all | solution.py:28
  94.5 98.7 %all-gather.7.cloned.1.call-start = ((), (), s32[]{:S(2)}) async-start(), calls=%async_computation.15 | async-start | bytes 8912896 | tf_op jit(solution)/shard_map/all_gather | solution.py:40
  95.5 388.3 %copy-start.19 = (bf16[128,1024]{1,0:T(8,128)(2,1)}, bf16[128,1024]{1,0:T(8,128)(2,1)S(1)}, u32[]{:S(2)}) copy-start(bf16[128,1024]{1,0:T(8,128)(2,1)S(1)} %gather_fusion.9) | copy-start | bytes 786436
  111.5 130.8 %copy-start.21 = (bf16[128,1024]{1,0:T(8,128)(2,1)}, bf16[128,1024]{1,0:T(8,128)(2,1)S(1)}, u32[]{:S(2)}) copy-start(bf16[128,1024]{1,0:T(8,128)(2,1)S(1)} %gather_fusion.3) | copy-start | bytes 786436
  142.1 240.1 %all-gather.9.cloned.1.call-start = ((), (), s32[]{:S(2)}) async-start(), calls=%async_computation.16 | async-start | bytes 18874368 | tf_op jit(solution)/shard_map/all_gather | solution.py:130
  145.9 289.3 %all-gather.11.cloned.1.call-start = ((), (), s32[]{:S(2)}) async-start(), calls=%async_computation.17 | async-start | bytes 8912896 | tf_op jit(solution)/shard_map/all_gather | solution.py:40
  146.9 523.3 %reduce-scatter.16.cloned.1.call-start = ((), (), s32[]{:S(2)}) async-start(), calls=%async_computation.20 | async-start | bytes 8912896
  147.0 235.2 %copy-start.66 = (f32[1,8,4,128]{3,1,2,0:T(8,128)}, f32[1,8,4,128]{3,1,2,0:T(8,128)S(1)}, u32[]{:S(2)}) copy-start(f32[1,8,4,128]{3,1,2,0:T(8,128)S(1)} %copy.114) | copy-start | bytes 49156
  150.5 62.1 %copy-start.16 = (bf16[128,1024]{0,1:T(8,128)(2,1)}, bf16[128,1024]{0,1:T(8,128)(2,1)S(1)}, u32[]{:S(2)}) copy-start(bf16[128,1024]{0,1:T(8,128)(2,1)S(1)} %copy.90) | copy-start | bytes 786436
  150.7 303.8 %copy-start.14 = (bf16[128,1024]{0,1:T(8,128)(2,1)}, bf16[128,1024]{0,1:T(8,128)(2,1)S(1)}, u32[]{:S(2)}) copy-start(bf16[128,1024]{0,1:T(8,128)(2,1)S(1)} %copy.94) | copy-start | bytes 786436
  231.7 10.6 copy-start.51
  242.3 144.7 %copy-start.32 = (bf16[16,64,128]{2,1,0:T(8,128)(2,1)}, bf16[16,64,128]{2,1,0:T(8,128)(2,1)S(1)}, u32[]{:S(2)}) copy-start(bf16[16,64,128]{2,1,0:T(8,128)(2,1)S(1)} %fusion.133) | copy-start | bytes 786436
  244.5 278.0 %copy-start.76 = (f32[128]{0:T(128)}, f32[128]{0:T(128)S(1)}, u32[]{:S(2)}) copy-start(f32[128]{0:T(128)S(1)} %broadcast_multiply_fusion.11) | copy-start | bytes 1540
  244.7 277.8 %copy-start.84 = (f32[128]{0:T(128)}, f32[128]{0:T(128)S(1)}, u32[]{:S(2)}) copy-start(f32[128]{0:T(128)S(1)} %add_rsqrt_fusion.3) | copy-start | bytes 1540
  386.9 9.4 copy-start.92
  486.0 102.6 %copy-start.70 = (f32[128]{0:T(128)}, f32[128]{0:T(128)S(1)}, u32[]{:S(2)}) copy-start(f32[128]{0:T(128)S(1)} %broadcast_multiply_fusion.9) | copy-start | bytes 1540
  486.3 102.3 %copy-start.72 = (f32[128]{0:T(128)}, f32[128]{0:T(128)S(1)}, u32[]{:S(2)}) copy-start(f32[128]{0:T(128)S(1)} %add_rsqrt_fusion.1) | copy-start | bytes 1540
  486.3 18.7 %slice-start.6 = ((s8[16777216]{0:T(1024)(128)(4,1)}), s8[4194304]{0:T(1024)(128)(4,1)S(1)}, s32[]{:S(2)}) async-start(s8[16777216]{0:T(1024)(128)(4,1)} %bitcast.239), calls=%async_computation.30 | async-start | bytes 8388608
  491.2 24.5 %copy-start.95 = (f32[128,4096]{1,0:T(8,128)}, f32[128,4096]{1,0:T(8,128)S(1)}, u32[]{:S(2)}) copy-start(f32[128,4096]{1,0:T(8,128)S(1)} %fusion.34) | copy-start | bytes 6291460
  491.2 10.7 copy-start.74
  491.2 10.7 copy-start.75
  491.2 13.8 %slice-start.7 = ((s8[16777216]{0:T(1024)(128)(4,1)}), s8[4194304]{0:T(1024)(128)(4,1)S(1)}, s32[]{:S(2)}) async-start(s8[16777216]{0:T(1024)(128)(4,1)} %bitcast.239), calls=%async_computation.31 | async-start | bytes 8388608
  491.2 13.8 %slice-start.8 = ((s8[16777216]{0:T(1024)(128)(4,1)}), s8[4194304]{0:T(1024)(128)(4,1)S(1)}, s32[]{:S(2)}) async-start(s8[16777216]{0:T(1024)(128)(4,1)} %bitcast.239), calls=%async_computation.32 | async-start | bytes 8388608
  491.2 13.8 %slice-start.9 = ((s8[16777216]{0:T(1024)(128)(4,1)}), s8[4194304]{0:T(1024)(128)(4,1)S(1)}, s32[]{:S(2)}) async-start(s8[16777216]{0:T(1024)(128)(4,1)} %bitcast.239), calls=%async_computation.33 | async-start | bytes 8388608
  505.0 17.5 %copy-start.45 = (f32[128,1024]{1,0:T(8,128)}, f32[128,1024]{1,0:T(8,128)S(1)}, u32[]{:S(2)}) copy-start(f32[128,1024]{1,0:T(8,128)S(1)} %get-tuple-element.132) | copy-start | bytes 1572868
  529.5 11.0 copy-start.7
  551.5 11.8 copy-start.17
  588.5 147.3 %reduce-scatter.18.cloned.1.call-start = ((), (), s32[]{:S(2)}) async-start(), calls=%async_computation.21 | async-start | bytes 8912896
  592.8 14.1 %copy-start.18 = (bf16[128,1024]{0,1:T(8,128)(2,1)}, bf16[128,1024]{0,1:T(8,128)(2,1)S(1)}, u32[]{:S(2)}) copy-start(bf16[128,1024]{0,1:T(8,128)(2,1)S(1)} %copy.97) | copy-start | bytes 786436
  606.9 17.1 %copy-start.15 = (bf16[128,1024]{0,1:T(8,128)(2,1)S(1)}, bf16[128,1024]{0,1:T(8,128)(2,1)}, u32[]{:S(2)}) copy-start(bf16[128,1024]{0,1:T(8,128)(2,1)} %copy-done.14) | copy-start | bytes 786436
  606.9 20.4 %slice-start = ((s8[16777216]{0:T(1024)(128)(4,1)}), s8[4194304]{0:T(1024)(128)(4,1)S(1)}, s32[]{:S(2)}) async-start(s8[16777216]{0:T(1024)(128)(4,1)} %bitcast.151), calls=%async_computation.24 | async-start | bytes 8388608
  606.9 20.4 %slice-start.1 = ((s8[16777216]{0:T(1024)(128)(4,1)}), s8[4194304]{0:T(1024)(128)(4,1)S(1)}, s32[]{:S(2)}) async-start(s8[16777216]{0:T(1024)(128)(4,1)} %bitcast.151), calls=%async_computation.25 | async-start | bytes 8388608
  606.9 20.4 %slice-start.2 = ((s8[16777216]{0:T(1024)(128)(4,1)}), s8[4194304]{0:T(1024)(128)(4,1)S(1)}, s32[]{:S(2)}) async-start(s8[16777216]{0:T(1024)(128)(4,1)} %bitcast.151), calls=%async_computation.26 | async-start | bytes 8388608
  653.8 219.3 %reduce-scatter.12.cloned.1.call-start = ((), (), s32[]{:S(2)}) async-start(), calls=%async_computation.18 | async-start | bytes 9437184 | tf_op jit(solution)/shard_map/reduce_scatter | solution.py:321
  657.7 9.4 slice-start.4
  667.1 70.1 %copy-start.38 = (bf16[16,64,128]{2,1,0:T(8,128)(2,1)}, bf16[16,64,128]{2,1,0:T(8,128)(2,1)S(1)}, u32[]{:S(2)}) copy-start(bf16[16,64,128]{2,1,0:T(8,128)(2,1)S(1)} %get-tuple-element.213) | copy-start | bytes 786436
  671.6 65.5 %copy-start.20 = (bf16[128,1024]{1,0:T(8,128)(2,1)S(1)}, bf16[128,1024]{1,0:T(8,128)(2,1)}, u32[]{:S(2)}) copy-start(bf16[128,1024]{1,0:T(8,128)(2,1)} %copy-done.19) | copy-start | bytes 786436
  756.7 308.6 %reduce-scatter.14.cloned.1.call-start = ((), (), s32[]{:S(2)}) async-start(), calls=%async_computation.19 | async-start | bytes 18874368 | tf_op jit(solution)/shard_map/reduce_scatter | solution.py:324
  769.1 9.0 copy-start.46
  769.2 9.0 copy-start.96
  811.2 329.0 %reduce-scatter.20.cloned.1.call-start = ((), (), s32[]{:S(2)}) async-start(), calls=%async_computation.22 | async-start | bytes 294912
  812.1 253.2 %copy-start.91 = (s32[128]{0:T(128)S(1)}, s32[128]{0:T(128)}, u32[]{:S(2)}) copy-start(s32[128]{0:T(128)} %copy-done.90) | copy-start | bytes 1540
  812.1 255.7 %copy-start.89 = (s32[128]{0:T(128)S(1)}, s32[128]{0:T(128)}, u32[]{:S(2)}) copy-start(s32[128]{0:T(128)} %copy-done.88) | copy-start | bytes 1540
  812.1 258.3 %copy-start.53 = (s32[16,8,1]{1,2,0:T(1,128)S(1)}, s32[16,8,1]{1,2,0:T(1,128)}, u32[]{:S(2)}) copy-start(s32[16,8,1]{1,2,0:T(1,128)} %get-tuple-element.217) | copy-start | bytes 1540
  812.2 258.4 %copy-start.52 = (s32[16,8,1]{1,2,0:T(1,128)S(1)}, s32[16,8,1]{1,2,0:T(1,128)}, u32[]{:S(2)}) copy-start(s32[16,8,1]{1,2,0:T(1,128)} %get-tuple-element.142) | copy-start | bytes 1540
  812.3 258.3 %copy-start.6 = (bf16[128,1024]{1,0:T(8,128)(2,1)S(1)}, bf16[128,1024]{1,0:T(8,128)(2,1)}, u32[]{:S(2)}) copy-start(bf16[128,1024]{1,0:T(8,128)(2,1)} %get-tuple-element.156) | copy-start | bytes 786436
  813.4 456.5 %all-reduce.3.cloned.1.call-start = ((), (), s32[]{:S(2)}) async-start(), calls=%async_computation.23 | async-start | bytes 6291456 | tf_op jit(solution)/shard_map/psum | solution.py:332
  1065.3 15.8 %copy-start.5 = (bf16[128,1024]{1,0:T(8,128)(2,1)S(1)}, bf16[128,1024]{1,0:T(8,128)(2,1)}, u32[]{:S(2)}) copy-start(bf16[128,1024]{1,0:T(8,128)(2,1)} %get-tuple-element.173) | copy-start | bytes 786436
  1072.2 20.5 %copy-start.25 = (f32[128,1024]{1,0:T(8,128)S(1)}, f32[128,1024]{1,0:T(8,128)}, u32[]{:S(2)}) copy-start(f32[128,1024]{1,0:T(8,128)} %copy-done.23) | copy-start | bytes 1572868
  1072.2 20.5 %copy-start.39 = (bf16[16,64,128]{2,1,0:T(8,128)(2,1)S(1)}, bf16[16,64,128]{2,1,0:T(8,128)(2,1)}, u32[]{:S(2)}) copy-start(bf16[16,64,128]{2,1,0:T(8,128)(2,1)} %copy-done.38) | copy-start | bytes 786436
  1072.2 16.2 %all-to-all-start.5 = ((bf16[16,8,1024]{2,1,0:T(8,128)(2,1)}), bf16[16,8,1024]{2,1,0:T(8,128)(2,1)S(1)}, u32[]{:S(2)}, u32[]{:S(2)}) async-start(bf16[16,8,1024]{2,1,0:T(8,128)(2,1)} %bitcast.39), calls=%async_computation.5 | async-start | bytes 524288 | tf_op jit(solution)/shard_map/all_to_all | solution.py:314
  1088.4 11.7 all-to-all-start.2
  1100.0 12.4 all-to-all-start.7
  1112.4 59.1 %all-to-all-start.6 = ((bf16[16,8,1024]{2,1,0:T(8,128)(2,1)}), bf16[16,8,1024]{2,1,0:T(8,128)(2,1)S(1)}, u32[]{:S(2)}, u32[]{:S(2)}) async-start(bf16[16,8,1024]{2,1,0:T(8,128)(2,1)} %bitcast.51), calls=%async_computation.6 | async-start | bytes 524288 | tf_op jit(solution)/shard_map/all_to_all | solution.py:315
  1172.4 119.7 %copy-start.9 = (f32[128,4096]{1,0:T(8,128)S(1)}, f32[128,4096]{1,0:T(8,128)}, u32[]{:S(2)}) copy-start(f32[128,4096]{1,0:T(8,128)} %param.17) | copy-start | bytes 6291460
  1269.9 22.2 %copy-start.11 = (bf16[128,4096]{1,0:T(8,128)(2,1)S(1)}, bf16[128,4096]{1,0:T(8,128)(2,1)}, u32[]{:S(2)}) copy-start(bf16[128,4096]{1,0:T(8,128)(2,1)} %get-tuple-element.118) | copy-start | bytes 3145732
  1292.1 9.1 copy-start.13
  (61 other events, 212.8 us)
Sparse Core Ops, SparseCore 0:
  10.9 123.0 all-gather.4
  142.2 50.9 all-gather.6
  196.1 186.0 all-gather.8
  384.3 50.9 all-gather.10
  588.6 71.7 reduce-scatter.15
  662.6 73.1 reduce-scatter.17
  756.8 116.2 reduce-scatter.11
  877.1 188.1 reduce-scatter.13
  1069.4 70.6 reduce-scatter.19
  1142.8 127.0 all-reduce.2
where the time goes:
time: 1330 us; the launch traced here: 1320 us
  waiting for transfers between devices  698 us (52%)
  matrix products  225 us (17%)
  other arithmetic  149 us (11%)
  local copies, waits for them, and re-layouts  105 us (8%)
  blocking collectives  67.1 us (5%)
  starting transfers between devices  52.9 us (4%)
  between operations  19.9 us (1%)
    reduce_scatter x1, waiting for transfers between devices, shards(): lax.psum_scatter(acc_ffn.astype(jnp.bfloat16), 'fsdp', scatter_dimension=...  192 us
    all_gather x1, waiting for transfers between devices, shards(): lax.all_gather(send_ffn, 'fsdp', axis=0, tiled=True)  137 us
    psum x1, waiting for transfers between devices, shards(): lax.psum(shares[0].astype(jnp.bfloat16), 'ctx').astype(jnp.float32)  96.6 us
    all_gather x2, waiting for transfers between devices, in_one_piece_2(): whole, at, outs = (lax.all_gather(both, axis, axis=dim, tiled=True), 0, [])  81.2 us
    unnamed x13, waiting for transfers between devices  78.1 us
    reduce_scatter x1, waiting for transfers between devices, shards(): lax.psum_scatter(acc_attn.astype(jnp.bfloat16), 'fsdp', scatter_dimension...  59.5 us
    unnamed x222, local copies, waits for them, and re-layouts  42.9 us
    slice x6, local copies, waits for them, and re-layouts, in_one_piece_2(): outs.append(lax.slice_in_dim(whole, at, at + a.shape[along], axis=along))  38.6 us
  transfers between devices with their start and end apart: 18, of which 14 were waited for; matrix products, arithmetic and copies ran while one was open for 20% of the time, Pallas kernels for 0%

commit v1 on v0

v1 whole, which is shorter than its diff:
```python
from functools import partial
import math

import jax
import jax.numpy as jnp
from jax import lax
from jax.experimental import pallas as pl
from jax.experimental.pallas import tpu as pltpu
from jax.sharding import Mesh, PartitionSpec as P

HEADS = 16
HEAD = 64
STEP = 10
MB = 2
TOK = 128
ROWS = MB * TOK
D = 1024
FF = 4096
N_CTX = 16
N_FSDP = 8
PACK = 2048
SENT = 208

NORM_EPS = 1e-05
CLIP_NORM = 1.0
BETA_FIRST = 0.9
BETA_SECOND = 0.999
ADAM_EPS = 1e-08
WEIGHT_DECAY = 0.01
RATE_VECTOR = 0.3
ATTN_RATE_SCALE = 3.0
NEG_LARGE = -1e30
SCALE2 = HEAD ** (-0.5) * math.log2(math.e)
SCALE = HEAD ** (-0.5)
CONTRACT_ROWS = (((0,), (0,)), ((), ()))
CONTRACT_COLS = (((1,), (1,)), ((), ()))
CTX = ("yl", "z", "core")
FSDP = ("x", "yh")
ALL = ("x", "yh", "yl", "z", "core")
BLK = 256
NBLK = PACK // BLK
f32 = jnp.float32
bf16 = jnp.bfloat16


def dot(a, b):
    return jnp.dot(a, b, preferred_element_type=f32)


def dot_nt(a, b):
    return lax.dot_general(a, b, CONTRACT_COLS, preferred_element_type=f32)


def dot_tn(a, b):
    return lax.dot_general(a, b, CONTRACT_ROWS, preferred_element_type=f32)


def load_side(qkv_ref, keys, values, keys_t, values_t, seg_col):
    for s in range(N_CTX):
        at = slice(s * TOK, (s + 1) * TOK)
        key_t = qkv_ref[s, 0, HEAD : 2 * HEAD, :]
        value_t = qkv_ref[s, 0, 2 * HEAD : 3 * HEAD, :]
        keys[at, :] = key_t.T
        if values is not None:
            values[at, :] = value_t.T
        if keys_t is not None:
            keys_t[:, at] = key_t
        if values_t is not None:
            values_t[:, at] = value_t
        seg = qkv_ref[s, 0, 3 * HEAD : 3 * HEAD + 1, :].astype(f32)
        seg_col[at, :] = jnp.broadcast_to(seg, (TOK, TOK)).T


def pair(ref, j, rows):
    return jnp.concatenate([ref[2 * j, 0, rows, :], ref[2 * j + 1, 0, rows, :]], axis=1)


def attn_fwd_kernel(qkv_ref, out_ref, full_ref, lse_ref, keys, values_t, seg_col, scores):
    load_side(qkv_ref, keys, None, None, values_t, seg_col)

    def query_block(j, _):
        query_t = pair(qkv_ref, j, slice(0, HEAD))
        seg_row = pair(qkv_ref, j, slice(3 * HEAD, 3 * HEAD + 1)).astype(f32)
        top = jnp.full((1, BLK), NEG_LARGE, f32)
        for k in range(NBLK):
            at = slice(k * BLK, (k + 1) * BLK)
            s = dot(keys[at, :], query_t) * SCALE2
            col = seg_col[at, :]
            same = jnp.concatenate([col, col], axis=1) == seg_row
            s = jnp.where(same, s, NEG_LARGE)
            scores[at, :] = s
            top = jnp.maximum(top, jnp.max(s, axis=0, keepdims=True))
        total = jnp.zeros((1, BLK), f32)
        acc = jnp.zeros((HEAD, BLK), f32)
        for k in range(NBLK):
            at = slice(k * BLK, (k + 1) * BLK)
            p = jnp.exp2(scores[at, :] - top)
            total = total + jnp.sum(p, axis=0, keepdims=True)
            acc = acc + dot(values_t[:, at], p.astype(bf16))
        acc = acc / total
        out_ref[2 * j, 0] = acc[:, :TOK].astype(bf16)
        out_ref[2 * j + 1, 0] = acc[:, TOK:].astype(bf16)
        full_ref[2 * j, 0] = acc[:, :TOK]
        full_ref[2 * j + 1, 0] = acc[:, TOK:]
        lse = top + jnp.log2(total)
        lse_ref[2 * j, 0] = lse[:, :TOK]
        lse_ref[2 * j + 1, 0] = lse[:, TOK:]
        return 0

    lax.fori_loop(0, NBLK, query_block, 0)


def attn_fwd(qkv):
    spec = lambda rows: pl.BlockSpec((N_CTX, 1, rows, TOK), lambda m: (0, m, 0, 0))
    shape = lambda rows, dt: jax.ShapeDtypeStruct((N_CTX, MB, rows, TOK), dt)
    return pl.pallas_call(
        attn_fwd_kernel,
        grid=(MB,),
        in_specs=[spec(SENT)],
        out_specs=[spec(HEAD), spec(HEAD), spec(1)],
        out_shape=[shape(HEAD, bf16), shape(HEAD, f32), shape(1, f32)],
        scratch_shapes=[
            pltpu.VMEM((PACK, HEAD), bf16),
            pltpu.VMEM((HEAD, PACK), bf16),
            pltpu.VMEM((PACK, TOK), f32),
            pltpu.VMEM((PACK, BLK), f32),
        ],
        compiler_params=pltpu.CompilerParams(vmem_limit_bytes=40 * 2**20),
        cost_estimate=pl.CostEstimate(
            flops=4 * MB * PACK * PACK * HEAD, bytes_accessed=4 * 2**20, transcendentals=MB * PACK * PACK
        ),
        name="attn_fwd",
    )(qkv)


def attn_bwd_kernel(
    qkv_ref, grad_ref, full_ref, lse_ref, out_ref, keys, values, keys_t, seg_col, acc_k, acc_v
):
    load_side(qkv_ref, keys, values, keys_t, None, seg_col)
    acc_k[...] = jnp.zeros_like(acc_k)
    acc_v[...] = jnp.zeros_like(acc_v)

    def query_block(j, _):
        query_t = pair(qkv_ref, j, slice(0, HEAD))
        seg_row = pair(qkv_ref, j, slice(3 * HEAD, 3 * HEAD + 1)).astype(f32)
        grad_t = pair(grad_ref, j, slice(0, HEAD))
        lse = pair(lse_ref, j, slice(0, 1))
        delta = jnp.sum(
            grad_t.astype(f32) * pair(full_ref, j, slice(0, HEAD)), axis=0, keepdims=True
        )
        acc_q = jnp.zeros((HEAD, BLK), f32)
        for k in range(NBLK):
            at = slice(k * BLK, (k + 1) * BLK)
            s = dot(keys[at, :], query_t) * SCALE2 - lse
            col = seg_col[at, :]
            same = jnp.concatenate([col, col], axis=1) == seg_row
            p = jnp.exp2(jnp.where(same, s, NEG_LARGE))
            dp = dot(values[at, :], grad_t)
            ds = (p * (dp - delta)).astype(bf16)
            acc_q = acc_q + dot(keys_t[:, at], ds)
            acc_k[:, at] += dot_nt(query_t, ds)
            acc_v[:, at] += dot_nt(grad_t, p.astype(bf16))
        acc_q = (acc_q * SCALE).astype(bf16)
        out_ref[2 * j, 0, :HEAD, :] = acc_q[:, :TOK]
        out_ref[2 * j + 1, 0, :HEAD, :] = acc_q[:, TOK:]
        return 0

    lax.fori_loop(0, NBLK, query_block, 0)
    for s in range(N_CTX):
        at = slice(s * TOK, (s + 1) * TOK)
        out_ref[s, 0, HEAD : 2 * HEAD, :] = (acc_k[:, at] * SCALE).astype(bf16)
        out_ref[s, 0, 2 * HEAD :, :] = acc_v[:, at].astype(bf16)


def attn_bwd(qkv, grad, full, lse):
    spec = lambda rows: pl.BlockSpec((N_CTX, 1, rows, TOK), lambda m: (0, m, 0, 0))
    return pl.pallas_call(
        attn_bwd_kernel,
        grid=(MB,),
        in_specs=[spec(SENT), spec(HEAD), spec(HEAD), spec(1)],
        out_specs=spec(3 * HEAD),
        out_shape=jax.ShapeDtypeStruct((N_CTX, MB, 3 * HEAD, TOK), bf16),
        scratch_shapes=[
            pltpu.VMEM((PACK, HEAD), bf16),
            pltpu.VMEM((PACK, HEAD), bf16),
            pltpu.VMEM((HEAD, PACK), bf16),
            pltpu.VMEM((PACK, TOK), f32),
            pltpu.VMEM((HEAD, PACK), f32),
            pltpu.VMEM((HEAD, PACK), f32),
        ],
        compiler_params=pltpu.CompilerParams(vmem_limit_bytes=40 * 2**20),
        cost_estimate=pl.CostEstimate(
            flops=10 * MB * PACK * PACK * HEAD, bytes_accessed=8 * 2**20, transcendentals=MB * PACK * PACK
        ),
        name="attn_bwd",
    )(qkv, grad, full, lse)


MESH_ID = pl.DeviceIdType.MESH
COLS = 512
N_BLK = 4
VEC_AT = 2048
PART_COLS = (2048 + 128, 2048, 2048)
ORDERS = (("x", "z", "y"), ("z", "y", "x"), ("y", "x", "z"))
BLOCKS = tuple(
    tuple((b * COLS, COLS) for b in range(N_BLK)) + (((VEC_AT, 128),) if p == 0 else ()) for p in range(3)
)
HALF_Z = 3072


def coordinate(axis):
    if axis == "y":
        return lax.axis_index("yh") * 2 + lax.axis_index("yl")
    return lax.axis_index(axis)


def peer(axis, step):
    at = lax.rem(coordinate(axis) + step, 4)
    if axis == "y":
        return {"yh": at // 2, "yl": lax.rem(at, 2)}, at
    return {axis: at}, at


def pick(ref, axis, at, dims, cols):
    index = []
    for d in dims:
        if d == axis:
            index.append(at)
        elif axis == "y" and d == "yh":
            index.append(at // 2)
        elif axis == "y" and d == "yl":
            index.append(lax.rem(at, 2))
        else:
            index.append(slice(None))
    return ref.at[(*index, slice(None), cols)]


def dims_after(order, n):
    dims = ["x", "yh", "yl", "z"]
    for axis in order[:n]:
        for d in ("yh", "yl") if axis == "y" else (axis,):
            dims.remove(d)
    return dims


SIZES = {"x": 4, "yh": 2, "yl": 2, "z": 4}


def lead(order, n):
    return tuple(SIZES[d] for d in dims_after(order, n))


def send(src, dst, sems, index, to):
    return pltpu.make_async_remote_copy(
        src_ref=src, dst_ref=dst, send_sem=sems[0].at[index], recv_sem=sems[1].at[index],
        device_id=to, device_id_type=MESH_ID,
    )


def greet():
    barrier = pltpu.get_barrier_semaphore()
    others = [peer(axis, step)[0] for axis in ("x", "y", "z") for step in (1, 2, 3)]
    others.append({"core": 1 - lax.axis_index("core")})
    for other in others:
        pl.semaphore_signal(barrier, inc=1, device_id=other, device_id_type=MESH_ID)
    pl.semaphore_wait(barrier, len(others))


def grads_kernel(
    left_x, left_o, left_h, left_f, right_q, right_o, right_u, right_g, vec,
    out_attn, out_ffn, out_vec, out_sq,
    peer_left, peer_right, peer_vec,
    w_0, w_1, w_2, s1_0, s1_1, s1_2, s2_0, s2_1, s2_2,
    r1_0, r1_1, r1_2, r2_0, r2_1, r2_2, r3_0, r3_1, r3_2,
    gathered, sq_z, sq_y, sq_x, sq_c,
    swap_send, swap_recv, ring_send, ring_recv, gather_send, gather_recv, sq_send, sq_recv, out_sem,
):
    core = lax.axis_index("core")
    other = 1 - core
    place = lax.axis_index("yl") * 4 + lax.axis_index("z")
    lefts = (left_x, left_o, left_h, left_f)
    rights = (right_q, right_o, right_u, right_g)
    widths = (1536, 512, 2048, 2048)
    offsets = (0, 1536, 2048, 4096)
    works, firsts, seconds = (w_0, w_1, w_2), (s1_0, s1_1, s1_2), (s2_0, s2_1, s2_2)
    recvs = ((r1_0, r1_1, r1_2), (r2_0, r2_1, r2_2), (r3_0, r3_1, r3_2))
    greet()

    to_core = {"core": other}
    swaps = []
    for i in range(4):
        swaps.append(send(lefts[i], peer_left.at[i], (swap_send, swap_recv), 2 * i, to_core))
        from_cols = pl.ds(pl.multiple_of(other * widths[i], 512), widths[i])
        swaps.append(
            send(
                rights[i].at[:, from_cols], peer_right.at[:, offsets[i] : offsets[i] + widths[i]],
                (swap_send, swap_recv), 2 * i + 1, to_core,
            )
        )
    swaps.append(send(vec, peer_vec, (swap_send, swap_recv), 8, to_core))
    for copy in swaps:
        copy.start()
    for copy in swaps:
        copy.wait()

    def product_of(p, b):
        if p == 0:
            return (0, b * COLS) if b < 3 else (1, 0)
        return (p + 1, b * COLS)

    def copies(p, phase, b):
        order = ORDERS[p]
        axis = order[phase]
        at, width = BLOCKS[p][b]
        cols = slice(at, at + width)
        src = (works, firsts, seconds)[phase][p]
        out = []
        for step in (1, 2, 3):
            to, index = peer(axis, step)
            chunk = pick(src, axis, index, dims_after(order, phase), cols)
            land = recvs[phase][p].at[(step - 1, *(slice(None),) * (len(lead(order, phase + 1)) + 1), cols)]
            out.append(send(chunk, land, (ring_send, ring_recv), ((p * 3 + phase) * 5 + b) * 3 + step - 1, to))
        return out

    for b in range(5):
        for p in range(3):
            if b >= len(BLOCKS[p]):
                continue
            at, width = BLOCKS[p][b]
            work = works[p]
            if b == 4:
                work[:, :, :, :, :, VEC_AT:] = (vec[...].astype(f32) + peer_vec[...].astype(f32)).astype(bf16)
            else:
                i, col = product_of(p, b)
                mine = pl.ds(pl.multiple_of(core * widths[i] + col, 512), COLS)
                theirs = slice(offsets[i] + col, offsets[i] + col + COLS)

                def rows_block(x, _, i=i, mine=mine, theirs=theirs, work=work, at=at):
                    rows = pl.ds(pl.multiple_of(x * 256, 256), 256)
                    value = dot(lefts[i][rows, :], rights[i][:, mine])
                    value = value + dot(peer_left[i, rows, :], peer_right[:, theirs])
                    work[x, :, :, :, :, at : at + COLS] = value.astype(bf16).reshape(2, 2, 4, 16, COLS)
                    return 0

                lax.fori_loop(0, 4, rows_block, 0)
            for copy in copies(p, 0, b):
                copy.start()

    squares = jnp.zeros((8, 128), f32)
    for phase in range(3):
        for b in range(5):
            for p in range(3):
                if b >= len(BLOCKS[p]):
                    continue
                at, width = BLOCKS[p][b]
                cols = slice(at, at + width)
                order = ORDERS[p]
                axis = order[phase]
                src = (works, firsts, seconds)[phase][p]
                land = recvs[phase][p]
                for copy in copies(p, phase, b):
                    copy.wait()
                own = pick(src, axis, coordinate(axis), dims_after(order, phase), cols)
                rest = len(lead(order, phase + 1)) - 1
                if phase < 2:
                    dst = (firsts, seconds)[phase][p]

                    def add(n, _, own=own, land=land, dst=dst, rest=rest, cols=cols):
                        tail = (*(slice(None),) * (rest + 1), cols)
                        inner = (*(slice(None),) * (rest + 1), slice(None))
                        value = own[(n, *inner)].astype(f32)
                        for step in range(3):
                            value = value + land[(step, n, *tail)].astype(f32)
                        dst[(n, *tail)] = value.astype(bf16)
                        return 0

                    lax.fori_loop(0, lead(order, phase + 1)[0], add, 0)
                    for copy in copies(p, phase + 1, b):
                        copy.start()
                else:
                    value = own[...].astype(f32)
                    for step in range(3):
                        value = value + land[step, :, cols].astype(f32)
                    to = p * 2048 + at if width == COLS else 6144
                    gathered[core, place, :, to : to + width] = value.astype(bf16)
                    square = value * value
                    if width != COLS:
                        square = square * jnp.where(core == 0, 1.0, 0.0)
                    for c in range(0, width, 128):
                        squares = squares + square[:8, c : c + 128] + square[8:, c : c + 128]

    yl, z = lax.axis_index("yl"), lax.axis_index("z")
    z_first, y_first = slice(0, HALF_Z), slice(HALF_Z, 6272)
    to_y = {"yl": 1 - yl}
    gather_sems = (gather_send, gather_recv)
    sq_sems = (sq_send, sq_recv)

    def spread(buffer, axis, base):
        at = coordinate(axis)
        out = []
        for step in (1, 2, 3):
            out.append(send(buffer.at[at], buffer.at[at], sq_sems, base + step - 1, peer(axis, step)[0]))
        return out

    def total(buffer):
        return (buffer[0] + buffer[1]) + (buffer[2] + buffer[3])

    sq_z[z] = squares
    squares_z = spread(sq_z, "z", 0)
    first_z = [
        send(gathered.at[core, place, :, z_first], gathered.at[core, place, :, z_first], gather_sems, step - 1, peer("z", step)[0])
        for step in (1, 2, 3)
    ]
    first_y = send(gathered.at[core, place, :, y_first], gathered.at[core, place, :, y_first], gather_sems, 3, to_y)
    for copy in (*squares_z, *first_z, first_y):
        copy.start()
    for copy in squares_z:
        copy.wait()
    y_at = coordinate("y")
    sq_y[y_at] = total(sq_z)
    squares_y = spread(sq_y, "y", 3)
    for copy in squares_y:
        copy.start()
    for copy in (*first_z, first_y):
        copy.wait()
    quarter = pl.ds(yl * 4, 4)
    second_y = send(
        gathered.at[core, quarter, :, z_first], gathered.at[core, quarter, :, z_first], gather_sems, 4, to_y
    )
    second_y.start()
    second_z = []
    for step in (1, 2, 3):
        for half in range(2):
            view = gathered.at[core, half * 4 + z, :, y_first]
            second_z.append(send(view, view, gather_sems, 5 + (step - 1) * 2 + half, peer("z", step)[0]))
    for copy in second_z:
        copy.start()
    for copy in squares_y:
        copy.wait()
    x_at = coordinate("x")
    sq_x[x_at] = total(sq_y)
    squares_x = spread(sq_x, "x", 6)
    for copy in squares_x:
        copy.start()
    for copy in squares_x:
        copy.wait()
    sq_c[core] = total(sq_x)
    square_c = send(sq_c.at[core], sq_c.at[core], sq_sems, 9, to_core)
    square_c.start()
    square_c.wait()
    out_sq[...] = sq_c[0] + sq_c[1]
    second_y.wait()
    for copy in second_z:
        copy.wait()
    last = send(gathered.at[core], gathered.at[core], gather_sems, 11, to_core)
    last.start()
    last.wait()
    locals_ = []
    n = 0
    for c in range(2):
        for i in range(4):
            target, base = ((out_attn, c * 1536), (out_attn, 3072 + c * 512), (out_ffn, c * 2048), (out_ffn, 4096 + c * 2048))[i]
            locals_.append(
                pltpu.make_async_copy(
                    gathered.at[c, :, :, offsets[i] : offsets[i] + widths[i]],
                    target.at[:, :, base : base + widths[i]], out_sem.at[n],
                )
            )
            n += 1
    locals_.append(pltpu.make_async_copy(gathered.at[0, :, :, 6144:], out_vec, out_sem.at[n]))
    for copy in locals_:
        copy.start()
    for copy in locals_:
        copy.wait()


def grads(lefts, rights, vec):
    scratch = [
        pltpu.VMEM((4, D, ROWS), bf16),
        pltpu.VMEM((ROWS, 6144), bf16),
        pltpu.VMEM((4, 2, 2, 4, 16, 128), bf16),
    ]
    for n in range(3):
        scratch += [pltpu.VMEM((*lead(ORDERS[p], n), 16, PART_COLS[p]), bf16) for p in range(3)]
    for n in range(1, 4):
        scratch += [pltpu.VMEM((3, *lead(ORDERS[p], n), 16, PART_COLS[p]), bf16) for p in range(3)]
    scratch += [
        pltpu.VMEM((2, 8, 16, 6272), bf16),
        pltpu.VMEM((4, 8, 128), f32),
        pltpu.VMEM((4, 8, 128), f32),
        pltpu.VMEM((4, 8, 128), f32),
        pltpu.VMEM((2, 8, 128), f32),
    ]
    for count in (9, 9, 135, 135, 12, 12, 10, 10, 9):
        scratch.append(pltpu.SemaphoreType.DMA((count,)))
    vmem = pl.BlockSpec(memory_space=pltpu.VMEM)
    hbm = pl.BlockSpec(memory_space=pl.ANY)
    out = pl.pallas_call(
        grads_kernel,
        in_specs=[vmem] * 9,
        out_specs=[hbm, hbm, hbm, vmem],
        out_shape=[
            jax.ShapeDtypeStruct((8, 16, 4 * D), bf16),
            jax.ShapeDtypeStruct((8, 16, 2 * FF), bf16),
            jax.ShapeDtypeStruct((8, 16, 128), bf16),
            jax.ShapeDtypeStruct((8, 128), f32),
        ],
        scratch_shapes=scratch,
        compiler_params=pltpu.CompilerParams(
            collective_id=1, has_side_effects=True, vmem_limit_bytes=60 * 2**20
        ),
        cost_estimate=pl.CostEstimate(flops=2 * 512 * D * 6144, bytes_accessed=16 * 2**20, transcendentals=0),
        name="grads",
    )(*lefts, *rights, vec)
    return out[0].reshape(TOK, 4 * D), out[1].reshape(TOK, 2 * FF), out[2][0, :12], jnp.sum(out[3])


def layer_stats(values, gain_row, shift_row):
    center = values - jnp.mean(values, axis=-1, keepdims=True)
    inverse = lax.rsqrt(jnp.mean(center * center, axis=-1, keepdims=True) + NORM_EPS)
    normal = center * inverse
    return (normal * gain_row + shift_row, normal, inverse)


def layer_back(grad_value, normal, inverse, gain_row):
    scaled = grad_value * gain_row
    return inverse * (
        scaled
        - jnp.mean(scaled, axis=-1, keepdims=True)
        - normal * jnp.mean(scaled * normal, axis=-1, keepdims=True)
    )


def column_sum(values):
    return jnp.sum(values.astype(f32), axis=0)


def adamw(weight, grad_value, first, second, rate, decay):
    first_new = BETA_FIRST * first + (1.0 - BETA_FIRST) * grad_value
    second_new = BETA_SECOND * second + (1.0 - BETA_SECOND) * grad_value * grad_value
    first_hat = first_new / (1.0 - BETA_FIRST**STEP)
    second_hat = second_new / (1.0 - BETA_SECOND**STEP)
    weight_new = weight - rate * (first_hat / (jnp.sqrt(second_hat) + ADAM_EPS) + decay * weight)
    return (weight_new, first_new, second_new)


def to_heads(rows, parts):
    t = rows.T.reshape(parts, HEADS, HEAD, MB, TOK)
    return jnp.transpose(t, (1, 3, 0, 2, 4)).reshape(HEADS, MB, parts * HEAD, TOK)


def from_heads(blocks, parts):
    t = blocks.reshape(HEADS, MB, parts, HEAD, TOK)
    return jnp.transpose(t, (1, 4, 2, 0, 3)).reshape(ROWS, parts * D)


def swap(value):
    return lax.all_to_all(value, CTX, 0, 0, tiled=True)


def shards(
    tokens, cotangent, dest, lengths, attn_weight, attn_first, attn_second,
    ffn_weight, ffn_first, ffn_second, vectors, vec_first, vec_second,
):
    place = lax.axis_index(CTX)
    own_rows = D // N_FSDP // N_CTX
    both = jnp.concatenate(
        [
            lax.dynamic_slice_in_dim(attn_weight, place * own_rows, own_rows).astype(bf16),
            lax.dynamic_slice_in_dim(ffn_weight, place * own_rows, own_rows).astype(bf16),
            jnp.pad(vectors.reshape(8, 192).astype(bf16), ((0, 0), (0, 64))),
        ],
        axis=1,
    )
    full = lax.all_gather(both, ALL, axis=0, tiled=True)
    w_qkv = full[:, : 3 * D]
    w_out = full[:, 3 * D : 4 * D]
    w_one = full[:, 4 * D : 4 * D + FF]
    w_two = full[:, 4 * D + FF : 4 * D + 2 * FF]
    small = full[:, 4 * D + 2 * FF : 4 * D + 2 * FF + 192].reshape(N_FSDP, N_CTX, 8, 192)[:, 0]
    small = jnp.transpose(small.reshape(N_FSDP, 12, TOK), (1, 0, 2)).reshape(12, D).astype(f32)

    x = tokens.reshape(ROWS, D)
    cot = cotangent.reshape(ROWS, D).astype(f32)
    ends = jnp.cumsum(lengths[:, 0], axis=1)
    seg = jnp.sum((dest[:, 0, :, None] >= ends[:, None, :]).astype(jnp.int32), axis=2)
    keep = (seg.reshape(ROWS, 1) < 8).astype(f32)

    bias = jnp.concatenate([small[0], jnp.zeros((D,), f32), small[1]])
    qkv = (dot(x, w_qkv) + bias).astype(bf16)
    seg_rows = jnp.broadcast_to(seg.astype(bf16)[None, :, None, :], (HEADS, MB, 16, TOK))
    held = swap(jnp.concatenate([to_heads(qkv, 3), seg_rows], axis=2))
    mixed_t, mixed_full, lse = attn_fwd(held)
    mixed = from_heads(swap(mixed_t), 1)

    branch = dot(mixed, w_out) + small[2]
    normed_one, normal_one, inverse_one = layer_stats(x.astype(f32) + branch, small[4], small[5])
    normed_low = normed_one.astype(bf16)
    hidden_pre = dot(normed_low, w_one) + small[8:].reshape(FF)
    activ, gelu_back = jax.vjp(partial(jax.nn.gelu, approximate=False), hidden_pre)
    activ_low = activ.astype(bf16)
    ffn_out = dot_nt(activ_low, w_two) + small[3]
    output, normal_two, inverse_two = layer_stats(normed_one + ffn_out, small[6], small[7])
    output = output * keep
    grad_out = cot * keep
    grad_two = layer_back(grad_out, normal_two, inverse_two, small[6])
    ffn_grad_low = grad_two.astype(bf16)
    grad_hidden = gelu_back(dot(ffn_grad_low, w_two))[0].astype(bf16)
    grad_normed = dot_nt(grad_hidden, w_one) + grad_two
    grad_one = layer_back(grad_normed, normal_one, inverse_one, small[4])
    branch_grad_low = grad_one.astype(bf16)
    grad_mixed = dot_nt(branch_grad_low, w_out).astype(bf16)

    grad_held = attn_bwd(held, swap(to_heads(grad_mixed, 1)), mixed_full, lse)
    grad_qkv = from_heads(swap(grad_held), 3)
    grad_tokens = grad_one + dot_nt(grad_qkv, w_qkv)

    step_vec = jnp.concatenate(
        [
            jnp.stack(
                [
                    column_sum(grad_qkv[:, :D]),
                    column_sum(grad_qkv[:, 2 * D :]),
                    column_sum(branch_grad_low),
                    column_sum(ffn_grad_low),
                    jnp.sum(grad_normed * normal_one, axis=0),
                    jnp.sum(grad_normed, axis=0),
                    jnp.sum(grad_out * normal_two, axis=0),
                    jnp.sum(grad_out, axis=0),
                ]
            ),
            column_sum(grad_hidden).reshape(4, D),
        ],
        axis=0,
    )
    vec_rows = jnp.transpose(step_vec.reshape(12, N_FSDP, TOK), (1, 0, 2)).astype(bf16)
    vec_rows = jnp.pad(vec_rows.reshape(N_FSDP, 1, 12, TOK), ((0, 0), (0, 7), (0, 4), (0, 0)))
    total_attn, total_ffn, total_vec, square_sum = grads(
        (x.T, mixed.T, normed_low.T, ffn_grad_low.T),
        (grad_qkv, branch_grad_low, grad_hidden, activ_low),
        vec_rows.reshape(4, 2, 2, 4, 16, TOK),
    )
    total_attn, total_ffn, total_vec = total_attn.astype(f32), total_ffn.astype(f32), total_vec.astype(f32)
    grad_norm = jnp.sqrt(square_sum)
    factor = jnp.minimum(1.0, CLIP_NORM / (grad_norm + 1e-06))
    rate_matrix = D ** (-0.5)
    attn_new, attn_first_new, attn_second_new = adamw(
        attn_weight, total_attn * factor, attn_first, attn_second, ATTN_RATE_SCALE * rate_matrix, WEIGHT_DECAY
    )
    ffn_new, ffn_first_new, ffn_second_new = adamw(
        ffn_weight, total_ffn * factor, ffn_first, ffn_second, rate_matrix, WEIGHT_DECAY
    )
    vec_new, vec_first_new, vec_second_new = adamw(
        vectors, total_vec * factor, vec_first, vec_second, RATE_VECTOR, 0.0
    )
    return (
        output.astype(bf16).reshape(tokens.shape),
        grad_tokens.astype(bf16).reshape(tokens.shape),
        grad_norm,
        attn_new, attn_first_new, attn_second_new,
        ffn_new, ffn_first_new, ffn_second_new,
        vec_new, vec_first_new, vec_second_new,
        attn_new.astype(bf16),
        ffn_new.astype(bf16),
        total_vec[2] * factor,
    )


def solution(mesh):
    fine = Mesh(mesh.devices.reshape(2, 4, 2, 4, 2), ("yl", "z", "core", "x", "yh"))
    act = P(None, FSDP, CTX, None)
    row = P(FSDP, None)
    col = P(None, FSDP)
    return jax.shard_map(
        shards,
        mesh=fine,
        in_specs=(act, act, P(None, FSDP, CTX), P(None, FSDP, None), row, row, row, row, row, row, col, col, col),
        out_specs=(act, act, P(), row, row, row, row, row, row, col, col, col, row, row, P(FSDP)),
        check_vma=False,
    )
```

time: 1330 us -> 465 us (0.35)
  waiting for transfers between devices: 698 us -> 123 us
  matrix products: 225 us -> 51 us
  Pallas kernels: 0 us -> 170 us
  other arithmetic: 149 us -> 28.7 us
  local copies, waits for them, and re-layouts: 105 us -> 19.9 us
  starting transfers between devices: 52.9 us -> 9.78 us
  blocking collectives: 67.1 us -> 41 us
    reduce_scatter x2 -> x0, waiting for transfers between devices: 252 us -> none  [the longest x1 192 us: shards(): lax.psum_scatter(acc_ffn.astype(jnp.bfloat16), 'fsdp', scatter_dimension=...]
    dot_general x36 -> x8, matrix products: 225 us -> 51 us  [the longest x4 29.3 us: dot(): return jnp.dot(a, b, preferred_element_type=f32)]
    pallas_call x0 -> x3, Pallas kernels: none -> 170 us  [the longest x1 109 us: grads(): pl.pallas_call(grads_kernel, in_specs=[vmem] * 9, out_specs=[hbm, hbm, hb...]
    all_gather x4 -> x1, waiting for transfers between devices: 241 us -> 97.2 us  [shards(): full = lax.all_gather(both, ALL, axis=0, tiled=True)]
    psum x1 -> x0, waiting for transfers between devices: 96.6 us -> none  [shards(): lax.psum(shares[0].astype(jnp.bfloat16), 'ctx').astype(jnp.float32)]
    unnamed x13 -> x1, waiting for transfers between devices: 78.1 us -> 0.02 us
    convert_element_type x14 -> x7, other arithmetic: 80.4 us -> 15.3 us  [the longest x1 7.02 us: shards(): ffn_new.astype(bf16)]
    all_to_all x8 -> x2, starting transfers between devices: 51.7 us -> 9.74 us  [swap(): return lax.all_to_all(value, CTX, 0, 0, tiled=True)]
  transfers between devices with their start and end apart: 18 -> 3, of which waited for: 14 -> 3; matrix products, arithmetic and copies ran while one was open for 20% -> 2% of each run, Pallas kernels for 0% -> 0%
where the time goes in v1:
time: 465 us; the launch traced here: 460 us
  Pallas kernels  170 us (37%)
  waiting for transfers between devices  123 us (26%)
  matrix products  51 us (11%)
  blocking collectives  41 us (9%)
  other arithmetic  28.7 us (6%)
  local copies, waits for them, and re-layouts  19.9 us (4%)
  between operations  16.5 us (4%)
  starting transfers between devices  9.78 us (2%)
    pallas_call x1, Pallas kernels, grads(): pl.pallas_call(grads_kernel, in_specs=[vmem] * 9, out_specs=[hbm, hbm, hb...  109 us
    all_gather x1, waiting for transfers between devices, shards(): full = lax.all_gather(both, ALL, axis=0, tiled=True)  97.2 us
    all_to_all x2, blocking collectives, swap(): return lax.all_to_all(value, CTX, 0, 0, tiled=True)  41 us
    pallas_call x1, Pallas kernels, attn_bwd(): pl.pallas_call(attn_bwd_kernel, grid=(MB,), in_specs=[spec(SENT), spec(HE...  40.3 us
    dot_general x4, matrix products, dot(): return jnp.dot(a, b, preferred_element_type=f32)  29.3 us
    all_to_all x2, waiting for transfers between devices, swap(): return lax.all_to_all(value, CTX, 0, 0, tiled=True)  25.3 us
    dot_general x4, matrix products, dot_nt(): return lax.dot_general(a, b, CONTRACT_COLS, preferred_element_type=f32)  21.7 us
    pallas_call x1, Pallas kernels, attn_fwd(): pl.pallas_call(attn_fwd_kernel, grid=(MB,), in_specs=[spec(SENT)], out_sp...  21.3 us
  transfers between devices with their start and end apart: 3, of which 3 were waited for; matrix products, arithmetic and copies ran while one was open for 2% of the time, Pallas kernels for 0%

profile of v1, /device:TPU:1, one launch (start us, length us, event | category | flops | bytes accessed | tf_op | source)
XLA Modules:
  0.0 459.9 jit_solution(11442417807914245032)
XLA Ops:
  7.2 0.0 all-gather.2.cloned.1.call-start
  7.2 0.7 convert_element_type.132
  7.9 0.1 convert_element_type.133
  8.0 1.0 dynamic-slice_convert_fusion
  9.0 0.9 dynamic-slice_convert_fusion.1
  9.9 0.7 fusion.67
  10.6 0.0 all-gather.2.cloned.1.call-update
  10.6 0.9 reduce_window_sum.14
  11.5 0.8 convert_reduce_fusion
  12.3 97.2 %all-gather.2.cloned.1.call-done = bf16[1024,12544]{1,0:T(8,128)(2,1)} async-done(((bf16[8,12544]{1,0:T(8,128)(2,1)}), bf16[1024,12544]{1,0:T(8,128)(2,1)}) %all-gather.2.cloned.1.call-update) | async-done | bytes 25690128 | tf_op jit(solution)/shard_map/all_gather | solution.py:575
  109.5 1.1 slice.89
  110.6 0.1 reshape.251
  110.7 5.1 %fusion.28 = bf16[3072,256]{1,0:T(8,128)(2,1)S(1)} fusion(bf16[256,1024]{1,0:T(8,128)(2,1)} %bitcast.146, bf16[1024,12544]{1,0:T(8,128)(2,1)} %all-gather.2.cloned.1.call-done, f32[3072]{0:T(1024)S(1)} %pad_maximum_fusion.1), kind=kOutput, calls=%fused_computation.37 | convolution fusion | flops 1612185600 | bytes 8400896 | tf_op jit(solution)/shard_map/dot_general | solution.py:47
  115.8 0.4 reshape.237
  116.2 0.4 copy.50
  116.6 0.1 pad_maximum_fusion
  116.8 27.3 %all_to_all.20.qkv_ref = bf16[16,2,208,128]{3,2,1,0:T(8,128)(2,1)S(1)} all-to-all(bf16[16,2,208,128]{3,2,1,0:T(8,128)(2,1)S(1)} %pad_maximum_fusion), channel_id=1, replica_groups=mesh['yl'=2,'z'=4,'core'=2,'x'=4,'yh'=2] {'yl','z','core'}, dimensions={0} | all-to-all | bytes 3407872 | tf_op jit(solution)/shard_map/all_to_all | solution.py:558
  144.1 21.3 %attn_fwd.1 = (bf16[16,2,64,128]{3,2,1,0:T(8,128)(2,1)}, f32[16,2,64,128]{3,2,1,0:T(8,128)S(1)}, f32[16,2,1,128]{3,2,1,0:T(1,128)S(1)}) custom-call(bf16[16,2,208,128]{3,2,1,0:T(8,128)(2,1)S(1)} %all_to_all.20.qkv_ref), custom_call_target="tpu_custom_call" | custom-call | flops 2147483648 | bytes 4194304 | tf_op jit(solution)/shard_map/attn_fwd/pallas_call | solution.py:116
  165.3 5.0 %all-to-all-start.1 = ((bf16[16,2,64,128]{3,2,1,0:T(8,128)(2,1)}), bf16[16,2,64,128]{3,2,1,0:T(8,128)(2,1)}, u32[]{:S(2)}, u32[]{:S(2)}) async-start(bf16[16,2,64,128]{3,2,1,0:T(8,128)(2,1)} %get-tuple-element.22), calls=%async_computation.1 | async-start | bytes 1048576 | tf_op jit(solution)/shard_map/all_to_all | solution.py:558
  170.3 0.3 fusion.62
  170.7 9.4 %all-to-all-done.1 = bf16[16,2,64,128]{3,2,1,0:T(8,128)(2,1)} async-done(((bf16[16,2,64,128]{3,2,1,0:T(8,128)(2,1)}), bf16[16,2,64,128]{3,2,1,0:T(8,128)(2,1)}, u32[]{:S(2)}, u32[]{:S(2)}) %all-to-all-start.1) | async-done | bytes 524320 | tf_op jit(solution)/shard_map/all_to_all | solution.py:558
  180.1 1.6 copy.51
  181.7 2.7 fusion.87
  184.4 0.3 multiply_reduce_fusion.6
  184.7 14.0 %multiply_convert_fusion = (bf16[256,4096]{1,0:T(8,128)(2,1)S(1)}, f32[256,4096]{1,0:T(8,128)S(1)}, f32[256,4096]{1,0:T(8,128)S(1)}) fusion(f32[4096]{0:T(1024)S(1)} %bitcast.165, bf16[1024,12544]{1,0:T(8,128)(2,1)} %all-gather.2.cloned.1.call-done, f32[256,1024]{1,0:T(8,128)S(1)} %get-tuple-element.115, f32[1024]{0:T(1024)S(1)} %bitcast.161, ...), kind=kOutput, calls=%fused_computation.22 | convolution fusion | flops 2218000384 | bytes 19949568 | tf_op jit(solution)/shard_map/dot_general | solution.py:47
  198.7 6.7 %fusion.88 = (f32[256]{0:T(256)S(1)}, f32[256,1024]{1,0:T(8,128)S(1)}) fusion(f32[1024]{0:T(1024)S(1)} %bitcast.168, bf16[256,4096]{1,0:T(8,128)(2,1)S(1)} %get-tuple-element.100.right_g, bf16[1024,12544]{1,0:T(8,128)(2,1)} %all-gather.2.cloned.1.call-done, f32[1024]{0:T(1024)S(1)} %bitcast.162, f32[1024]{0:T(1024)S(1)} %bitcast.157, ...), kind=kOutput, calls=%fused_computation.129 | convolution fusion | flops 2149318400 | bytes 12598272 | tf_op jit(solution)/shard_map/dot_general | solution.py:51
  205.4 0.2 multiply_reduce_fusion.5
  205.7 1.3 multiply_reduce_fusion
  207.0 0.4 convert_reduce_fusion.1
  207.4 0.0 copy-start.4
  207.4 7.5 %fusion.89 = (bf16[4096]{0:T(1024)(128)(2,1)S(1)}, bf16[256,4096]{1,0:T(8,128)(2,1)S(1)}) fusion(f32[256,4096]{1,0:T(8,128)S(1)} %get-tuple-element.101, f32[256,4096]{1,0:T(8,128)S(1)} %get-tuple-element.116, bf16[1024,12544]{1,0:T(8,128)(2,1)} %all-gather.2.cloned.1.call-done, f32[256,1024]{1,0:T(8,128)S(1)} %get-tuple-element.96), kind=kOutput, calls=%fused_computation.130 | convolution fusion | flops 2163470336 | bytes 19931136 | tf_op jit(solution)/shard_map/dot_general | solution.py:47
  215.0 6.5 %fusion.46 = f32[256,1024]{1,0:T(8,128)S(1)} fusion(f32[256,1024]{1,0:T(8,128)S(1)} %get-tuple-element.96, bf16[256,4096]{1,0:T(8,128)(2,1)S(1)} %get-tuple-element.120.right_u, bf16[1024,12544]{1,0:T(8,128)(2,1)} %all-gather.2.cloned.1.call-done), kind=kOutput, calls=%fused_computation.53 | convolution fusion | flops 2147745792 | bytes 12582912 | tf_op jit(solution)/shard_map/dot_general | solution.py:51
  221.5 1.3 multiply_reduce_fusion.1
  222.9 1.4 fusion.84
  224.2 0.8 copy-done.11
  225.0 3.1 fusion.55
  228.2 1.2 reshape.242
  229.3 0.1 copy.79
  229.5 13.7 %all_to_all.21.grad_ref = bf16[16,2,64,128]{3,2,1,0:T(8,128)(2,1)S(1)} all-to-all(bf16[16,2,64,128]{3,2,1,0:T(8,128)(2,1)S(1)} %bitcast.143), channel_id=1, replica_groups=mesh['yl'=2,'z'=4,'core'=2,'x'=4,'yh'=2] {'yl','z','core'}, dimensions={0} | all-to-all | bytes 1048576 | tf_op jit(solution)/shard_map/all_to_all | solution.py:558
  243.2 40.3 %attn_bwd.1 = bf16[16,2,192,128]{3,2,1,0:T(8,128)(2,1)} custom-call(bf16[16,2,208,128]{3,2,1,0:T(8,128)(2,1)S(1)} %all_to_all.20.qkv_ref, bf16[16,2,64,128]{3,2,1,0:T(8,128)(2,1)S(1)} %all_to_all.21.grad_ref, f32[16,2,64,128]{3,2,1,0:T(8,128)S(1)} %get-tuple-element.23.full_ref, f32[16,2,1,128]{3,2,1,0:T(1,128)S(1)} %get-tuple-element.24.lse_ref), custom_call_target="tpu_custom_call" | custom-call | flops 5368709120 | bytes 8388608 | tf_op jit(solution)/shard_map/attn_bwd/pallas_call | solution.py:177
  283.5 4.8 %all-to-all-start.3 = ((bf16[16,2,192,128]{3,2,1,0:T(8,128)(2,1)}), bf16[16,2,192,128]{3,2,1,0:T(8,128)(2,1)S(1)}, u32[]{:S(2)}, u32[]{:S(2)}) async-start(bf16[16,2,192,128]{3,2,1,0:T(8,128)(2,1)} %attn_bwd.1), calls=%async_computation.3 | async-start | bytes 3145728 | tf_op jit(solution)/shard_map/all_to_all | solution.py:558
  288.3 2.0 copy.56.left_x
  290.4 1.9 copy.78
  292.3 1.0 copy.57.left_h
  293.3 0.1 convert_bitcast_fusion
  293.4 1.0 copy.58.left_f
  294.4 15.9 %all-to-all-done.3 = bf16[16,2,192,128]{3,2,1,0:T(8,128)(2,1)S(1)} async-done(((bf16[16,2,192,128]{3,2,1,0:T(8,128)(2,1)}), bf16[16,2,192,128]{3,2,1,0:T(8,128)(2,1)S(1)}, u32[]{:S(2)}, u32[]{:S(2)}) %all-to-all-start.3) | async-done | bytes 1572896 | tf_op jit(solution)/shard_map/all_to_all | solution.py:558
  310.2 1.6 copy.54
  311.8 0.2 copy.77
  312.1 1.7 copy.59.right_q
  313.8 0.4 slice_reduce_fusion
  314.3 0.7 pad.9.clone
  315.0 108.8 %grads.1 = (bf16[8,16,4096]{2,1,0:T(8,128)(2,1)}, bf16[8,16,8192]{2,1,0:T(8,128)(2,1)}, bf16[8,16,128]{2,1,0:T(8,128)(2,1)}, f32[8,128]{1,0:T(8,128)}) custom-call(bf16[1024,256]{1,0:T(8,128)(2,1)} %copy.56.left_x, bf16[1024,256]{1,0:T(8,128)(2,1)} %bitcast.149, bf16[1024,256]{1,0:T(8,128)(2,1)} %copy.57.left_h, bf16[1024,256]{1,0:T(8,128)(2,1)} %copy.58.left_f, ...), custom_call_target="tpu_custom_call" | custom-call | flops 6442450944 | bytes 16777216 | tf_op jit(solution)/shard_map/grads/pallas_call | solution.py:498
  423.8 1.3 reduce_sum.189
  425.9 1.6 convert_multiply_fusion.1
  427.5 0.2 copy-done.7
  427.8 0.4 convert_multiply_fusion
  428.2 0.7 slice_convert_fusion
  428.9 0.5 fusion.71
  429.4 1.3 multiply_subtract_fusion.2
  430.8 6.9 %fusion.79 = (bf16[128,4096]{1,0:T(8,128)(2,1)}, f32[128,4096]{1,0:T(8,128)}, f32[128,4096]{1,0:T(8,128)}, f32[128,4096]{1,0:T(8,128)}) fusion(f32[128,4096]{1,0:T(8,128)S(1)} %copy-done.6, f32[8,16,4096]{2,1,0:T(8,128)S(1)} %convert_multiply_fusion.1, f32[128,4096]{1,0:T(8,128)} %param.18, f32[128,4096]{1,0:T(8,128)} %param.19), kind=kLoop, calls=%fused_computation.125 | loop fusion | flops 8388608 | bytes 15728640 | tf_op jit(solution)/shard_map/convert_element_type | solution.py:663
  437.7 1.6 copy-done.3
  439.3 7.0 %fusion.76 = (bf16[128,8192]{1,0:T(8,128)(2,1)}, f32[128,8192]{1,0:T(8,128)}, f32[128,8192]{1,0:T(8,128)}, f32[128,8192]{1,0:T(8,128)}) fusion(f32[128,8192]{1,0:T(8,128)S(1)} %copy-done.1, f32[8,16,8192]{2,1,0:T(8,128)S(1)} %convert_multiply_fusion, f32[128,8192]{1,0:T(8,128)S(1)} %copy-done.2, f32[128,8192]{1,0:T(8,128)S(1)} %copy-done.3), kind=kLoop, calls=%fused_computation.124 | loop fusion | flops 16777216 | bytes 31457280 | tf_op jit(solution)/shard_map/convert_element_type | solution.py:664
  446.3 5.4 %fusion.58 = bf16[256,1024]{1,0:T(8,128)(2,1)} fusion(f32[256,1024]{1,0:T(8,128)S(1)} %copy-done.10, bf16[1024,12544]{1,0:T(8,128)(2,1)} %all-gather.2.cloned.1.call-done, bf16[384,8,2,128]{3,2,1,0:T(2,128)(2,1)S(1)} %bitcast.138), kind=kOutput, calls=%fused_computation.57 | convolution fusion | flops 1611137024 | bytes 9437184 | tf_op jit(solution)/shard_map/dot_general | solution.py:51
  (56 shorter events, 0.3 us)
Async XLA Ops:
  7.2 102.3 %all-gather.2.cloned.1.call-start = ((), (), s32[]{:S(2)}) async-start(), calls=%async_computation.4 | async-start | bytes 25890816 | tf_op jit(solution)/shard_map/all_gather | solution.py:575
  144.1 26.3 %copy-start = (bf16[2,1,128,1024]{3,2,1,0:T(8,128)(2,1)S(1)}, bf16[2,1,128,1024]{3,2,1,0:T(8,128)(2,1)}, u32[]{:S(2)}) copy-start(bf16[2,1,128,1024]{3,2,1,0:T(8,128)(2,1)} %param.14) | copy-start | bytes 1572868
  165.3 14.8 %all-to-all-start.1 = ((bf16[16,2,64,128]{3,2,1,0:T(8,128)(2,1)}), bf16[16,2,64,128]{3,2,1,0:T(8,128)(2,1)}, u32[]{:S(2)}, u32[]{:S(2)}) async-start(bf16[16,2,64,128]{3,2,1,0:T(8,128)(2,1)} %get-tuple-element.22), calls=%async_computation.1 | async-start | bytes 1048576 | tf_op jit(solution)/shard_map/all_to_all | solution.py:558
  181.7 17.0 %copy-start.9 = (bf16[2,128,1,16,64]{1,0,4,3,2:T(2,128)(2,1)}, bf16[2,128,1,16,64]{1,0,4,3,2:T(2,128)(2,1)S(1)}, u32[]{:S(2)}) copy-start(bf16[2,128,1,16,64]{1,0,4,3,2:T(2,128)(2,1)S(1)} %copy.51) | copy-start | bytes 1572868
  198.7 6.7 %copy-start.16 = (bf16[256,4096]{1,0:T(8,128)(2,1)}, bf16[256,4096]{1,0:T(8,128)(2,1)S(1)}, u32[]{:S(2)}) copy-start(bf16[256,4096]{1,0:T(8,128)(2,1)S(1)} %get-tuple-element.100.right_g) | copy-start | bytes 6291460
  207.4 7.6 %copy-start.4 = (f32[256,1024]{1,0:T(8,128)}, f32[256,1024]{1,0:T(8,128)S(1)}, u32[]{:S(2)}) copy-start(f32[256,1024]{1,0:T(8,128)S(1)} %get-tuple-element.96) | copy-start | bytes 3145732
  215.0 6.5 %copy-start.15 = (bf16[256,4096]{1,0:T(8,128)(2,1)}, bf16[256,4096]{1,0:T(8,128)(2,1)S(1)}, u32[]{:S(2)}) copy-start(bf16[256,4096]{1,0:T(8,128)(2,1)S(1)} %get-tuple-element.120.right_u) | copy-start | bytes 6291460
  224.2 0.8 copy-start.11
  283.5 8.8 %copy-start.8 = (bf16[1024,256]{0,1:T(8,128)(2,1)S(1)}, bf16[1024,256]{0,1:T(8,128)(2,1)}, u32[]{:S(2)}) copy-start(bf16[1024,256]{0,1:T(8,128)(2,1)} %get-tuple-element.103) | copy-start | bytes 1572868
  283.5 9.8 %copy-start.5 = (f32[256,1024]{1,0:T(8,128)S(1)}, f32[256,1024]{1,0:T(8,128)}, u32[]{:S(2)}) copy-start(f32[256,1024]{1,0:T(8,128)} %copy-done.4) | copy-start | bytes 3145732
  283.5 26.7 %all-to-all-start.3 = ((bf16[16,2,192,128]{3,2,1,0:T(8,128)(2,1)}), bf16[16,2,192,128]{3,2,1,0:T(8,128)(2,1)S(1)}, u32[]{:S(2)}, u32[]{:S(2)}) async-start(bf16[16,2,192,128]{3,2,1,0:T(8,128)(2,1)} %attn_bwd.1), calls=%async_computation.3 | async-start | bytes 3145728 | tf_op jit(solution)/shard_map/all_to_all | solution.py:558
  425.9 1.9 copy-start.7
  425.9 3.6 copy-start.12
  425.9 3.6 copy-start.13
  425.9 3.5 copy-start.14
  425.9 4.8 %copy-start.6 = (f32[128,4096]{1,0:T(8,128)S(1)}, f32[128,4096]{1,0:T(8,128)}, u32[]{:S(2)}) copy-start(f32[128,4096]{1,0:T(8,128)} %param.17) | copy-start | bytes 6291460
  430.8 6.9 %copy-start.1 = (f32[128,8192]{1,0:T(8,128)S(1)}, f32[128,8192]{1,0:T(8,128)}, u32[]{:S(2)}) copy-start(f32[128,8192]{1,0:T(8,128)} %param.20) | copy-start | bytes 12582916
  430.8 6.9 %copy-start.2 = (f32[128,8192]{1,0:T(8,128)S(1)}, f32[128,8192]{1,0:T(8,128)}, u32[]{:S(2)}) copy-start(f32[128,8192]{1,0:T(8,128)} %param.21) | copy-start | bytes 12582916
  430.8 8.5 %copy-start.3 = (f32[128,8192]{1,0:T(8,128)S(1)}, f32[128,8192]{1,0:T(8,128)}, u32[]{:S(2)}) copy-start(f32[128,8192]{1,0:T(8,128)} %param.22) | copy-start | bytes 12582916
  439.3 7.0 %copy-start.10 = (f32[256,1024]{1,0:T(8,128)S(1)}, f32[256,1024]{1,0:T(8,128)}, u32[]{:S(2)}) copy-start(f32[256,1024]{1,0:T(8,128)} %get-tuple-element.99) | copy-start | bytes 3145732
Sparse Core Ops, SparseCore 0:
  11.6 97.8 all-gather.1

commit v2 on v1

v2 whole, which is shorter than its diff:
```python
from functools import partial
import math

import jax
import jax.numpy as jnp
from jax import lax
from jax.experimental import pallas as pl
from jax.experimental.pallas import tpu as pltpu
from jax.sharding import Mesh, PartitionSpec as P

HEADS = 16
HEAD = 64
STEP = 10
MB = 2
TOK = 128
ROWS = MB * TOK
D = 1024
FF = 4096
N_CTX = 16
N_FSDP = 8
PACK = 2048
SENT = 208

NORM_EPS = 1e-05
CLIP_NORM = 1.0
BETA_FIRST = 0.9
BETA_SECOND = 0.999
ADAM_EPS = 1e-08
WEIGHT_DECAY = 0.01
RATE_VECTOR = 0.3
ATTN_RATE_SCALE = 3.0
NEG_LARGE = -1e30
SCALE2 = HEAD ** (-0.5) * math.log2(math.e)
SCALE = HEAD ** (-0.5)
CONTRACT_ROWS = (((0,), (0,)), ((), ()))
CONTRACT_COLS = (((1,), (1,)), ((), ()))
CTX = ("yl", "z", "core")
FSDP = ("x", "yh")
ALL = ("x", "yh", "yl", "z", "core")
BLK = 256
NBLK = PACK // BLK
N_GROUPS = 3
STEPS = (1, 3, 6, 9, 12)
f32 = jnp.float32
bf16 = jnp.bfloat16


def dot(a, b):
    return jnp.dot(a, b, preferred_element_type=f32)


def dot_nt(a, b):
    return lax.dot_general(a, b, CONTRACT_COLS, preferred_element_type=f32)


def dot_tn(a, b):
    return lax.dot_general(a, b, CONTRACT_ROWS, preferred_element_type=f32)


MESH_ID = pl.DeviceIdType.MESH
COLS = 512
N_BLK = 4
ORDERS = (("x", "z", "y"), ("z", "y", "x"), ("y", "x", "z"))
EARLY = ((2, 0), (2, 512), (2, 1024), (2, 1536), (3, 0), (3, 512), (3, 1024), (3, 1536), (1, 0))
PRODUCT = tuple(
    tuple(EARLY[b * 3 + p] for b in range(3)) + ((0, p * COLS),) for p in range(3)
)
VEC_AT = 2048
PART_COLS = (2048 + 128, 2048, 2048)
WIDTHS = (1536, 512, 2048, 2048)
OFFSETS = (0, 1536, 2048, 4096)
HALF_Z = 3072
TASKS = {}
for _n, _at in enumerate((1, 2, 4, 5, 7, 8, 10, 11, 13)):
    TASKS.setdefault(_at, []).append((0, _n // 3, _n % 3))
for _n, _at in enumerate((6, 7, 9, 10, 12, 13, 15)):
    TASKS.setdefault(_at, []).append((1, _n // 3, _n % 3))


def coordinate(axis):
    if axis == "y":
        return lax.axis_index("yh") * 2 + lax.axis_index("yl")
    return lax.axis_index(axis)


def peer(axis, step):
    at = lax.rem(coordinate(axis) + step, 4)
    if axis == "y":
        return {"yh": at // 2, "yl": lax.rem(at, 2)}, at
    return {axis: at}, at


def pick(ref, axis, at, dims, cols):
    index = []
    for d in dims:
        if d == axis:
            index.append(at)
        elif axis == "y" and d == "yh":
            index.append(at // 2)
        elif axis == "y" and d == "yl":
            index.append(lax.rem(at, 2))
        else:
            index.append(slice(None))
    return ref.at[(*index, slice(None), cols)]


def dims_after(order, n):
    dims = ["x", "yh", "yl", "z"]
    for axis in order[:n]:
        for d in ("yh", "yl") if axis == "y" else (axis,):
            dims.remove(d)
    return dims


SIZES = {"x": 4, "yh": 2, "yl": 2, "z": 4}


def lead(order, n):
    return tuple(SIZES[d] for d in dims_after(order, n))


def send(src, dst, sems, index, to):
    return pltpu.make_async_remote_copy(
        src_ref=src, dst_ref=dst, send_sem=sems[0].at[index], recv_sem=sems[1].at[index],
        device_id=to, device_id_type=MESH_ID,
    )


def load_side(qkv_ref, m, keys, values, keys_t, values_t, seg_col):
    for s in range(N_CTX):
        at = slice(s * TOK, (s + 1) * TOK)
        key_t = qkv_ref[s, m, HEAD : 2 * HEAD, :]
        value_t = qkv_ref[s, m, 2 * HEAD : 3 * HEAD, :]
        keys[at, :] = key_t.T
        if values is not None:
            values[at, :] = value_t.T
        if keys_t is not None:
            keys_t[:, at] = key_t
        if values_t is not None:
            values_t[:, at] = value_t
        seg = qkv_ref[s, m, 3 * HEAD : 3 * HEAD + 1, :].astype(f32)
        seg_col[at, :] = jnp.broadcast_to(seg, (TOK, TOK)).T


def pair(ref, m, j, rows):
    return jnp.concatenate([ref[2 * j, m, rows, :], ref[2 * j + 1, m, rows, :]], axis=1)


def query_forward(held, m, j, out, full, lse_out, keys, values_t, seg_col, scores):
    query_t = pair(held, m, j, slice(0, HEAD))
    seg_row = pair(held, m, j, slice(3 * HEAD, 3 * HEAD + 1)).astype(f32)
    top = jnp.full((1, BLK), NEG_LARGE, f32)
    for k in range(NBLK):
        at = slice(k * BLK, (k + 1) * BLK)
        s = dot(keys[at, :], query_t) * SCALE2
        col = seg_col[at, :]
        same = jnp.concatenate([col, col], axis=1) == seg_row
        s = jnp.where(same, s, NEG_LARGE)
        scores[at, :] = s
        top = jnp.maximum(top, jnp.max(s, axis=0, keepdims=True))
    total = jnp.zeros((1, BLK), f32)
    acc = jnp.zeros((HEAD, BLK), f32)
    for k in range(NBLK):
        at = slice(k * BLK, (k + 1) * BLK)
        p = jnp.exp2(scores[at, :] - top)
        total = total + jnp.sum(p, axis=0, keepdims=True)
        acc = acc + dot(values_t[:, at], p.astype(bf16))
    acc = acc / total
    lse = top + jnp.log2(total)
    for half in range(2):
        cols = slice(half * TOK, (half + 1) * TOK)
        out[2 * j + half, m] = acc[:, cols].astype(bf16)
        full[2 * j + half, m] = acc[:, cols]
        lse_out[2 * j + half, m] = lse[:, cols]


X_COLS, Y_COLS, Z_COLS = slice(0, 512), slice(512, 1152), slice(1152, 2048)
GROUP = 2048
N_COPY = 31


def ctx_device(t):
    return {"yl": t // 8, "z": lax.rem(t // 2, 4), "core": lax.rem(t, 2)}


def rows_at(start, size):
    return pl.ds(pl.multiple_of(start, 16), size)


class Gather:
    def __init__(self, g, shard, dest, sems, base, local_sem):
        core = lax.axis_index("core")
        x, z = lax.axis_index("x"), lax.axis_index("z")
        yh, yl = lax.axis_index("yh"), lax.axis_index("yl")
        y = yh * 2 + yl
        every = slice(None)
        zq, half = rows_at(z * 32, 32), rows_at(yl * 64, 64)
        cross = {"yh": 1 - yh, "yl": 1 - yl}
        count = [0]

        def make(src, dst, to):
            copy = send(src, dst, sems, base + count[0], to)
            count[0] += 1
            return copy

        def own(rows, cols, to):
            return make(shard.at[g, rows, cols], dest(core, x, yh, rows, cols), to)

        def pass_on(xs, yhs, rows, cols, to):
            view = dest(core, xs, yhs, rows, cols)
            return make(view, view, to)

        x_to = {step: peer("x", step)[0] for step in (1, 2, 3)}
        y_to = {step: peer("y", step)[0] for step in (1, 3)}
        z_to = {step: peer("z", step)[0] for step in (1, 3)}
        self.x1 = own(every, X_COLS, cross)
        self.x2 = [own(every, X_COLS, x_to[s]) for s in (1, 3)]
        self.z1 = own(zq, Z_COLS, cross)
        self.z2 = [own(zq, Z_COLS, x_to[s]) for s in (1, 3, 2)]
        self.y1 = [own(half, Y_COLS, x_to[s]) for s in (1, 3, 2)]
        self.x3 = [pass_on(x, 1 - yh, every, X_COLS, x_to[s]) for s in (1, 3)]
        self.z3 = [pass_on(x, 1 - yh, zq, Z_COLS, x_to[s]) for s in (1, 3, 2)]
        self.y2 = [pass_on(every, yh, half, Y_COLS, y_to[s]) for s in (1, 3)]
        self.z4 = [pass_on(every, every, zq, Z_COLS, z_to[s]) for s in (1, 3)]
        before, after = lax.rem(x + 3, 4), lax.rem(x + 1, 4)
        self.x4 = [
            pass_on(before, yh, slice(0, 64), X_COLS, x_to[1]),
            pass_on(after, yh, slice(64, 128), X_COLS, x_to[3]),
        ]
        self.x5 = [
            pass_on(before, 1 - yh, slice(0, 64), X_COLS, x_to[1]),
            pass_on(after, 1 - yh, slice(64, 128), X_COLS, x_to[3]),
        ]
        before, after = lax.rem(y + 3, 4), lax.rem(y + 1, 4)
        self.y3 = [
            pass_on(every, before // 2, rows_at(lax.rem(before, 2) * 64, 32), Y_COLS, y_to[1]),
            pass_on(every, after // 2, rows_at(lax.rem(after, 2) * 64 + 32, 32), Y_COLS, y_to[3]),
        ]
        before, after = lax.rem(z + 3, 4), lax.rem(z + 1, 4)
        self.z5 = [
            pass_on(every, every, rows_at(before * 32, 16), Z_COLS, z_to[1]),
            pass_on(every, every, rows_at(after * 32 + 16, 16), Z_COLS, z_to[3]),
        ]
        self.swap = [
            pass_on(every, every, every, cols, {"core": 1 - core}) for cols in (X_COLS, Y_COLS, Z_COLS)
        ]
        self.place = [
            pltpu.make_async_copy(shard.at[g, rows, cols], dest(core, x, yh, rows, cols), local_sem.at[3 * g + n])
            for n, (rows, cols) in enumerate(((every, X_COLS), (half, Y_COLS), (zq, Z_COLS)))
        ]

    def start(self, copies):
        for copy in copies:
            copy.start()

    def arrive(self, copies):
        for copy in copies:
            copy.wait_recv()

    def stage(self, n):
        if n == 0:
            self.start([self.z1, self.x1, *self.z2, *self.y1, *self.x2, *self.place])
        elif n == 1:
            self.arrive([self.z1])
            self.start(self.z3)
            self.arrive([self.x1])
            self.start(self.x3)
            for copy in self.place:
                copy.wait()
        elif n == 2:
            self.arrive(self.y1)
            self.start(self.y2)
            self.arrive([*self.z2, *self.z3])
            self.start(self.z4)
        elif n == 3:
            self.arrive(self.x2)
            self.start(self.x4)
            self.arrive(self.y2)
            self.start(self.y3)
        elif n == 4:
            self.arrive(self.x3)
            self.start(self.x5)
            self.arrive(self.z4)
            self.start(self.z5)
        elif n == 5:
            self.arrive([*self.x4, *self.x5])
            self.start(self.swap[:1])
            self.arrive(self.y3)
            self.start(self.swap[1:2])
            self.arrive(self.z5)
            self.start(self.swap[2:])
        else:
            self.arrive(self.swap)
            for copy in (
                self.x1, self.z1, *self.x2, *self.z2, *self.y1, *self.x3, *self.z3, *self.y2, *self.z4,
                *self.x4, *self.x5, *self.y3, *self.z5, *self.swap,
            ):
                copy.wait_send()


def greet_all():
    barrier = pltpu.get_barrier_semaphore()
    place = lax.axis_index(CTX)
    others = [ctx_device(lax.rem(place + d, N_CTX)) for d in range(1, N_CTX)]
    others += [peer(axis, step)[0] for axis in ("x", "y") for step in (1, 2, 3)]
    for other in others:
        pl.semaphore_signal(barrier, inc=1, device_id=other, device_id_type=MESH_ID)
    pl.semaphore_wait(barrier, len(others))


def front_kernel(
    shard, vec_shard, x_ref, seg_ref,
    out_attn, out_ffn, out_vec, out_held, out_mixed, out_full, out_lse,
    wa, vecs, ready, held, mixed, out_t, keys, values_t, seg_col, scores,
    ag_send, ag_recv, vec_send, vec_recv, q_send, q_recv, o_send, o_recv, local_sem, out_sem,
):
    core = lax.axis_index("core")
    place = lax.axis_index(CTX)
    x, yh, yl = lax.axis_index("x"), lax.axis_index("yh"), lax.axis_index("yl")

    def dest(g):
        def view(c, xs, yhs, rows, cols):
            if g == 0:
                return wa.at[c, xs, yhs, rows, cols]
            start = (g - 1) * FF + c * GROUP + cols.start
            return out_ffn.at[xs, yhs, rows, pl.ds(pl.multiple_of(start, 128), cols.stop - cols.start)]

        return view

    gathers = [
        Gather(g, shard, dest(g), (ag_send, ag_recv), g * N_COPY, local_sem) for g in range(N_GROUPS)
    ]
    vec_sems = (vec_send, vec_recv)
    vec_cross = send(vec_shard, vecs.at[x, yh], vec_sems, 0, {"yh": 1 - yh, "yl": 1 - yl})
    vec_x = [send(vec_shard, vecs.at[x, yh], vec_sems, s, peer("x", s)[0]) for s in (1, 2, 3)]
    vec_x2 = [
        send(vecs.at[x, 1 - yh], vecs.at[x, 1 - yh], vec_sems, 3 + s, peer("x", s)[0]) for s in (1, 2, 3)
    ]
    greet_all()
    for copy in (vec_cross, *vec_x):
        copy.start()
    gathers[0].stage(0)
    vecs[x, yh] = vec_shard[...]
    for s in range(N_CTX):
        ready[s, :, 3 * HEAD :, :] = seg_ref[...]
    vec_cross.wait_recv()
    for copy in vec_x2:
        copy.start()
    for n in range(1, 7):
        gathers[0].stage(n)
    vec_cross.wait_send()
    for copy in (*vec_x, *vec_x2):
        copy.wait()

    for part in range(6):
        c, col = part // 3, (part % 3) * 512
        kind, first = part // 2, (part % 2) * 8
        value = jnp.zeros((ROWS, 512), f32)
        weight = wa[c, :, :, :, col : col + 512].reshape(D, 512)
        value = dot(x_ref[...], weight)
        if kind != 1:
            row = 0 if kind == 0 else 1
            value = value + jnp.concatenate(
                [vecs[f // 2, f % 2, row : row + 1, :].astype(f32) for f in range(first // 2, first // 2 + 4)], axis=1
            )
        value = value.T.astype(bf16)
        for h in range(8):
            for m in range(MB):
                ready[first + h, m, kind * HEAD : (kind + 1) * HEAD, :] = value[
                    h * HEAD : (h + 1) * HEAD, m * TOK : (m + 1) * TOK
                ]
    swaps = [[], []]
    for m in range(MB):
        for d in range(1, N_CTX):
            t = lax.rem(place + d, N_CTX)
            swaps[m].append(send(ready.at[t, m], held.at[place, m], (q_send, q_recv), m * N_CTX + d, ctx_device(t)))
            swaps[m][-1].start()
    held[place] = ready[place]
    returns = [[], []]
    for m in range(MB):
        for d in range(1, N_CTX):
            t = lax.rem(place + d, N_CTX)
            returns[m].append(
                send(out_t.at[t, m], mixed.at[place, m], (o_send, o_recv), m * N_CTX + d, ctx_device(t))
            )
    for gather in gathers[1:]:
        gather.stage(0)
    outs = []
    for c in range(2):
        outs.append((wa.at[c, :, :, :, 0:1536], out_attn.at[:, :, :, c * 1536 : (c + 1) * 1536]))
        outs.append((wa.at[c, :, :, :, 1536:2048], out_attn.at[:, :, :, 3072 + c * 512 : 3584 + c * 512]))
    outs = [pltpu.make_async_copy(src, dst, out_sem.at[n]) for n, (src, dst) in enumerate(outs)]
    for copy in outs:
        copy.start()
    for m in range(MB):
        for copy in swaps[m]:
            copy.wait_recv()
        load_side(held, m, keys, None, None, values_t, seg_col)

        def query_block(j, _, m=m):
            for n, at in enumerate(STEPS):
                if at // NBLK == m:

                    @pl.when(j == at % NBLK)
                    def _(n=n):
                        for gather in gathers[1:]:
                            gather.stage(n + 1)

            query_forward(held, m, j, out_t, out_full, out_lse, keys, values_t, seg_col, scores)
            return 0

        lax.fori_loop(0, NBLK, query_block, 0)
        for copy in returns[m]:
            copy.start()
        mixed[place, m] = out_t[place, m]
    last = [pltpu.make_async_copy(held, out_held, out_sem.at[4])]
    last[0].start()
    out_vec[...] = vecs[...]
    for n in range(len(STEPS) + 1, 7):
        for gather in gathers[1:]:
            gather.stage(n)
    for m in range(MB):
        for copy in swaps[m]:
            copy.wait_send()
        for copy in returns[m]:
            copy.wait()
    last.append(pltpu.make_async_copy(mixed, out_mixed, out_sem.at[5]))
    last[1].start()
    for copy in (*outs, *last):
        copy.wait()


def front(shard, vec_shard, x, seg_rows):
    vmem = pl.BlockSpec(memory_space=pltpu.VMEM)
    hbm = pl.BlockSpec(memory_space=pl.ANY)
    sem = lambda n: pltpu.SemaphoreType.DMA((n,))
    blocks = lambda rows, dt: (N_CTX, MB, rows, TOK)
    ffn_cols = 2 * FF if N_GROUPS > 1 else 128
    return pl.pallas_call(
        front_kernel,
        in_specs=[hbm, vmem, vmem, vmem],
        out_specs=[hbm, hbm, vmem, hbm, hbm, vmem, vmem],
        out_shape=[
            jax.ShapeDtypeStruct((4, 2, TOK, 4 * D), bf16),
            jax.ShapeDtypeStruct((4, 2, TOK, ffn_cols), bf16),
            jax.ShapeDtypeStruct((4, 2, 16, TOK), bf16),
            jax.ShapeDtypeStruct((N_CTX, MB, SENT, TOK), bf16),
            jax.ShapeDtypeStruct((N_CTX, MB, HEAD, TOK), bf16),
            jax.ShapeDtypeStruct((N_CTX, MB, HEAD, TOK), f32),
            jax.ShapeDtypeStruct((N_CTX, MB, 1, TOK), f32),
        ],
        scratch_shapes=[
            pltpu.VMEM((2, 4, 2, TOK, GROUP), bf16),
            pltpu.VMEM((4, 2, 16, TOK), bf16),
            pltpu.VMEM((N_CTX, MB, SENT, TOK), bf16),
            pltpu.VMEM((N_CTX, MB, SENT, TOK), bf16),
            pltpu.VMEM((N_CTX, MB, HEAD, TOK), bf16),
            pltpu.VMEM((N_CTX, MB, HEAD, TOK), bf16),
            pltpu.VMEM((PACK, HEAD), bf16),
            pltpu.VMEM((HEAD, PACK), bf16),
            pltpu.VMEM((PACK, TOK), f32),
            pltpu.VMEM((PACK, BLK), f32),
            sem(N_COPY * N_GROUPS), sem(N_COPY * N_GROUPS), sem(7), sem(7), sem(32), sem(32), sem(32), sem(32),
            sem(3 * N_GROUPS), sem(6),
        ],
        compiler_params=pltpu.CompilerParams(
            collective_id=2, has_side_effects=True, vmem_limit_bytes=48 * 2**20
        ),
        cost_estimate=pl.CostEstimate(
            flops=4 * MB * PACK * PACK * HEAD + 2 * ROWS * D * 3 * D, bytes_accessed=32 * 2**20,
            transcendentals=MB * PACK * PACK,
        ),
        name="front",
    )(shard, vec_shard, x, seg_rows)


def back_kernel(
    left_x, left_o, left_h, left_f, right_o, right_u, right_g, vec, grad_ready, held_in, full, lse,
    out_attn, out_ffn, out_vec, out_sq, out_q,
    peer_left, own_right, peer_right, own_vec, peer_vec,
    w_0, w_1, w_2, s1_0, s1_1, s1_2, s2_0, s2_1, s2_2,
    r1_0, r1_1, r1_2, r2_0, r2_1, r2_2, r3_0, r3_1, r3_2,
    gathered, sq_z, sq_y, sq_x, sq_c,
    held, grad_held, out_t, landed, right_q, keys, values, keys_t, seg_col, acc_k, acc_v, square_acc,
    swap_send, swap_recv, ring_send, ring_recv, gather_send, gather_recv, sq_send, sq_recv,
    o_send, o_recv, q_send, q_recv, local_sem, out_sem,
):
    core = lax.axis_index("core")
    other = 1 - core
    place = lax.axis_index(CTX)
    row_place = lax.axis_index("yl") * 4 + lax.axis_index("z")
    lefts = (left_x, left_o, left_h, left_f)
    rights = (None, right_o, right_u, right_g)
    works, firsts, seconds = (w_0, w_1, w_2), (s1_0, s1_1, s1_2), (s2_0, s2_1, s2_2)
    recvs = ((r1_0, r1_1, r1_2), (r2_0, r2_1, r2_2), (r3_0, r3_1, r3_2))
    to_core = {"core": other}

    fetch = pltpu.make_async_copy(held_in, held, local_sem.at[0])
    fetch.start()
    fetches = [fetch]
    for i in range(1, 4):
        cols = pl.ds(pl.multiple_of(core * WIDTHS[i], 512), WIDTHS[i])
        fetches.append(
            pltpu.make_async_copy(
                rights[i].at[:, cols], own_right.at[:, OFFSETS[i] : OFFSETS[i] + WIDTHS[i]], local_sem.at[i]
            )
        )
        fetches[-1].start()
    greet_all()

    pushes, returns = [[], []], [[], []]
    for m in range(MB):
        for d in range(1, N_CTX):
            t = lax.rem(place + d, N_CTX)
            to = ctx_device(t)
            pushes[m].append(
                send(grad_ready.at[t, m], grad_held.at[place, m], (o_send, o_recv), m * N_CTX + d, to)
            )
            returns[m].append(send(out_t.at[t, m], landed.at[place, m], (q_send, q_recv), m * N_CTX + d, to))
    swaps = []
    for i in (2, 3, 1, 0):
        swaps.append(send(lefts[i], peer_left.at[i], (swap_send, swap_recv), 2 * i, to_core))
        if i:
            from_cols = pl.ds(pl.multiple_of(other * WIDTHS[i], 512), WIDTHS[i])
            swaps.append(
                send(
                    rights[i].at[:, from_cols], peer_right.at[:, OFFSETS[i] : OFFSETS[i] + WIDTHS[i]],
                    (swap_send, swap_recv), 2 * i + 1, to_core,
                )
            )
    for m in range(MB):
        for copy in pushes[m]:
            copy.start()
    for copy in swaps:
        copy.start()
    grad_held[place] = grad_ready[place]
    for copy in fetches:
        copy.wait()

    def blocks(b):
        out = [(p, b * COLS, COLS) for p in range(3)]
        if b == 3:
            out.append((0, VEC_AT, 128))
        return out

    def copies(p, phase, at, width):
        order = ORDERS[p]
        axis = order[phase]
        cols = slice(at, at + width)
        src = (works, firsts, seconds)[phase][p]
        out = []
        for step in (1, 2, 3):
            to, index = peer(axis, step)
            chunk = pick(src, axis, index, dims_after(order, phase), cols)
            land = recvs[phase][p].at[(step - 1, *(slice(None),) * (len(lead(order, phase + 1)) + 1), cols)]
            out.append(
                send(chunk, land, (ring_send, ring_recv), ((p * 3 + phase) * 5 + at // COLS) * 3 + step - 1, to)
            )
        return out

    def multiply(p, b):
        i, col = PRODUCT[p][b]
        if i == 0:
            mine = right_q.at[:, pl.ds(pl.multiple_of(core * WIDTHS[0] + col, 512), COLS)]
        else:
            mine = own_right.at[:, OFFSETS[i] + col : OFFSETS[i] + col + COLS]
        theirs = peer_right.at[:, OFFSETS[i] + col : OFFSETS[i] + col + COLS]

        def rows_block(x, _):
            rows = pl.ds(pl.multiple_of(x * 256, 256), 256)
            value = dot(lefts[i][rows, :], mine[...]) + dot(peer_left[i, rows, :], theirs[...])
            works[p][x, :, :, :, :, b * COLS : (b + 1) * COLS] = value.astype(bf16).reshape(2, 2, 4, 16, COLS)
            return 0

        lax.fori_loop(0, 4, rows_block, 0)

    def reduce(phase, p, at, width):
        cols = slice(at, at + width)
        order = ORDERS[p]
        axis = order[phase]
        src = (works, firsts, seconds)[phase][p]
        land = recvs[phase][p]
        for copy in copies(p, phase, at, width):
            copy.wait()
        own = pick(src, axis, coordinate(axis), dims_after(order, phase), cols)
        rest = len(lead(order, phase + 1)) - 1
        if phase < 2:
            dst = (firsts, seconds)[phase][p]

            def add(n, _):
                tail = (*(slice(None),) * (rest + 1), cols)
                inner = (*(slice(None),) * (rest + 1), slice(None))
                value = own[(n, *inner)].astype(f32)
                for step in range(3):
                    value = value + land[(step, n, *tail)].astype(f32)
                dst[(n, *tail)] = value.astype(bf16)
                return 0

            lax.fori_loop(0, lead(order, phase + 1)[0], add, 0)
            for copy in copies(p, phase + 1, at, width):
                copy.start()
            return
        value = own[...].astype(f32)
        for step in range(3):
            value = value + land[step, :, cols].astype(f32)
        to = p * 2048 + at if width == COLS else 6144
        gathered[core, row_place, :, to : to + width] = value.astype(bf16)
        square = value * value
        if width != COLS:
            square = square * jnp.where(core == 0, 1.0, 0.0)
        squares = square_acc[...]
        for c in range(0, width, 128):
            squares = squares + square[:8, c : c + 128] + square[8:, c : c + 128]
        square_acc[...] = squares

    square_acc[...] = jnp.zeros_like(square_acc)
    for copy in swaps:
        copy.wait()
    for b in range(3):
        for p, at, width in blocks(b):
            multiply(p, b)
            for copy in copies(p, 0, at, width):
                copy.start()

    for m in range(MB):
        load_side(held, m, keys, values, keys_t, None, seg_col)
        acc_k[...] = jnp.zeros_like(acc_k)
        acc_v[...] = jnp.zeros_like(acc_v)
        for copy in pushes[m]:
            copy.wait_recv()

        def query_block(j, _, m=m):
            for at, tasks in TASKS.items():
                if at // NBLK == m:

                    @pl.when(j == at % NBLK)
                    def _(tasks=tasks):
                        for phase, b, p in tasks:
                            reduce(phase, p, b * COLS, COLS)

            query_t = pair(held, m, j, slice(0, HEAD))
            seg_row = pair(held, m, j, slice(3 * HEAD, 3 * HEAD + 1)).astype(f32)
            grad_t = pair(grad_held, m, j, slice(0, HEAD))
            row_lse = pair(lse, m, j, slice(0, 1))
            delta = jnp.sum(grad_t.astype(f32) * pair(full, m, j, slice(0, HEAD)), axis=0, keepdims=True)
            acc_q = jnp.zeros((HEAD, BLK), f32)
            for k in range(NBLK):
                at = slice(k * BLK, (k + 1) * BLK)
                s = dot(keys[at, :], query_t) * SCALE2 - row_lse
                col = seg_col[at, :]
                same = jnp.concatenate([col, col], axis=1) == seg_row
                p = jnp.exp2(jnp.where(same, s, NEG_LARGE))
                dp = dot(values[at, :], grad_t)
                ds = (p * (dp - delta)).astype(bf16)
                acc_q = acc_q + dot(keys_t[:, at], ds)
                acc_k[:, at] += dot_nt(query_t, ds)
                acc_v[:, at] += dot_nt(grad_t, p.astype(bf16))
            acc_q = (acc_q * SCALE).astype(bf16)
            out_t[2 * j, m, :HEAD, :] = acc_q[:, :TOK]
            out_t[2 * j + 1, m, :HEAD, :] = acc_q[:, TOK:]
            return 0

        lax.fori_loop(0, NBLK, query_block, 0)
        for s in range(N_CTX):
            at = slice(s * TOK, (s + 1) * TOK)
            out_t[s, m, HEAD : 2 * HEAD, :] = (acc_k[:, at] * SCALE).astype(bf16)
            out_t[s, m, 2 * HEAD :, :] = acc_v[:, at].astype(bf16)
        for copy in returns[m]:
            copy.start()
        landed[place, m] = out_t[place, m]

    done = [task for tasks in TASKS.values() for task in tasks]
    for phase in (0, 1):
        for b in range(3):
            for p in range(3):
                if (phase, b, p) not in done:
                    reduce(phase, p, b * COLS, COLS)
    for m in range(MB):
        for copy in pushes[m]:
            copy.wait_send()
        for copy in returns[m]:
            copy.wait()
        for i in range(HEADS // 2):
            for kind in range(3):
                rows = slice(kind * HEAD, (kind + 1) * HEAD)
                both = jnp.concatenate([landed[2 * i, m, rows, :], landed[2 * i + 1, m, rows, :]], axis=0)
                right_q[m * TOK : (m + 1) * TOK, kind * D + i * 128 : kind * D + (i + 1) * 128] = both.T
    give = send(
        right_q.at[:, pl.ds(pl.multiple_of(other * WIDTHS[0], 512), WIDTHS[0])], peer_right.at[:, 0 : WIDTHS[0]],
        (swap_send, swap_recv), 1, to_core,
    )
    give.start()
    sum_q = jnp.sum(right_q[:, :D].astype(f32), axis=0, keepdims=True)
    sum_v = jnp.sum(right_q[:, 2 * D :].astype(f32), axis=0, keepdims=True)
    row = lax.broadcasted_iota(jnp.int32, (16, TOK), 0)
    own_vec[...] = jnp.zeros_like(own_vec)
    for f in range(N_FSDP):
        cols = slice(f * TOK, (f + 1) * TOK)
        value = jnp.where(row == 0, sum_q[:, cols], jnp.where(row == 1, sum_v[:, cols], vec[f]))
        own_vec[f // 2, f % 2, 0, 0] = value.astype(bf16)
    give_vec = send(own_vec, peer_vec, (swap_send, swap_recv), 8, to_core)
    give_vec.start()
    keep_q = pltpu.make_async_copy(right_q, out_q, local_sem.at[4])
    keep_q.start()
    give.wait()
    for p, at, width in blocks(3):
        if width == COLS:
            multiply(p, 3)
        else:
            give_vec.wait()
            works[0][:, :, :, :, :, VEC_AT:] = (own_vec[...].astype(f32) + peer_vec[...].astype(f32)).astype(bf16)
        for copy in copies(p, 0, at, width):
            copy.start()
    for b in range(3):
        for p, at, width in blocks(b):
            reduce(2, p, at, width)
    for phase in range(3):
        for p, at, width in blocks(3):
            reduce(phase, p, at, width)
    squares = square_acc[...]
    yl, z = lax.axis_index("yl"), lax.axis_index("z")
    z_first, y_first = slice(0, HALF_Z), slice(HALF_Z, 6272)
    to_y = {"yl": 1 - yl}
    gather_sems = (gather_send, gather_recv)
    sq_sems = (sq_send, sq_recv)

    def spread(buffer, axis, base):
        at = coordinate(axis)
        out = []
        for step in (1, 2, 3):
            out.append(send(buffer.at[at], buffer.at[at], sq_sems, base + step - 1, peer(axis, step)[0]))
        return out

    def total(buffer):
        return (buffer[0] + buffer[1]) + (buffer[2] + buffer[3])

    sq_z[z] = squares
    squares_z = spread(sq_z, "z", 0)
    first_z = [
        send(gathered.at[core, row_place, :, z_first], gathered.at[core, row_place, :, z_first], gather_sems, step - 1, peer("z", step)[0])
        for step in (1, 2, 3)
    ]
    first_y = send(gathered.at[core, row_place, :, y_first], gathered.at[core, row_place, :, y_first], gather_sems, 3, to_y)
    for copy in (*squares_z, *first_z, first_y):
        copy.start()
    for copy in squares_z:
        copy.wait()
    y_at = coordinate("y")
    sq_y[y_at] = total(sq_z)
    squares_y = spread(sq_y, "y", 3)
    for copy in squares_y:
        copy.start()
    for copy in (*first_z, first_y):
        copy.wait()
    quarter = pl.ds(yl * 4, 4)
    second_y = send(
        gathered.at[core, quarter, :, z_first], gathered.at[core, quarter, :, z_first], gather_sems, 4, to_y
    )
    second_y.start()
    second_z = []
    for step in (1, 2, 3):
        for half in range(2):
            view = gathered.at[core, half * 4 + z, :, y_first]
            second_z.append(send(view, view, gather_sems, 5 + (step - 1) * 2 + half, peer("z", step)[0]))
    for copy in second_z:
        copy.start()
    for copy in squares_y:
        copy.wait()
    x_at = coordinate("x")
    sq_x[x_at] = total(sq_y)
    squares_x = spread(sq_x, "x", 6)
    for copy in squares_x:
        copy.start()
    for copy in squares_x:
        copy.wait()
    sq_c[core] = total(sq_x)
    square_c = send(sq_c.at[core], sq_c.at[core], sq_sems, 9, to_core)
    square_c.start()
    square_c.wait()
    out_sq[...] = sq_c[0] + sq_c[1]
    second_y.wait()
    for copy in second_z:
        copy.wait()
    last = send(gathered.at[core], gathered.at[core], gather_sems, 11, to_core)
    last.start()
    last.wait()
    locals_ = []
    for c in range(2):
        for p in range(3):
            for b in range(4):
                i, col = PRODUCT[p][b]
                target, base = ((out_attn, 0), (out_attn, 3072), (out_ffn, 0), (out_ffn, FF))[i]
                base = base + c * WIDTHS[i] + col
                at = p * 2048 + b * COLS
                locals_.append(
                    pltpu.make_async_copy(
                        gathered.at[c, :, :, at : at + COLS], target.at[:, :, base : base + COLS],
                        out_sem.at[len(locals_)],
                    )
                )
    locals_.append(pltpu.make_async_copy(gathered.at[0, :, :, 6144:], out_vec, out_sem.at[len(locals_)]))
    for copy in locals_:
        copy.start()
    for copy in locals_:
        copy.wait()
    keep_q.wait()


def back(lefts, rights, vec, grad_ready, held, full, lse):
    vmem = pl.BlockSpec(memory_space=pltpu.VMEM)
    hbm = pl.BlockSpec(memory_space=pl.ANY)
    scratch = [
        pltpu.VMEM((4, D, ROWS), bf16),
        pltpu.VMEM((ROWS, 6144), bf16),
        pltpu.VMEM((ROWS, 6144), bf16),
        pltpu.VMEM((4, 2, 2, 4, 16, 128), bf16),
        pltpu.VMEM((4, 2, 2, 4, 16, 128), bf16),
    ]
    for n in range(3):
        scratch += [pltpu.VMEM((*lead(ORDERS[p], n), 16, PART_COLS[p]), bf16) for p in range(3)]
    for n in range(1, 4):
        scratch += [pltpu.VMEM((3, *lead(ORDERS[p], n), 16, PART_COLS[p]), bf16) for p in range(3)]
    scratch += [
        pltpu.VMEM((2, 8, 16, 6272), bf16),
        pltpu.VMEM((4, 8, 128), f32),
        pltpu.VMEM((4, 8, 128), f32),
        pltpu.VMEM((4, 8, 128), f32),
        pltpu.VMEM((2, 8, 128), f32),
        pltpu.VMEM((N_CTX, MB, SENT, TOK), bf16),
        pltpu.VMEM((N_CTX, MB, HEAD, TOK), bf16),
        pltpu.VMEM((N_CTX, MB, 3 * HEAD, TOK), bf16),
        pltpu.VMEM((N_CTX, MB, 3 * HEAD, TOK), bf16),
        pltpu.VMEM((ROWS, 3 * D), bf16),
        pltpu.VMEM((PACK, HEAD), bf16),
        pltpu.VMEM((PACK, HEAD), bf16),
        pltpu.VMEM((HEAD, PACK), bf16),
        pltpu.VMEM((PACK, TOK), f32),
        pltpu.VMEM((HEAD, PACK), f32),
        pltpu.VMEM((HEAD, PACK), f32),
        pltpu.VMEM((8, 128), f32),
    ]
    for count in (9, 9, 135, 135, 12, 12, 10, 10, 32, 32, 32, 32, 5, 25):
        scratch.append(pltpu.SemaphoreType.DMA((count,)))
    out = pl.pallas_call(
        back_kernel,
        in_specs=[vmem] * 4 + [hbm] * 3 + [vmem, vmem, hbm, vmem, vmem],
        out_specs=[hbm, hbm, hbm, vmem, hbm],
        out_shape=[
            jax.ShapeDtypeStruct((8, 16, 4 * D), bf16),
            jax.ShapeDtypeStruct((8, 16, 2 * FF), bf16),
            jax.ShapeDtypeStruct((8, 16, 128), bf16),
            jax.ShapeDtypeStruct((8, 128), f32),
            jax.ShapeDtypeStruct((ROWS, 3 * D), bf16),
        ],
        scratch_shapes=scratch,
        compiler_params=pltpu.CompilerParams(
            collective_id=1, has_side_effects=True, vmem_limit_bytes=60 * 2**20
        ),
        cost_estimate=pl.CostEstimate(
            flops=2 * 512 * D * 6144 + 10 * MB * PACK * PACK * HEAD, bytes_accessed=16 * 2**20,
            transcendentals=MB * PACK * PACK,
        ),
        name="back",
    )(*lefts, *rights, vec, grad_ready, held, full, lse)
    return out[0].reshape(TOK, 4 * D), out[1].reshape(TOK, 2 * FF), out[2][0, :12], jnp.sum(out[3]), out[4]


def layer_stats(values, gain_row, shift_row):
    center = values - jnp.mean(values, axis=-1, keepdims=True)
    inverse = lax.rsqrt(jnp.mean(center * center, axis=-1, keepdims=True) + NORM_EPS)
    normal = center * inverse
    return (normal * gain_row + shift_row, normal, inverse)


def layer_back(grad_value, normal, inverse, gain_row):
    scaled = grad_value * gain_row
    return inverse * (
        scaled
        - jnp.mean(scaled, axis=-1, keepdims=True)
        - normal * jnp.mean(scaled * normal, axis=-1, keepdims=True)
    )


def column_sum(values):
    return jnp.sum(values.astype(f32), axis=0)


def adamw(weight, grad_value, first, second, rate, decay):
    first_new = BETA_FIRST * first + (1.0 - BETA_FIRST) * grad_value
    second_new = BETA_SECOND * second + (1.0 - BETA_SECOND) * grad_value * grad_value
    first_hat = first_new / (1.0 - BETA_FIRST**STEP)
    second_hat = second_new / (1.0 - BETA_SECOND**STEP)
    weight_new = weight - rate * (first_hat / (jnp.sqrt(second_hat) + ADAM_EPS) + decay * weight)
    return (weight_new, first_new, second_new)


def to_heads(rows, parts):
    t = rows.T.reshape(parts, HEADS, HEAD, MB, TOK)
    return jnp.transpose(t, (1, 3, 0, 2, 4)).reshape(HEADS, MB, parts * HEAD, TOK)


def from_heads(blocks, parts):
    t = blocks.reshape(HEADS, MB, parts, HEAD, TOK)
    return jnp.transpose(t, (1, 4, 2, 0, 3)).reshape(ROWS, parts * D)


def shards(
    tokens, cotangent, dest, lengths, attn_weight, attn_first, attn_second,
    ffn_weight, ffn_first, ffn_second, vectors, vec_first, vec_second,
):
    place, core = lax.axis_index(CTX), lax.axis_index("core")

    def half(weight, base, width):
        return lax.dynamic_slice_in_dim(weight, base + core * width, width, 1).astype(bf16)

    attn_half = jnp.concatenate([half(attn_weight, 0, 1536), half(attn_weight, 3 * D, 512)], axis=1)
    own_rows = D // N_FSDP // N_CTX
    if N_GROUPS == 1:
        shard = attn_half[None]
        w_ffn = lax.all_gather(
            lax.dynamic_slice_in_dim(ffn_weight, place * own_rows, own_rows).astype(bf16), ALL, axis=0, tiled=True
        )
    else:
        shard = jnp.stack([attn_half, half(ffn_weight, 0, GROUP), half(ffn_weight, FF, GROUP)])

    x = tokens.reshape(ROWS, D)
    cot = cotangent.reshape(ROWS, D).astype(f32)
    ends = jnp.cumsum(lengths[:, 0], axis=1)
    seg = jnp.sum((dest[:, 0, :, None] >= ends[:, None, :]).astype(jnp.int32), axis=2)
    keep = (seg.reshape(ROWS, 1) < 8).astype(f32)

    seg_rows = jnp.broadcast_to(seg.astype(bf16)[:, None, :], (MB, 16, TOK))
    vec_shard = jnp.pad(vectors.astype(bf16), ((0, 4), (0, 0)))
    w_attn, ffn_out, vecs, held, mixed_t, mixed_full, lse = front(shard, vec_shard, x, seg_rows)
    w_attn = w_attn.reshape(D, 4 * D)
    if N_GROUPS > 1:
        w_ffn = ffn_out.reshape(D, 2 * FF)
    small = jnp.transpose(vecs.reshape(N_FSDP, 16, TOK), (1, 0, 2)).reshape(16, D)[:12].astype(f32)
    w_qkv, w_out = w_attn[:, : 3 * D], w_attn[:, 3 * D :]
    w_one, w_two = w_ffn[:, :FF], w_ffn[:, FF:]
    mixed = from_heads(mixed_t, 1)

    branch = dot(mixed, w_out) + small[2]
    normed_one, normal_one, inverse_one = layer_stats(x.astype(f32) + branch, small[4], small[5])
    normed_low = normed_one.astype(bf16)
    hidden_pre = dot(normed_low, w_one) + small[8:].reshape(FF)
    activ, gelu_back = jax.vjp(partial(jax.nn.gelu, approximate=False), hidden_pre)
    activ_low = activ.astype(bf16)
    ffn_out = dot_nt(activ_low, w_two) + small[3]
    output, normal_two, inverse_two = layer_stats(normed_one + ffn_out, small[6], small[7])
    output = output * keep
    grad_out = cot * keep
    grad_two = layer_back(grad_out, normal_two, inverse_two, small[6])
    ffn_grad_low = grad_two.astype(bf16)
    grad_hidden = gelu_back(dot(ffn_grad_low, w_two))[0].astype(bf16)
    grad_normed = dot_nt(grad_hidden, w_one) + grad_two
    grad_one = layer_back(grad_normed, normal_one, inverse_one, small[4])
    branch_grad_low = grad_one.astype(bf16)
    grad_mixed = dot_nt(branch_grad_low, w_out).astype(bf16)

    step_vec = jnp.concatenate(
        [
            jnp.stack(
                [
                    jnp.zeros((D,), f32),
                    jnp.zeros((D,), f32),
                    column_sum(branch_grad_low),
                    column_sum(ffn_grad_low),
                    jnp.sum(grad_normed * normal_one, axis=0),
                    jnp.sum(grad_normed, axis=0),
                    jnp.sum(grad_out * normal_two, axis=0),
                    jnp.sum(grad_out, axis=0),
                ]
            ),
            column_sum(grad_hidden).reshape(4, D),
        ],
        axis=0,
    )
    vec_rows = jnp.transpose(step_vec.reshape(12, N_FSDP, TOK), (1, 0, 2))
    vec_rows = jnp.pad(vec_rows, ((0, 0), (0, 4), (0, 0)))
    total_attn, total_ffn, total_vec, square_sum, grad_qkv = back(
        (x.T, mixed.T, normed_low.T, ffn_grad_low.T),
        (branch_grad_low, grad_hidden, activ_low),
        vec_rows,
        to_heads(grad_mixed, 1),
        held,
        mixed_full,
        lse,
    )
    grad_tokens = grad_one + dot_nt(grad_qkv, w_qkv)
    total_attn, total_ffn, total_vec = total_attn.astype(f32), total_ffn.astype(f32), total_vec.astype(f32)
    grad_norm = jnp.sqrt(square_sum)
    factor = jnp.minimum(1.0, CLIP_NORM / (grad_norm + 1e-06))
    rate_matrix = D ** (-0.5)
    attn_new, attn_first_new, attn_second_new = adamw(
        attn_weight, total_attn * factor, attn_first, attn_second, ATTN_RATE_SCALE * rate_matrix, WEIGHT_DECAY
    )
    ffn_new, ffn_first_new, ffn_second_new = adamw(
        ffn_weight, total_ffn * factor, ffn_first, ffn_second, rate_matrix, WEIGHT_DECAY
    )
    vec_new, vec_first_new, vec_second_new = adamw(
        vectors, total_vec * factor, vec_first, vec_second, RATE_VECTOR, 0.0
    )
    return (
        output.astype(bf16).reshape(tokens.shape),
        grad_tokens.astype(bf16).reshape(tokens.shape),
        grad_norm,
        attn_new, attn_first_new, attn_second_new,
        ffn_new, ffn_first_new, ffn_second_new,
        vec_new, vec_first_new, vec_second_new,
        attn_new.astype(bf16),
        ffn_new.astype(bf16),
        total_vec[2] * factor,
    )


def solution(mesh):
    fine = Mesh(mesh.devices.reshape(2, 4, 2, 4, 2), ("yl", "z", "core", "x", "yh"))
    act = P(None, FSDP, CTX, None)
    row = P(FSDP, None)
    col = P(None, FSDP)
    return jax.shard_map(
        shards,
        mesh=fine,
        in_specs=(act, act, P(None, FSDP, CTX), P(None, FSDP, None), row, row, row, row, row, row, col, col, col),
        out_specs=(act, act, P(), row, row, row, row, row, row, col, col, col, row, row, P(FSDP)),
        check_vma=False,
    )
```

time: 465 us -> 357 us (0.77)
  waiting for transfers between devices: 123 us -> 0 us
  Pallas kernels: 170 us -> 262 us
  blocking collectives: 41 us -> 0 us
  between operations: 16.5 us -> 3.42 us
  starting transfers between devices: 9.78 us -> 0 us
  local copies, waits for them, and re-layouts: 19.9 us -> 11.7 us
  matrix products: 51 us -> 45.8 us
    all_gather x1 -> x0, waiting for transfers between devices: 97.2 us -> none  [shards(): full = lax.all_gather(both, ALL, axis=0, tiled=True)]
    pallas_call x3 -> x2, Pallas kernels: 170 us -> 262 us  [the longest x1 148 us: back(): pl.pallas_call(back_kernel, in_specs=[vmem] * 4 + [hbm] * 3 + [vmem, vmem...]
    all_to_all x2 -> x0, blocking collectives: 41 us -> none  [swap(): return lax.all_to_all(value, CTX, 0, 0, tiled=True)]
    all_to_all x2 -> x0, waiting for transfers between devices: 25.3 us -> none  [swap(): return lax.all_to_all(value, CTX, 0, 0, tiled=True)]
    all_to_all x2 -> x0, starting transfers between devices: 9.74 us -> none  [swap(): return lax.all_to_all(value, CTX, 0, 0, tiled=True)]
    dot_general x4, matrix products: 21.7 us -> 16.6 us  [dot_nt(): return lax.dot_general(a, b, CONTRACT_COLS, preferred_element_type=f32)]
    dot_general x4 -> x3, matrix products: 29.3 us -> 29.2 us  [dot(): return jnp.dot(a, b, preferred_element_type=f32)]
  transfers between devices with their start and end apart: 3 -> 0, of which waited for: 3 -> 0; matrix products, arithmetic and copies ran while one was open for 2% -> 0% of each run, Pallas kernels for 0% -> 0%
where the time goes in v2:
time: 357 us; the launch traced here: 351 us
  Pallas kernels  262 us (73%)
  matrix products  45.8 us (13%)
  other arithmetic  27.8 us (8%)
  local copies, waits for them, and re-layouts  11.7 us (3%)
    pallas_call x1, Pallas kernels, back(): pl.pallas_call(back_kernel, in_specs=[vmem] * 4 + [hbm] * 3 + [vmem, vmem...  148 us
    pallas_call x1, Pallas kernels, front(): pl.pallas_call(front_kernel, in_specs=[hbm, vmem, vmem, vmem], out_specs=...  114 us
    dot_general x3, matrix products, dot(): return jnp.dot(a, b, preferred_element_type=f32)  29.2 us
    dot_general x4, matrix products, dot_nt(): return lax.dot_general(a, b, CONTRACT_COLS, preferred_element_type=f32)  16.6 us
    convert_element_type x1, other arithmetic, shards(): ffn_new.astype(bf16)  10.2 us

profile of v2, /device:TPU:1, one launch (start us, length us, event | category | flops | bytes accessed | tf_op | source)
XLA Modules:
  0.0 350.6 jit_solution(8944556159956000868)
XLA Ops:
  0.6 0.0 copy-start.16
  0.7 0.0 copy-start.15
  0.7 0.0 copy-start
  0.7 0.0 copy-start.12
  0.7 1.2 dynamic-slice_convert_fusion.2
  1.9 1.0 dynamic-slice_convert_fusion.3
  2.9 1.8 fusion.56
  4.7 0.2 pad_maximum_fusion.shard
  4.9 0.0 copy-done.16
  4.9 0.2 reduce_window_sum.14
  5.1 0.0 copy-done.15
  5.1 0.1 convert_reduce_fusion.3
  5.2 0.0 copy-done.12
  5.2 0.0 copy-done
  5.2 114.0 %front.1 = (bf16[4,2,128,4096]{3,2,1,0:T(8,128)(2,1)}, bf16[4,2,128,8192]{3,2,1,0:T(8,128)(2,1)}, bf16[4,2,16,128]{3,2,1,0:T(8,128)(2,1)S(1)}, bf16[16,2,208,128...) custom-call(bf16[3,128,2048]{2,1,0:T(8,128)(2,1)S(1)} %pad_maximum_f, ...), custom_call_target="tpu_custom_call" | custom-call | flops 3758096384 | bytes 33554432 | tf_op jit(solution)/shard_map/front/pallas_call | solution.py:439
  119.2 0.0 copy-start.1
  119.2 0.0 copy-start.2
  119.2 0.5 copy.43
  119.8 2.7 fusion.76
  122.6 0.3 multiply_reduce_fusion.6
  122.9 15.9 %multiply_convert_fusion = (bf16[256,4096]{1,0:T(8,128)(2,1)S(1)}, f32[256,4096]{1,0:T(8,128)}, f32[256,4096]{1,0:T(8,128)}) fusion(f32[4096]{0:T(1024)S(1)} %slice_bitcast_fusion, bf16[1024,8192]{1,0:T(8,128)(2,1)} %bitcast.134, f32[256,1024]{1,0:T(8,128)S(1)} %get-tuple-element.123, f32[1024]{0:T(1024)S(1)} %get-tuple-element.117, ...), kind=kOutput, calls=%fused_computation.21 | convolution fusion | flops 2218000384 | bytes 19949568 | tf_op jit(solution)/shard_map/dot_general | solution.py:49
  138.8 0.0 copy-done.2
  138.8 0.0 copy-start.18
  138.8 0.0 copy-start.5
  138.8 6.7 %fusion.77 = (f32[256]{0:T(256)S(1)}, f32[256,1024]{1,0:T(8,128)S(1)}) fusion(f32[1024]{0:T(1024)S(1)} %get-tuple-element.116, bf16[256,4096]{1,0:T(8,128)(2,1)S(1)} %get-tuple-element.108.right_g, bf16[1024,8192]{1,0:T(8,128)(2,1)} %bitcast.135, f32[1024]{0:T(1024)S(1)} %get-tuple-element.117, f32[1024]{0:T(1024)S(1)} %get-tuple-element.118, ...), kind=kOutput, calls=%fused_computation.120 | convolution fusion | flops 2149318400 | bytes 12598272 | tf_op jit(solution)/shard_map/dot_general | solution.py:53
  145.5 0.2 multiply_reduce_fusion.5
  145.8 0.0 copy-done.5
  145.8 0.5 multiply_reduce_fusion
  146.3 0.3 fusion.54
  146.7 0.0 slice-start
  146.7 1.3 convert_reduce_fusion.1
  148.0 10.5 %convert_reduce_fusion = (f32[4096]{0:T(1024)S(1)}, bf16[256,4096]{1,0:T(8,128)(2,1)}) fusion(f32[256,4096]{1,0:T(8,128)} %get-tuple-element.109, f32[256,4096]{1,0:T(8,128)} %get-tuple-element.124, bf16[1024,8192]{1,0:T(8,128)(2,1)} %bitcast.136, f32[256,1024]{1,0:T(8,128)S(1)} %get-tuple-element.104), kind=kOutput, calls=%fused_computation.19 | convolution fusion | flops 2164518912 | bytes 19939328 | tf_op jit(solution)/shard_map/dot_general | solution.py:49
  158.6 4.1 %fusion.38 = f32[256,1024]{1,0:T(8,128)S(1)} fusion(f32[256,1024]{1,0:T(8,128)S(1)} %get-tuple-element.104, bf16[256,4096]{1,0:T(8,128)(2,1)} %get-tuple-element.128.right_u, bf16[1024,8192]{1,0:T(8,128)(2,1)S(1)} %bitcast.139), kind=kOutput, calls=%fused_computation.49 | convolution fusion | flops 2147745792 | bytes 12582912 | tf_op jit(solution)/shard_map/dot_general | solution.py:53
  162.7 0.7 multiply_reduce_fusion.1
  163.4 1.3 convert_reduce_fusion.2
  164.7 0.8 copy-done.11
  165.5 3.1 fusion.47
  168.6 1.2 reshape.210
  169.8 0.9 copy.63
  170.8 0.1 concatenate.33
  170.8 0.6 pad.9.vec
  171.5 1.0 copy.48.left_h
  172.5 0.1 convert_bitcast_fusion
  172.5 1.0 copy.49.left_f
  173.5 0.9 copy.62
  174.4 1.0 copy.47.left_x
  175.4 147.9 %back.1 = (bf16[8,16,4096]{2,1,0:T(8,128)(2,1)}, bf16[8,16,8192]{2,1,0:T(8,128)(2,1)}, bf16[8,16,128]{2,1,0:T(8,128)(2,1)}, f32[8,128]{1,0:T(8,128)}, bf16[256,3072]{1,0:T(8,128)(2,1)}) custom-call(bf16[1024,256]{1,0:T(8,128)(2,1)} %copy.47.left_x, bf16[1024,256]{1,0:T(8,128)(2,1)} %bitcast.121, bf16[1024,256]{1,0:T(8,128)(2,1)} %copy.48.left_h, ...), custom_call_target="tpu_custom_call" | custom-call | flops 11811160064 | bytes 16777216 | tf_op jit(solution)/shard_map/back/pallas_call | solution.py:844
  323.4 0.7 slice_convert_fusion.1
  324.1 1.3 reduce_sum.169
  326.1 0.0 copy-start.4
  326.1 0.5 fusion.62
  326.6 0.0 copy-done.13
  326.6 1.6 multiply_subtract_fusion.2
  328.2 2.2 convert_multiply_fusion
  330.4 0.0 copy-done.4
  330.4 0.0 copy-start.9
  330.4 0.0 copy-start.7
  330.4 0.0 copy-start.8
  330.4 0.0 slice-start.5
  330.4 10.2 %fusion.67 = (bf16[128,8192]{1,0:T(8,128)(2,1)}, f32[128,8192]{1,0:T(8,128)}, f32[128,8192]{1,0:T(8,128)}, f32[128,8192]{1,0:T(8,128)}) fusion(f32[128,8192]{1,0:T(8,128)S(1)} %copy-done.4, f32[8,16,8192]{2,1,0:T(8,128)S(1)} %convert_multiply_fusion, f32[128,8192]{1,0:T(8,128)} %param.21, f32[128,8192]{1,0:T(8,128)} %param.22), kind=kLoop, calls=%fused_computation.117 | loop fusion | flops 16777216 | bytes 31457280 | tf_op jit(solution)/shard_map/convert_element_type | solution.py:1012
  340.6 0.2 convert_multiply_fusion.1
  340.9 1.3 copy-done.6
  342.2 4.2 %fusion.70 = (bf16[128,4096]{1,0:T(8,128)(2,1)}, f32[128,4096]{1,0:T(8,128)}, f32[128,4096]{1,0:T(8,128)}, f32[128,4096]{1,0:T(8,128)}) fusion(f32[128,4096]{1,0:T(8,128)S(1)} %copy-done.6, f32[8,16,4096]{2,1,0:T(8,128)S(1)} %convert_multiply_fusion.1, f32[128,4096]{1,0:T(8,128)S(1)} %copy-done.7, f32[128,4096]{1,0:T(8,128)S(1)} %copy-done.8), kind=kLoop, calls=%fused_computation.118 | loop fusion | flops 8388608 | bytes 15728640 | tf_op jit(solution)/shard_map/convert_element_type | solution.py:1011
  346.4 2.6 fusion.50
  (47 shorter events, 0.2 us)
Async XLA Ops:
  0.6 4.2 %copy-start.16 = (s32[2,1,8]{2,1,0:T(1,128)S(1)}, s32[2,1,8]{2,1,0:T(1,128)}, u32[]{:S(2)}) copy-start(s32[2,1,8]{2,1,0:T(1,128)} %param.16) | copy-start | bytes 196
  0.7 4.4 %copy-start.15 = (s32[2,1,128]{2,1,0:T(1,128)S(1)}, s32[2,1,128]{2,1,0:T(1,128)}, u32[]{:S(2)}) copy-start(s32[2,1,128]{2,1,0:T(1,128)} %param.15) | copy-start | bytes 3076
  0.7 4.5 %copy-start = (bf16[2,1,128,1024]{3,2,1,0:T(8,128)(2,1)S(1)}, bf16[2,1,128,1024]{3,2,1,0:T(8,128)(2,1)}, u32[]{:S(2)}) copy-start(bf16[2,1,128,1024]{3,2,1,0:T(8,128)(2,1)} %param.13) | copy-start | bytes 1572868
  0.7 4.5 %copy-start.12 = (f32[12,128]{1,0:T(8,128)S(1)}, f32[12,128]{1,0:T(8,128)}, u32[]{:S(2)}) copy-start(f32[12,128]{1,0:T(8,128)} %param.23) | copy-start | bytes 18436
  119.2 19.6 %copy-start.1 = (bf16[16,2,208,128]{3,2,1,0:T(8,128)(2,1)}, bf16[16,2,208,128]{3,2,1,0:T(8,128)(2,1)S(1)}, u32[]{:S(2)}) copy-start(bf16[16,2,208,128]{3,2,1,0:T(8,128)(2,1)S(1)} %get-tuple-element.31.held_in) | copy-start | bytes 5111812
  119.2 19.6 %copy-start.2 = (f32[16,2,64,128]{3,2,1,0:T(8,128)}, f32[16,2,64,128]{3,2,1,0:T(8,128)S(1)}, u32[]{:S(2)}) copy-start(f32[16,2,64,128]{3,2,1,0:T(8,128)S(1)} %get-tuple-element.32.full) | copy-start | bytes 3145732
  119.2 19.6 %copy-start.3 = (f32[16,2,1,128]{3,2,1,0:T(1,128)}, f32[16,2,1,128]{3,2,1,0:T(1,128)S(1)}, u32[]{:S(2)}) copy-start(f32[16,2,1,128]{3,2,1,0:T(1,128)S(1)} %get-tuple-element.33.lse) | copy-start | bytes 49156
  138.8 6.7 %copy-start.18 = (bf16[256,4096]{1,0:T(8,128)(2,1)}, bf16[256,4096]{1,0:T(8,128)(2,1)S(1)}, u32[]{:S(2)}) copy-start(bf16[256,4096]{1,0:T(8,128)(2,1)S(1)} %get-tuple-element.108.right_g) | copy-start | bytes 6291460
  138.8 7.0 %copy-start.5 = (bf16[2,1,128,1024]{3,2,1,0:T(8,128)(2,1)S(1)}, bf16[2,1,128,1024]{3,2,1,0:T(8,128)(2,1)}, u32[]{:S(2)}) copy-start(bf16[2,1,128,1024]{3,2,1,0:T(8,128)(2,1)} %param.14) | copy-start | bytes 1572868
  146.7 11.9 %slice-start = ((s8[16777216]{0:T(1024)(128)(4,1)}), s8[4194304]{0:T(1024)(128)(4,1)S(1)}, s32[]{:S(2)}) async-start(s8[16777216]{0:T(1024)(128)(4,1)} %bitcast.137), calls=%async_computation | async-start | bytes 8388608
  148.0 10.6 %slice-start.1 = ((s8[16777216]{0:T(1024)(128)(4,1)}), s8[4194304]{0:T(1024)(128)(4,1)S(1)}, s32[]{:S(2)}) async-start(s8[16777216]{0:T(1024)(128)(4,1)} %bitcast.137), calls=%async_computation.1 | async-start | bytes 8388608
  148.0 10.6 %slice-start.2 = ((s8[16777216]{0:T(1024)(128)(4,1)}), s8[4194304]{0:T(1024)(128)(4,1)S(1)}, s32[]{:S(2)}) async-start(s8[16777216]{0:T(1024)(128)(4,1)} %bitcast.137), calls=%async_computation.2 | async-start | bytes 8388608
  148.0 10.6 %slice-start.3 = ((s8[16777216]{0:T(1024)(128)(4,1)}), s8[4194304]{0:T(1024)(128)(4,1)S(1)}, s32[]{:S(2)}) async-start(s8[16777216]{0:T(1024)(128)(4,1)} %bitcast.137), calls=%async_computation.3 | async-start | bytes 8388608
  164.7 0.8 copy-start.11
  175.4 151.2 %copy-start.13 = (f32[12,128]{1,0:T(8,128)S(1)}, f32[12,128]{1,0:T(8,128)}, u32[]{:S(2)}) copy-start(f32[12,128]{1,0:T(8,128)} %param.24) | copy-start | bytes 18436
  175.4 151.2 %copy-start.14 = (f32[12,128]{1,0:T(8,128)S(1)}, f32[12,128]{1,0:T(8,128)}, u32[]{:S(2)}) copy-start(f32[12,128]{1,0:T(8,128)} %param.25) | copy-start | bytes 18436
  326.1 4.3 %copy-start.4 = (f32[128,8192]{1,0:T(8,128)S(1)}, f32[128,8192]{1,0:T(8,128)}, u32[]{:S(2)}) copy-start(f32[128,8192]{1,0:T(8,128)} %param.20) | copy-start | bytes 12582916
  328.2 18.2 %slice-start.4 = ((s8[8388608]{0:T(1024)(128)(4,1)}), s8[4194304]{0:T(1024)(128)(4,1)S(1)}, s32[]{:S(2)}) async-start(s8[8388608]{0:T(1024)(128)(4,1)} %bitcast.142), calls=%async_computation.4 | async-start | bytes 8388608
  330.4 10.2 %copy-start.9 = (bf16[8,16,4096]{2,1,0:T(8,128)(2,1)S(1)}, bf16[8,16,4096]{2,1,0:T(8,128)(2,1)}, u32[]{:S(2)}) copy-start(bf16[8,16,4096]{2,1,0:T(8,128)(2,1)} %get-tuple-element.36) | copy-start | bytes 3145732
  330.4 10.5 %copy-start.7 = (f32[128,4096]{1,0:T(8,128)S(1)}, f32[128,4096]{1,0:T(8,128)}, u32[]{:S(2)}) copy-start(f32[128,4096]{1,0:T(8,128)} %param.18) | copy-start | bytes 6291460
  330.4 10.5 %copy-start.8 = (f32[128,4096]{1,0:T(8,128)S(1)}, f32[128,4096]{1,0:T(8,128)}, u32[]{:S(2)}) copy-start(f32[128,4096]{1,0:T(8,128)} %param.19) | copy-start | bytes 6291460
  330.4 16.0 %slice-start.5 = ((s8[8388608]{0:T(1024)(128)(4,1)}), s8[4194304]{0:T(1024)(128)(4,1)S(1)}, s32[]{:S(2)}) async-start(s8[8388608]{0:T(1024)(128)(4,1)} %bitcast.142), calls=%async_computation.5 | async-start | bytes 8388608
  340.6 1.6 copy-start.6
  342.2 4.2 %copy-start.10 = (f32[256,1024]{1,0:T(8,128)S(1)}, f32[256,1024]{1,0:T(8,128)}, u32[]{:S(2)}) copy-start(f32[256,1024]{1,0:T(8,128)} %get-tuple-element.107) | copy-start | bytes 3145732
  342.2 4.2 %copy-start.17 = (bf16[256,3072]{1,0:T(8,128)(2,1)S(1)}, bf16[256,3072]{1,0:T(8,128)(2,1)}, u32[]{:S(2)}) copy-start(bf16[256,3072]{1,0:T(8,128)(2,1)} %get-tuple-element.34) | copy-start | bytes 4718596

commit v3 on v2

--- a/solution.py
+++ b/solution.py
@@ -1,4 +1,3 @@
-from functools import partial
 import math
 
 import jax
@@ -39,8 +38,6 @@
 ALL = ("x", "yh", "yl", "z", "core")
 BLK = 256
 NBLK = PACK // BLK
-N_GROUPS = 3
-STEPS = (1, 3, 6, 9, 12)
 f32 = jnp.float32
 bf16 = jnp.bfloat16
 
@@ -71,9 +68,9 @@
 OFFSETS = (0, 1536, 2048, 4096)
 HALF_Z = 3072
 TASKS = {}
-for _n, _at in enumerate((1, 2, 4, 5, 7, 8, 10, 11, 13)):
+for _n, _at in enumerate((7, 8, 9, 10, 11, 12, 13, 14, 15)):
     TASKS.setdefault(_at, []).append((0, _n // 3, _n % 3))
-for _n, _at in enumerate((6, 7, 9, 10, 12, 13, 15)):
+for _n, _at in enumerate(()):
     TASKS.setdefault(_at, []).append((1, _n // 3, _n % 3))
 
 
@@ -174,9 +171,24 @@
         lse_out[2 * j + half, m] = lse[:, cols]
 
 
-X_COLS, Y_COLS, Z_COLS = slice(0, 512), slice(512, 1152), slice(1152, 2048)
-GROUP = 2048
+GROUP_COLS = (1536, 2048, 2048, 512)
+GROUP_AT = (0, 2048, 4096, 1536)
+SPLITS = ((512, 1024), (1024, 1536), (1024, 1536), (128, 256))
 N_COPY = 31
+GROUPS = (1, 2, 3)
+BEFORE = tuple((0, op) for op in ("z1", "x1", "z2", "y1", "z3", "x2", "x3", "y2", "z4", "x4", "x5"))
+BEFORE += tuple((g, op) for op in ("z1", "z2", "y1") for g in GROUPS)
+BEFORE += tuple((0, op) for op in ("y3", "z5", "sx", "sy", "sz", "end"))
+PUSHED = tuple((g, op) for op in ("z3", "x1", "x2", "x3") for g in GROUPS)
+STEPS = {
+    0: tuple((g, "z4") for g in GROUPS),
+    1: tuple((g, "y2") for g in GROUPS),
+    3: tuple((g, "x4") for g in GROUPS),
+    6: tuple((g, "x5") for g in GROUPS),
+    9: tuple((g, "y3") for g in GROUPS),
+    12: tuple((g, "z5") for g in GROUPS),
+}
+LAST = tuple((g, op) for op in ("sx", "sy", "sz", "end") for g in GROUPS)
 
 
 def ctx_device(t):
@@ -197,6 +209,11 @@
         zq, half = rows_at(z * 32, 32), rows_at(yl * 64, 64)
         cross = {"yh": 1 - yh, "yl": 1 - yl}
         count = [0]
+        x_end, y_end = SPLITS[g]
+        x_cols, y_cols, z_cols = slice(0, x_end), slice(x_end, y_end), slice(y_end, GROUP_COLS[g])
+
+        def given(rows, cols):
+            return shard.at[rows, GROUP_AT[g] + cols.start : GROUP_AT[g] + cols.stop]
 
         def make(src, dst, to):
             copy = send(src, dst, sems, base + count[0], to)
@@ -204,7 +221,7 @@
             return copy
 
         def own(rows, cols, to):
-            return make(shard.at[g, rows, cols], dest(core, x, yh, rows, cols), to)
+            return make(given(rows, cols), dest(core, x, yh, rows, cols), to)
 
         def pass_on(xs, yhs, rows, cols, to):
             view = dest(core, xs, yhs, rows, cols)
@@ -213,89 +230,67 @@
         x_to = {step: peer("x", step)[0] for step in (1, 2, 3)}
         y_to = {step: peer("y", step)[0] for step in (1, 3)}
         z_to = {step: peer("z", step)[0] for step in (1, 3)}
-        self.x1 = own(every, X_COLS, cross)
-        self.x2 = [own(every, X_COLS, x_to[s]) for s in (1, 3)]
-        self.z1 = own(zq, Z_COLS, cross)
-        self.z2 = [own(zq, Z_COLS, x_to[s]) for s in (1, 3, 2)]
-        self.y1 = [own(half, Y_COLS, x_to[s]) for s in (1, 3, 2)]
-        self.x3 = [pass_on(x, 1 - yh, every, X_COLS, x_to[s]) for s in (1, 3)]
-        self.z3 = [pass_on(x, 1 - yh, zq, Z_COLS, x_to[s]) for s in (1, 3, 2)]
-        self.y2 = [pass_on(every, yh, half, Y_COLS, y_to[s]) for s in (1, 3)]
-        self.z4 = [pass_on(every, every, zq, Z_COLS, z_to[s]) for s in (1, 3)]
-        before, after = lax.rem(x + 3, 4), lax.rem(x + 1, 4)
-        self.x4 = [
-            pass_on(before, yh, slice(0, 64), X_COLS, x_to[1]),
-            pass_on(after, yh, slice(64, 128), X_COLS, x_to[3]),
+        x_before, x_after = lax.rem(x + 3, 4), lax.rem(x + 1, 4)
+        y_before, y_after = lax.rem(y + 3, 4), lax.rem(y + 1, 4)
+        z_before, z_after = lax.rem(z + 3, 4), lax.rem(z + 1, 4)
+        self.copies = {
+            "x1": [own(every, x_cols, cross)],
+            "x2": [own(every, x_cols, x_to[s]) for s in (1, 3)],
+            "z1": [own(zq, z_cols, cross)],
+            "z2": [own(zq, z_cols, x_to[s]) for s in (1, 3, 2)],
+            "y1": [own(half, y_cols, x_to[s]) for s in (1, 3, 2)],
+            "x3": [pass_on(x, 1 - yh, every, x_cols, x_to[s]) for s in (1, 3)],
+            "z3": [pass_on(x, 1 - yh, zq, z_cols, x_to[s]) for s in (1, 3, 2)],
+            "y2": [pass_on(every, yh, half, y_cols, y_to[s]) for s in (1, 3)],
+            "z4": [pass_on(every, every, zq, z_cols, z_to[s]) for s in (1, 3)],
+            "x4": [
+                pass_on(x_before, yh, slice(0, 64), x_cols, x_to[1]),
+                pass_on(x_after, yh, slice(64, 128), x_cols, x_to[3]),
+            ],
+            "x5": [
+                pass_on(x_before, 1 - yh, slice(0, 64), x_cols, x_to[1]),
+                pass_on(x_after, 1 - yh, slice(64, 128), x_cols, x_to[3]),
+            ],
+            "y3": [
+                pass_on(every, y_before // 2, rows_at(lax.rem(y_before, 2) * 64, 32), y_cols, y_to[1]),
+                pass_on(every, y_after // 2, rows_at(lax.rem(y_after, 2) * 64 + 32, 32), y_cols, y_to[3]),
+            ],
+            "z5": [
+                pass_on(every, every, rows_at(z_before * 32, 16), z_cols, z_to[1]),
+                pass_on(every, every, rows_at(z_after * 32 + 16, 16), z_cols, z_to[3]),
+            ],
+        }
+        for name, cols in (("sx", x_cols), ("sy", y_cols), ("sz", z_cols)):
+            self.copies[name] = [pass_on(every, every, every, cols, {"core": 1 - core})]
+        self.places = [
+            pltpu.make_async_copy(given(rows, cols), dest(core, x, yh, rows, cols), local_sem.at[3 * g + n])
+            for n, (rows, cols) in enumerate(((every, x_cols), (half, y_cols), (zq, z_cols)))
         ]
-        self.x5 = [
-            pass_on(before, 1 - yh, slice(0, 64), X_COLS, x_to[1]),
-            pass_on(after, 1 - yh, slice(64, 128), X_COLS, x_to[3]),
-        ]
-        before, after = lax.rem(y + 3, 4), lax.rem(y + 1, 4)
-        self.y3 = [
-            pass_on(every, before // 2, rows_at(lax.rem(before, 2) * 64, 32), Y_COLS, y_to[1]),
-            pass_on(every, after // 2, rows_at(lax.rem(after, 2) * 64 + 32, 32), Y_COLS, y_to[3]),
-        ]
-        before, after = lax.rem(z + 3, 4), lax.rem(z + 1, 4)
-        self.z5 = [
-            pass_on(every, every, rows_at(before * 32, 16), Z_COLS, z_to[1]),
-            pass_on(every, every, rows_at(after * 32 + 16, 16), Z_COLS, z_to[3]),
-        ]
-        self.swap = [
-            pass_on(every, every, every, cols, {"core": 1 - core}) for cols in (X_COLS, Y_COLS, Z_COLS)
-        ]
-        self.place = [
-            pltpu.make_async_copy(shard.at[g, rows, cols], dest(core, x, yh, rows, cols), local_sem.at[3 * g + n])
-            for n, (rows, cols) in enumerate(((every, X_COLS), (half, Y_COLS), (zq, Z_COLS)))
-        ]
-
-    def start(self, copies):
-        for copy in copies:
+
+    needs = {
+        "x3": ("x1",), "z3": ("z1",), "y2": ("y1",), "z4": ("z2", "z3"), "x4": ("x2",), "x5": ("x3",), "y3": ("y2",),
+        "z5": ("z4",), "sx": ("x4", "x5"), "sy": ("y3",), "sz": ("z5",),
+    }
+
+    def step(self, name):
+        if name == "end":
+            for copy in (*self.copies["sx"], *self.copies["sy"], *self.copies["sz"]):
+                copy.wait_recv()
+            for copies in self.copies.values():
+                for copy in copies:
+                    copy.wait_send()
+            return
+        for need in self.needs.get(name, ()):
+            for copy in self.copies[need]:
+                copy.wait_recv()
+        if name == "z1":
+            for copy in self.places:
+                copy.start()
+        if name == "z3":
+            for copy in self.places:
+                copy.wait()
+        for copy in self.copies[name]:
             copy.start()
-
-    def arrive(self, copies):
-        for copy in copies:
-            copy.wait_recv()
-
-    def stage(self, n):
-        if n == 0:
-            self.start([self.z1, self.x1, *self.z2, *self.y1, *self.x2, *self.place])
-        elif n == 1:
-            self.arrive([self.z1])
-            self.start(self.z3)
-            self.arrive([self.x1])
-            self.start(self.x3)
-            for copy in self.place:
-                copy.wait()
-        elif n == 2:
-            self.arrive(self.y1)
-            self.start(self.y2)
-            self.arrive([*self.z2, *self.z3])
-            self.start(self.z4)
-        elif n == 3:
-            self.arrive(self.x2)
-            self.start(self.x4)
-            self.arrive(self.y2)
-            self.start(self.y3)
-        elif n == 4:
-            self.arrive(self.x3)
-            self.start(self.x5)
-            self.arrive(self.z4)
-            self.start(self.z5)
-        elif n == 5:
-            self.arrive([*self.x4, *self.x5])
-            self.start(self.swap[:1])
-            self.arrive(self.y3)
-            self.start(self.swap[1:2])
-            self.arrive(self.z5)
-            self.start(self.swap[2:])
-        else:
-            self.arrive(self.swap)
-            for copy in (
-                self.x1, self.z1, *self.x2, *self.z2, *self.y1, *self.x3, *self.z3, *self.y2, *self.z4,
-                *self.x4, *self.x5, *self.y3, *self.z5, *self.swap,
-            ):
-                copy.wait_send()
 
 
 def greet_all():
@@ -322,13 +317,14 @@
         def view(c, xs, yhs, rows, cols):
             if g == 0:
                 return wa.at[c, xs, yhs, rows, cols]
-            start = (g - 1) * FF + c * GROUP + cols.start
-            return out_ffn.at[xs, yhs, rows, pl.ds(pl.multiple_of(start, 128), cols.stop - cols.start)]
+            start = (0, 0, FF, 3 * D)[g] + c * GROUP_COLS[g] + cols.start
+            target = out_attn if g == 3 else out_ffn
+            return target.at[xs, yhs, rows, pl.ds(pl.multiple_of(start, 128), cols.stop - cols.start)]
 
         return view
 
     gathers = [
-        Gather(g, shard, dest(g), (ag_send, ag_recv), g * N_COPY, local_sem) for g in range(N_GROUPS)
+        Gather(g, shard, dest(g), (ag_send, ag_recv), g * N_COPY, local_sem) for g in range(4)
     ]
     vec_sems = (vec_send, vec_recv)
     vec_cross = send(vec_shard, vecs.at[x, yh], vec_sems, 0, {"yh": 1 - yh, "yl": 1 - yl})
@@ -339,15 +335,22 @@
     greet_all()
     for copy in (vec_cross, *vec_x):
         copy.start()
-    gathers[0].stage(0)
+    done = set()
+
+    def stages(todo):
+        for g, n in todo:
+            if (g, n) not in done:
+                done.add((g, n))
+                gathers[g].step(n)
+
+    stages(BEFORE[:4])
     vecs[x, yh] = vec_shard[...]
     for s in range(N_CTX):
         ready[s, :, 3 * HEAD :, :] = seg_ref[...]
     vec_cross.wait_recv()
     for copy in vec_x2:
         copy.start()
-    for n in range(1, 7):
-        gathers[0].stage(n)
+    stages(BEFORE)
     vec_cross.wait_send()
     for copy in (*vec_x, *vec_x2):
         copy.wait()
@@ -383,12 +386,8 @@
             returns[m].append(
                 send(out_t.at[t, m], mixed.at[place, m], (o_send, o_recv), m * N_CTX + d, ctx_device(t))
             )
-    for gather in gathers[1:]:
-        gather.stage(0)
-    outs = []
-    for c in range(2):
-        outs.append((wa.at[c, :, :, :, 0:1536], out_attn.at[:, :, :, c * 1536 : (c + 1) * 1536]))
-        outs.append((wa.at[c, :, :, :, 1536:2048], out_attn.at[:, :, :, 3072 + c * 512 : 3584 + c * 512]))
+    stages(PUSHED)
+    outs = [(wa.at[c], out_attn.at[:, :, :, c * 1536 : (c + 1) * 1536]) for c in range(2)]
     outs = [pltpu.make_async_copy(src, dst, out_sem.at[n]) for n, (src, dst) in enumerate(outs)]
     for copy in outs:
         copy.start()
@@ -398,13 +397,12 @@
         load_side(held, m, keys, None, None, values_t, seg_col)
 
         def query_block(j, _, m=m):
-            for n, at in enumerate(STEPS):
+            for at, todo in STEPS.items():
                 if at // NBLK == m:
 
                     @pl.when(j == at % NBLK)
-                    def _(n=n):
-                        for gather in gathers[1:]:
-                            gather.stage(n + 1)
+                    def _(todo=todo):
+                        stages(todo)
 
             query_forward(held, m, j, out_t, out_full, out_lse, keys, values_t, seg_col, scores)
             return 0
@@ -416,9 +414,7 @@
     last = [pltpu.make_async_copy(held, out_held, out_sem.at[4])]
     last[0].start()
     out_vec[...] = vecs[...]
-    for n in range(len(STEPS) + 1, 7):
-        for gather in gathers[1:]:
-            gather.stage(n)
+    stages(LAST)
     for m in range(MB):
         for copy in swaps[m]:
             copy.wait_send()
@@ -435,14 +431,13 @@
     hbm = pl.BlockSpec(memory_space=pl.ANY)
     sem = lambda n: pltpu.SemaphoreType.DMA((n,))
     blocks = lambda rows, dt: (N_CTX, MB, rows, TOK)
-    ffn_cols = 2 * FF if N_GROUPS > 1 else 128
     return pl.pallas_call(
         front_kernel,
         in_specs=[hbm, vmem, vmem, vmem],
         out_specs=[hbm, hbm, vmem, hbm, hbm, vmem, vmem],
         out_shape=[
             jax.ShapeDtypeStruct((4, 2, TOK, 4 * D), bf16),
-            jax.ShapeDtypeStruct((4, 2, TOK, ffn_cols), bf16),
+            jax.ShapeDtypeStruct((4, 2, TOK, 2 * FF), bf16),
             jax.ShapeDtypeStruct((4, 2, 16, TOK), bf16),
             jax.ShapeDtypeStruct((N_CTX, MB, SENT, TOK), bf16),
             jax.ShapeDtypeStruct((N_CTX, MB, HEAD, TOK), bf16),
@@ -450,7 +445,7 @@
             jax.ShapeDtypeStruct((N_CTX, MB, 1, TOK), f32),
         ],
         scratch_shapes=[
-            pltpu.VMEM((2, 4, 2, TOK, GROUP), bf16),
+            pltpu.VMEM((2, 4, 2, TOK, 1536), bf16),
             pltpu.VMEM((4, 2, 16, TOK), bf16),
             pltpu.VMEM((N_CTX, MB, SENT, TOK), bf16),
             pltpu.VMEM((N_CTX, MB, SENT, TOK), bf16),
@@ -460,8 +455,8 @@
             pltpu.VMEM((HEAD, PACK), bf16),
             pltpu.VMEM((PACK, TOK), f32),
             pltpu.VMEM((PACK, BLK), f32),
-            sem(N_COPY * N_GROUPS), sem(N_COPY * N_GROUPS), sem(7), sem(7), sem(32), sem(32), sem(32), sem(32),
-            sem(3 * N_GROUPS), sem(6),
+            sem(4 * N_COPY), sem(4 * N_COPY), sem(7), sem(7), sem(32), sem(32), sem(32), sem(32),
+            sem(12), sem(6),
         ],
         compiler_params=pltpu.CompilerParams(
             collective_id=2, has_side_effects=True, vmem_limit_bytes=48 * 2**20
@@ -881,8 +876,152 @@
     )
 
 
-def column_sum(values):
-    return jnp.sum(values.astype(f32), axis=0)
+N_CHUNK = 8
+CHUNK = FF // N_CHUNK
+ERF_TOP = (
+    -2.72614225801306e-10, 2.77068142495902e-08, -2.10102402082508e-06, -5.69250639462346e-05,
+    -7.34990630326855e-04, -2.95459980854025e-03, -1.60960333262415e-02,
+)
+ERF_LOW = (
+    -1.45660718464996e-05, -2.13374055278905e-04, -1.68282697438203e-03, -7.37332916720468e-03,
+    -1.42647390514189e-02,
+)
+
+
+def erf(value):
+    value = jnp.clip(value, -4.0, 4.0)
+    square = value * value
+    top, low = jnp.full_like(square, ERF_TOP[0]), jnp.full_like(square, ERF_LOW[0])
+    for c in ERF_TOP[1:]:
+        top = top * square + c
+    for c in ERF_LOW[1:]:
+        low = low * square + c
+    return value * top / low
+
+
+def dense_kernel(
+    mixed_ref, x_ref, cot_ref, keep_ref, small_ref, w_attn, w_ffn,
+    out_ref, one_ref, x_t, o_t, h_t, f_t, a_low_ref, du_ref, g_ref, vec_ref, ready_ref,
+    w_out, w_one, w_two, mixed, normal_one_ref, slope, total, sem,
+):
+    fetch_out = pltpu.make_async_copy(w_attn.at[:, 3 * D :], w_out, sem.at[0])
+    fetch_out.start()
+    fetch_one, fetch_two = [], []
+    for n in range(N_CHUNK):
+        at = n * CHUNK
+        fetch_one.append(pltpu.make_async_copy(w_ffn.at[:, at : at + CHUNK], w_one.at[n], sem.at[1 + n]))
+        fetch_two.append(
+            pltpu.make_async_copy(w_ffn.at[:, FF + at : FF + at + CHUNK], w_two.at[n], sem.at[1 + N_CHUNK + n])
+        )
+        fetch_one[n].start()
+        fetch_two[n].start()
+
+    def row(i):
+        return small_ref[i : i + 1, :]
+
+    def put(i, value):
+        for f in range(N_FSDP):
+            vec_ref[f, i : i + 1, :] = value[:, f * TOK : (f + 1) * TOK]
+
+    def sums(value):
+        return jnp.sum(value, axis=0, keepdims=True)
+
+    vec_ref[...] = jnp.zeros_like(vec_ref)
+    for m in range(MB):
+        tok = slice(m * TOK, (m + 1) * TOK)
+        for i in range(HEADS // 2):
+            both = jnp.concatenate([mixed_ref[2 * i, m], mixed_ref[2 * i + 1, m]], axis=0)
+            o_t[i * 128 : (i + 1) * 128, tok] = both
+            mixed[tok, i * 128 : (i + 1) * 128] = both.T
+    x_t[...] = x_ref[...].T
+    fetch_out.wait()
+    normed_one, normal_one, inverse_one = layer_stats(
+        x_ref[...].astype(f32) + dot(mixed[...], w_out[...]) + row(2), row(4), row(5)
+    )
+    normal_one_ref[...] = normal_one
+    normed_low = normed_one.astype(bf16)
+    h_t[...] = normed_low.T
+    total[...] = normed_one + row(3)
+    for n in range(N_CHUNK):
+        cols = slice(n * CHUNK, (n + 1) * CHUNK)
+        fetch_one[n].wait()
+        bias = small_ref[8 + n // 2 : 9 + n // 2, (n % 2) * CHUNK : (n % 2 + 1) * CHUNK]
+        u = dot(normed_low, w_one[n]) + bias
+        share = 0.5 + 0.5 * erf(u * math.sqrt(0.5))
+        g = (u * share).astype(bf16)
+        g_ref[:, cols] = g
+        slope[:, cols] = share + u * (jnp.exp(-0.5 * u * u) * (1.0 / math.sqrt(2.0 * math.pi)))
+        fetch_two[n].wait()
+        total[...] += dot_nt(g, w_two[n])
+    output, normal_two, inverse_two = layer_stats(total[...], row(6), row(7))
+    keep = keep_ref[...]
+    out_ref[...] = (output * keep).astype(bf16)
+    grad_out = cot_ref[...].astype(f32) * keep
+    put(6, sums(grad_out * normal_two))
+    put(7, sums(grad_out))
+    grad_two = layer_back(grad_out, normal_two, inverse_two, row(6))
+    f_low = grad_two.astype(bf16)
+    f_t[...] = f_low.T
+    put(3, sums(f_low.astype(f32)))
+    total[...] = grad_two
+    for n in range(N_CHUNK):
+        cols = slice(n * CHUNK, (n + 1) * CHUNK)
+        du = (dot(f_low, w_two[n]) * slope[:, cols]).astype(bf16)
+        du_ref[:, cols] = du
+        part = sums(du.astype(f32))
+        for i in range(CHUNK // TOK):
+            f = (n % 2) * (CHUNK // TOK) + i
+            vec_ref[f, 8 + n // 2 : 9 + n // 2, :] = part[:, i * TOK : (i + 1) * TOK]
+        total[...] += dot_nt(du, w_one[n])
+    grad_normed = total[...]
+    normal_one = normal_one_ref[...]
+    put(4, sums(grad_normed * normal_one))
+    put(5, sums(grad_normed))
+    grad_one = layer_back(grad_normed, normal_one, inverse_one, row(4))
+    one_ref[...] = grad_one
+    a_low = grad_one.astype(bf16)
+    a_low_ref[...] = a_low
+    put(2, sums(a_low.astype(f32)))
+    grad_mixed = dot_nt(a_low, w_out[...]).T.astype(bf16)
+    for h in range(HEADS):
+        for m in range(MB):
+            ready_ref[h, m] = grad_mixed[h * HEAD : (h + 1) * HEAD, m * TOK : (m + 1) * TOK]
+
+
+def dense(mixed_t, x, cot, keep, small, w_attn, w_ffn):
+    vmem = pl.BlockSpec(memory_space=pltpu.VMEM)
+    hbm = pl.BlockSpec(memory_space=pl.ANY)
+    turned = jax.ShapeDtypeStruct((D, ROWS), bf16)
+    return pl.pallas_call(
+        dense_kernel,
+        in_specs=[vmem] * 5 + [hbm, hbm],
+        out_specs=[vmem] * 11,
+        out_shape=[
+            jax.ShapeDtypeStruct((ROWS, D), bf16),
+            jax.ShapeDtypeStruct((ROWS, D), f32),
+            turned, turned, turned, turned,
+            jax.ShapeDtypeStruct((ROWS, D), bf16),
+            jax.ShapeDtypeStruct((ROWS, FF), bf16),
+            jax.ShapeDtypeStruct((ROWS, FF), bf16),
+            jax.ShapeDtypeStruct((N_FSDP, 16, TOK), f32),
+            jax.ShapeDtypeStruct((HEADS, MB, HEAD, TOK), bf16),
+        ],
+        scratch_shapes=[
+            pltpu.VMEM((D, D), bf16),
+            pltpu.VMEM((N_CHUNK, D, CHUNK), bf16),
+            pltpu.VMEM((N_CHUNK, D, CHUNK), bf16),
+            pltpu.VMEM((ROWS, D), bf16),
+            pltpu.VMEM((ROWS, D), f32),
+            pltpu.VMEM((ROWS, FF), f32),
+            pltpu.VMEM((ROWS, D), f32),
+            pltpu.SemaphoreType.DMA((1 + 2 * N_CHUNK,)),
+        ],
+        compiler_params=pltpu.CompilerParams(vmem_limit_bytes=56 * 2**20),
+        cost_estimate=pl.CostEstimate(
+            flops=2 * ROWS * D * (2 * D + 4 * FF), bytes_accessed=32 * 2**20, transcendentals=ROWS * FF
+        ),
+        name="dense",
+    )(mixed_t, x, cot, keep, small, w_attn, w_ffn)
 
 
 def adamw(weight, grad_value, first, second, rate, decay):
@@ -894,37 +1033,21 @@
     return (weight_new, first_new, second_new)
 
 
-def to_heads(rows, parts):
-    t = rows.T.reshape(parts, HEADS, HEAD, MB, TOK)
-    return jnp.transpose(t, (1, 3, 0, 2, 4)).reshape(HEADS, MB, parts * HEAD, TOK)
-
-
-def from_heads(blocks, parts):
-    t = blocks.reshape(HEADS, MB, parts, HEAD, TOK)
-    return jnp.transpose(t, (1, 4, 2, 0, 3)).reshape(ROWS, parts * D)
-
-
 def shards(
     tokens, cotangent, dest, lengths, attn_weight, attn_first, attn_second,
     ffn_weight, ffn_first, ffn_second, vectors, vec_first, vec_second,
 ):
-    place, core = lax.axis_index(CTX), lax.axis_index("core")
+    core = lax.axis_index("core")
 
     def half(weight, base, width):
         return lax.dynamic_slice_in_dim(weight, base + core * width, width, 1).astype(bf16)
 
-    attn_half = jnp.concatenate([half(attn_weight, 0, 1536), half(attn_weight, 3 * D, 512)], axis=1)
-    own_rows = D // N_FSDP // N_CTX
-    if N_GROUPS == 1:
-        shard = attn_half[None]
-        w_ffn = lax.all_gather(
-            lax.dynamic_slice_in_dim(ffn_weight, place * own_rows, own_rows).astype(bf16), ALL, axis=0, tiled=True
-        )
-    else:
-        shard = jnp.stack([attn_half, half(ffn_weight, 0, GROUP), half(ffn_weight, FF, GROUP)])
-
+    shard = jnp.concatenate(
+        [half(attn_weight, 0, 1536), half(attn_weight, 3 * D, 512), half(ffn_weight, 0, 2048), half(ffn_weight, FF, 2048)],
+        axis=1,
+    )
     x = tokens.reshape(ROWS, D)
-    cot = cotangent.reshape(ROWS, D).astype(f32)
+    cot = cotangent.reshape(ROWS, D)
     ends = jnp.cumsum(lengths[:, 0], axis=1)
     seg = jnp.sum((dest[:, 0, :, None] >= ends[:, None, :]).astype(jnp.int32), axis=2)
     keep = (seg.reshape(ROWS, 1) < 8).astype(f32)
@@ -933,61 +1056,21 @@
     vec_shard = jnp.pad(vectors.astype(bf16), ((0, 4), (0, 0)))
     w_attn, ffn_out, vecs, held, mixed_t, mixed_full, lse = front(shard, vec_shard, x, seg_rows)
     w_attn = w_attn.reshape(D, 4 * D)
-    if N_GROUPS > 1:
-        w_ffn = ffn_out.reshape(D, 2 * FF)
-    small = jnp.transpose(vecs.reshape(N_FSDP, 16, TOK), (1, 0, 2)).reshape(16, D)[:12].astype(f32)
-    w_qkv, w_out = w_attn[:, : 3 * D], w_attn[:, 3 * D :]
-    w_one, w_two = w_ffn[:, :FF], w_ffn[:, FF:]
-    mixed = from_heads(mixed_t, 1)
-
-    branch = dot(mixed, w_out) + small[2]
-    normed_one, normal_one, inverse_one = layer_stats(x.astype(f32) + branch, small[4], small[5])
-    normed_low = normed_one.astype(bf16)
-    hidden_pre = dot(normed_low, w_one) + small[8:].reshape(FF)
-    activ, gelu_back = jax.vjp(partial(jax.nn.gelu, approximate=False), hidden_pre)
-    activ_low = activ.astype(bf16)
-    ffn_out = dot_nt(activ_low, w_two) + small[3]
-    output, normal_two, inverse_two = layer_stats(normed_one + ffn_out, small[6], small[7])
-    output = output * keep
-    grad_out = cot * keep
-    grad_two = layer_back(grad_out, normal_two, inverse_two, small[6])
-    ffn_grad_low = grad_two.astype(bf16)
-    grad_hidden = gelu_back(dot(ffn_grad_low, w_two))[0].astype(bf16)
-    grad_normed = dot_nt(grad_hidden, w_one) + grad_two
-    grad_one = layer_back(grad_normed, normal_one, inverse_one, small[4])
-    branch_grad_low = grad_one.astype(bf16)
-    grad_mixed = dot_nt(branch_grad_low, w_out).astype(bf16)
-
-    step_vec = jnp.concatenate(
-        [
-            jnp.stack(
-                [
-                    jnp.zeros((D,), f32),
-                    jnp.zeros((D,), f32),
-                    column_sum(branch_grad_low),
-                    column_sum(ffn_grad_low),
-                    jnp.sum(grad_normed * normal_one, axis=0),
-                    jnp.sum(grad_normed, axis=0),
-                    jnp.sum(grad_out * normal_two, axis=0),
-                    jnp.sum(grad_out, axis=0),
-                ]
-            ),
-            column_sum(grad_hidden).reshape(4, D),
-        ],
-        axis=0,
-    )
-    vec_rows = jnp.transpose(step_vec.reshape(12, N_FSDP, TOK), (1, 0, 2))
-    vec_rows = jnp.pad(vec_rows, ((0, 0), (0, 4), (0, 0)))
+    w_ffn = ffn_out.reshape(D, 2 * FF)
+    small = jnp.transpose(vecs.reshape(N_FSDP, 16, TOK), (1, 0, 2)).reshape(16, D).astype(f32)
+    output, grad_one, x_t, o_t, h_t, f_t, a_low, du, g, vec_rows, grad_ready = dense(
+        mixed_t, x, cot, keep, small, w_attn, w_ffn
+    )
     total_attn, total_ffn, total_vec, square_sum, grad_qkv = back(
-        (x.T, mixed.T, normed_low.T, ffn_grad_low.T),
-        (branch_grad_low, grad_hidden, activ_low),
+        (x_t, o_t, h_t, f_t),
+        (a_low, du, g),
         vec_rows,
-        to_heads(grad_mixed, 1),
+        grad_ready,
         held,
         mixed_full,
         lse,
     )
-    grad_tokens = grad_one + dot_nt(grad_qkv, w_qkv)
+    grad_tokens = grad_one + dot_nt(grad_qkv, w_attn[:, : 3 * D])
     total_attn, total_ffn, total_vec = total_attn.astype(f32), total_ffn.astype(f32), total_vec.astype(f32)
     grad_norm = jnp.sqrt(square_sum)
     factor = jnp.minimum(1.0, CLIP_NORM / (grad_norm + 1e-06))
@@ -1002,7 +1085,7 @@
         vectors, total_vec * factor, vec_first, vec_second, RATE_VECTOR, 0.0
     )
     return (
-        output.astype(bf16).reshape(tokens.shape),
+        output.reshape(tokens.shape),
         grad_tokens.astype(bf16).reshape(tokens.shape),
         grad_norm,
         attn_new, attn_first_new, attn_second_new,

time: 357 us -> 305 us (0.85)
  matrix products: 45.8 us -> 5.97 us
  other arithmetic: 27.8 us -> 18 us
  Pallas kernels: 262 us -> 257 us
    dot_general x3 -> x0, matrix products: 29.2 us -> none  [dot(): return jnp.dot(a, b, preferred_element_type=f32)]
    pallas_call x0 -> x1, Pallas kernels: none -> 24.7 us  [dense(): pl.pallas_call(dense_kernel, in_specs=[vmem] * 5 + [hbm, hbm], out_specs=...]
    pallas_call x1, Pallas kernels: 114 us -> 95.8 us  [front(): pl.pallas_call(front_kernel, in_specs=[hbm, vmem, vmem, vmem], out_specs=...]
    pallas_call x1, Pallas kernels: 148 us -> 136 us  [back(): pl.pallas_call(back_kernel, in_specs=[vmem] * 4 + [hbm] * 3 + [vmem, vmem...]
    dot_general x4 -> x1, matrix products: 16.6 us -> 5.97 us  [dot_nt(): return lax.dot_general(a, b, CONTRACT_COLS, preferred_element_type=f32)]
    unnamed x51 -> x35, local copies, waits for them, and re-layouts: 3.11 us -> 10.3 us
    reduce_sum x7 -> x0, other arithmetic: 4.64 us -> none  [the longest x2 2.66 us: column_sum(): return jnp.sum(values.astype(f32), axis=0)]
    convert_element_type x1, other arithmetic: 10.2 us -> 6.57 us  [shards(): ffn_new.astype(bf16)]
where the time goes in v3:
time: 305 us; the launch traced here: 299 us
  Pallas kernels  257 us (84%)
  other arithmetic  18 us (6%)
  local copies, waits for them, and re-layouts  15 us (5%)
  matrix products  5.97 us (2%)
  between operations  3.14 us (1%)
    pallas_call x1, Pallas kernels, back(): pl.pallas_call(back_kernel, in_specs=[vmem] * 4 + [hbm] * 3 + [vmem, vmem...  136 us
    pallas_call x1, Pallas kernels, front(): pl.pallas_call(front_kernel, in_specs=[hbm, vmem, vmem, vmem], out_specs=...  95.8 us
    pallas_call x1, Pallas kernels, dense(): pl.pallas_call(dense_kernel, in_specs=[vmem] * 5 + [hbm, hbm], out_specs=...  24.7 us
    unnamed x35, local copies, waits for them, and re-layouts  10.3 us
    convert_element_type x1, other arithmetic, shards(): ffn_new.astype(bf16)  6.57 us

profile of v3, /device:TPU:1, one launch (start us, length us, event | category | flops | bytes accessed | tf_op | source)
XLA Modules:
  0.0 299.0 jit_solution(16122256451120298147)
XLA Ops:
  0.7 0.9 reduce_window_sum.14
  1.5 0.8 convert_reduce_fusion
  2.3 0.7 convert_element_type.66
  3.0 0.8 copy.36.keep_ref
  3.8 1.0 dynamic-slice_convert_fusion.3
  4.8 1.2 dynamic-slice_convert_fusion.2
  5.9 1.7 dynamic-slice_convert_fusion.1
  7.6 0.0 copy-start
  7.7 0.1 pad_maximum_fusion.shard
  7.8 0.9 copy-done
  8.7 95.8 %front.1 = (bf16[4,2,128,4096]{3,2,1,0:T(8,128)(2,1)}, bf16[4,2,128,8192]{3,2,1,0:T(8,128)(2,1)}, bf16[4,2,16,128]{3,2,1,0:T(8,128)(2,1)S(1)}, bf16[16,2,208,128...) custom-call(bf16[128,6144]{1,0:T(8,128)(2,1)S(1)} %pad_maximum_fusio, ...), custom_call_target="tpu_custom_call" | custom-call | flops 3758096384 | bytes 33554432 | tf_op jit(solution)/shard_map/front/pallas_call | solution.py:434
  104.4 0.0 copy-start.1
  104.5 1.2 copy-done.1
  105.6 0.0 copy-start.2
  105.6 0.8 copy-done.2
  106.4 0.0 copy-start.3
  106.4 1.0 copy-done.3
  107.4 0.0 copy-start.4
  107.4 0.6 copy-done.4
  108.0 0.6 copy.41
  108.6 24.7 %dense.1 = (bf16[256,1024]{1,0:T(8,128)(2,1)}, f32[256,1024]{1,0:T(8,128)}, bf16[1024,256]{1,0:T(8,128)(2,1)}, bf16[1024,256]{1,0:T(8,128)(2,1)}, bf16[1024,256]...) custom-call(bf16[16,2,64,128]{3,2,1,0:T(8,128)(2,1)} %copy-done.2, ...), custom_call_target="tpu_custom_call" | custom-call | flops 9663676416 | bytes 33554432 | tf_op jit(solution)/shard_map/dense/pallas_call | solution.py:995
  133.3 0.0 copy-start.16
  133.3 136.5 %back.1 = (bf16[8,16,4096]{2,1,0:T(8,128)(2,1)}, bf16[8,16,8192]{2,1,0:T(8,128)(2,1)}, bf16[8,16,128]{2,1,0:T(8,128)(2,1)}, f32[8,128]{1,0:T(8,128)}, bf16[256,3072]{1,0:T(8,128)(2,1)}) custom-call(bf16[1024,256]{1,0:T(8,128)(2,1)} %get-tuple-element.44.left_x, bf16[1024,256]{1,0:T(8,128)(2,1)} %get-tuple-element.45.left_o, ...), custom_call_target="tpu_custom_call" | custom-call | flops 11811160064 | bytes 16777216 | tf_op jit(solution)/shard_map/back/pallas_call | solution.py:839
  269.8 1.3 reduce_sum.19
  271.8 0.0 copy-done.16
  271.8 0.0 copy-start.13
  271.8 0.0 copy-start.14
  271.9 0.0 copy-start.15
  271.9 0.0 copy-start.12
  271.9 6.0 %fusion.9 = bf16[256,1024]{1,0:T(8,128)(2,1)} fusion(f32[256,1024]{1,0:T(8,128)S(1)} %copy-done.16, bf16[256,3072]{1,0:T(8,128)(2,1)} %get-tuple-element.56, bf16[1024,4096]{1,0:T(8,128)(2,1)} %bitcast.55), kind=kOutput, calls=%fused_computation.16 | convolution fusion | flops 1611137024 | bytes 9437184 | tf_op jit(solution)/shard_map/dot_general | solution.py:50
  277.8 0.0 copy-start.11
  277.8 0.8 slice_convert_fusion
  278.7 0.0 copy-done.13
  278.7 0.0 copy-done.14
  278.7 0.0 copy-done.15
  278.7 1.3 multiply_subtract_fusion.2
  280.0 0.5 fusion.14
  280.5 0.0 copy-done.12
  280.5 0.2 convert_multiply_fusion.1
  280.7 0.0 copy-done.11
  280.7 0.0 copy-start.8
  280.7 0.0 copy-start.9
  280.7 0.0 copy-start.10
  280.7 0.4 convert_multiply_fusion
  281.2 1.1 copy-done.8
  282.3 0.6 copy-done.9
  282.9 0.6 copy-done.10
  283.6 0.0 copy-start.5
  283.6 0.0 copy-start.6
  283.6 0.0 copy-start.7
  283.6 4.4 %fusion.18 = (bf16[128,4096]{1,0:T(8,128)(2,1)}, f32[128,4096]{1,0:T(8,128)}, f32[128,4096]{1,0:T(8,128)}, f32[128,4096]{1,0:T(8,128)}) fusion(f32[128,4096]{1,0:T(8,128)S(1)} %copy-done.8, f32[8,16,4096]{2,1,0:T(8,128)S(1)} %convert_multiply_fusion.1, f32[128,4096]{1,0:T(8,128)S(1)} %copy-done.9, f32[128,4096]{1,0:T(8,128)S(1)} %copy-done.10), kind=kLoop, calls=%fused_computation.34 | loop fusion | flops 8388608 | bytes 15728640 | tf_op jit(solution)/shard_map/convert_element_type | solution.py:1094
  288.0 0.0 copy-done.5
  288.0 1.7 copy-done.6
  289.7 1.2 copy-done.7
  290.9 6.6 %fusion.15 = (bf16[128,8192]{1,0:T(8,128)(2,1)}, f32[128,8192]{1,0:T(8,128)}, f32[128,8192]{1,0:T(8,128)}, f32[128,8192]{1,0:T(8,128)}) fusion(f32[128,8192]{1,0:T(8,128)S(1)} %copy-done.5, f32[8,16,8192]{2,1,0:T(8,128)S(1)} %convert_multiply_fusion, f32[128,8192]{1,0:T(8,128)S(1)} %copy-done.6, f32[128,8192]{1,0:T(8,128)S(1)} %copy-done.7), kind=kLoop, calls=%fused_computation.33 | loop fusion | flops 16777216 | bytes 31457280 | tf_op jit(solution)/shard_map/convert_element_type | solution.py:1095
  (6 shorter events, 0.1 us)
Async XLA Ops:
  7.6 1.0 copy-start
  104.4 1.2 copy-start.1
  105.6 0.8 copy-start.2
  106.4 1.0 copy-start.3
  107.4 0.6 copy-start.4
  133.3 138.5 %copy-start.16 = (f32[256,1024]{1,0:T(8,128)S(1)}, f32[256,1024]{1,0:T(8,128)}, u32[]{:S(2)}) copy-start(f32[256,1024]{1,0:T(8,128)} %get-tuple-element.43) | copy-start | bytes 3145732
  271.8 6.8 %copy-start.13 = (f32[12,128]{1,0:T(8,128)S(1)}, f32[12,128]{1,0:T(8,128)}, u32[]{:S(2)}) copy-start(f32[12,128]{1,0:T(8,128)} %param.23) | copy-start | bytes 18436
  271.8 6.8 %copy-start.14 = (f32[12,128]{1,0:T(8,128)S(1)}, f32[12,128]{1,0:T(8,128)}, u32[]{:S(2)}) copy-start(f32[12,128]{1,0:T(8,128)} %param.24) | copy-start | bytes 18436
  271.9 6.8 %copy-start.15 = (f32[12,128]{1,0:T(8,128)S(1)}, f32[12,128]{1,0:T(8,128)}, u32[]{:S(2)}) copy-start(f32[12,128]{1,0:T(8,128)} %param.25) | copy-start | bytes 18436
  271.9 8.6 %copy-start.12 = (bf16[8,16,4096]{2,1,0:T(8,128)(2,1)S(1)}, bf16[8,16,4096]{2,1,0:T(8,128)(2,1)}, u32[]{:S(2)}) copy-start(bf16[8,16,4096]{2,1,0:T(8,128)(2,1)} %get-tuple-element.58) | copy-start | bytes 3145732
  277.8 2.9 copy-start.11
  280.7 1.6 copy-start.8
  280.7 2.2 copy-start.9
  280.7 2.8 copy-start.10
  283.6 4.4 %copy-start.5 = (f32[128,8192]{1,0:T(8,128)S(1)}, f32[128,8192]{1,0:T(8,128)}, u32[]{:S(2)}) copy-start(f32[128,8192]{1,0:T(8,128)} %param.20) | copy-start | bytes 12582916
  283.6 6.1 %copy-start.6 = (f32[128,8192]{1,0:T(8,128)S(1)}, f32[128,8192]{1,0:T(8,128)}, u32[]{:S(2)}) copy-start(f32[128,8192]{1,0:T(8,128)} %param.21) | copy-start | bytes 12582916
  283.6 7.3 %copy-start.7 = (f32[128,8192]{1,0:T(8,128)S(1)}, f32[128,8192]{1,0:T(8,128)}, u32[]{:S(2)}) copy-start(f32[128,8192]{1,0:T(8,128)} %param.22) | copy-start | bytes 12582916

commit v4 on v3

--- a/solution.py
+++ b/solution.py
@@ -175,10 +175,10 @@
 GROUP_AT = (0, 2048, 4096, 1536)
 SPLITS = ((512, 1024), (1024, 1536), (1024, 1536), (128, 256))
 N_COPY = 31
-GROUPS = (1, 2, 3)
+GROUPS = (3, 1, 2)
 BEFORE = tuple((0, op) for op in ("z1", "x1", "z2", "y1", "z3", "x2", "x3", "y2", "z4", "x4", "x5"))
 BEFORE += tuple((g, op) for op in ("z1", "z2", "y1") for g in GROUPS)
-BEFORE += tuple((0, op) for op in ("y3", "z5", "sx", "sy", "sz", "end"))
+BEFORE += tuple((0, op) for op in ("y3", "z5", "sx", "sy", "sz", "got"))
 PUSHED = tuple((g, op) for op in ("z3", "x1", "x2", "x3") for g in GROUPS)
 STEPS = {
     0: tuple((g, "z4") for g in GROUPS),
@@ -188,7 +188,11 @@
     9: tuple((g, "y3") for g in GROUPS),
     12: tuple((g, "z5") for g in GROUPS),
 }
-LAST = tuple((g, op) for op in ("sx", "sy", "sz", "end") for g in GROUPS)
+LAST = (
+    tuple((g, op) for g in (3, 1) for op in ("sx", "sy", "sz")) + ((3, "got"),),
+    tuple((2, op) for op in ("sx", "sy", "sz")) + ((1, "got"),),
+    ((2, "got"),),
+)
 
 
 def ctx_device(t):
@@ -273,9 +277,11 @@
     }
 
     def step(self, name):
-        if name == "end":
+        if name == "got":
             for copy in (*self.copies["sx"], *self.copies["sy"], *self.copies["sz"]):
                 copy.wait_recv()
+            return
+        if name == "end":
             for copies in self.copies.values():
                 for copy in copies:
                     copy.wait_send()
@@ -304,22 +310,22 @@
 
 
 def front_kernel(
-    shard, vec_shard, x_ref, seg_ref,
-    out_attn, out_ffn, out_vec, out_held, out_mixed, out_full, out_lse,
-    wa, vecs, ready, held, mixed, out_t, keys, values_t, seg_col, scores,
+    shard, vec_shard, x_ref, seg_ref, cot_ref, keep_ref,
+    out_attn, out_held, out_full, out_lse,
+    out_ref, one_ref, x_t, o_t, h_t, f_t, a_low_ref, du_ref, g_ref, vec_ref, ready_ref,
+    wa, w_one, w_two, w_out, vecs, small, ready, held, mixed, out_t, keys, values_t, seg_col, scores,
+    mixed_rows, normal_one, slope, total,
     ag_send, ag_recv, vec_send, vec_recv, q_send, q_recv, o_send, o_recv, local_sem, out_sem,
 ):
     core = lax.axis_index("core")
     place = lax.axis_index(CTX)
     x, yh, yl = lax.axis_index("x"), lax.axis_index("yh"), lax.axis_index("yl")
 
+    weights = (wa, w_one, w_two, w_out)
+
     def dest(g):
         def view(c, xs, yhs, rows, cols):
-            if g == 0:
-                return wa.at[c, xs, yhs, rows, cols]
-            start = (0, 0, FF, 3 * D)[g] + c * GROUP_COLS[g] + cols.start
-            target = out_attn if g == 3 else out_ffn
-            return target.at[xs, yhs, rows, pl.ds(pl.multiple_of(start, 128), cols.stop - cols.start)]
+            return weights[g].at[c, xs, yhs, rows, cols]
 
         return view
 
@@ -354,6 +360,8 @@
     vec_cross.wait_send()
     for copy in (*vec_x, *vec_x2):
         copy.wait()
+    for f in range(N_FSDP):
+        small[:, f * TOK : (f + 1) * TOK] = vecs[f // 2, f % 2].astype(f32)
 
     for part in range(6):
         c, col = part // 3, (part % 3) * 512
@@ -363,9 +371,7 @@
         value = dot(x_ref[...], weight)
         if kind != 1:
             row = 0 if kind == 0 else 1
-            value = value + jnp.concatenate(
-                [vecs[f // 2, f % 2, row : row + 1, :].astype(f32) for f in range(first // 2, first // 2 + 4)], axis=1
-            )
+            value = value + small[row : row + 1, first * HEAD : first * HEAD + 512]
         value = value.T.astype(bf16)
         for h in range(8):
             for m in range(MB):
@@ -411,42 +417,55 @@
         for copy in returns[m]:
             copy.start()
         mixed[place, m] = out_t[place, m]
-    last = [pltpu.make_async_copy(held, out_held, out_sem.at[4])]
-    last[0].start()
-    out_vec[...] = vecs[...]
-    stages(LAST)
+    outs.append(pltpu.make_async_copy(held, out_held, out_sem.at[4]))
+    outs[-1].start()
+
+    def before(n):
+        stages(LAST[n])
+
     for m in range(MB):
-        for copy in swaps[m]:
+        for copy in returns[m]:
+            copy.wait_recv()
+    dense_part(
+        mixed, x_ref, cot_ref, keep_ref, small, w_out, w_one, w_two, before,
+        out_ref, one_ref, x_t, o_t, h_t, f_t, a_low_ref, du_ref, g_ref, vec_ref, ready_ref,
+        mixed_rows, normal_one, slope, total,
+    )
+    for m in range(MB):
+        for copy in (*swaps[m], *returns[m]):
             copy.wait_send()
-        for copy in returns[m]:
-            copy.wait()
-    last.append(pltpu.make_async_copy(mixed, out_mixed, out_sem.at[5]))
-    last[1].start()
-    for copy in (*outs, *last):
+    stages([(g, "end") for g in (0, *GROUPS)])
+    for copy in outs:
         copy.wait()
 
 
-def front(shard, vec_shard, x, seg_rows):
+def front(shard, vec_shard, x, seg_rows, cot, keep):
     vmem = pl.BlockSpec(memory_space=pltpu.VMEM)
     hbm = pl.BlockSpec(memory_space=pl.ANY)
     sem = lambda n: pltpu.SemaphoreType.DMA((n,))
-    blocks = lambda rows, dt: (N_CTX, MB, rows, TOK)
+    turned = jax.ShapeDtypeStruct((D, ROWS), bf16)
     return pl.pallas_call(
         front_kernel,
-        in_specs=[hbm, vmem, vmem, vmem],
-        out_specs=[hbm, hbm, vmem, hbm, hbm, vmem, vmem],
+        in_specs=[hbm, vmem, vmem, vmem, vmem, vmem],
+        out_specs=[hbm, hbm] + [vmem] * 13,
         out_shape=[
-            jax.ShapeDtypeStruct((4, 2, TOK, 4 * D), bf16),
-            jax.ShapeDtypeStruct((4, 2, TOK, 2 * FF), bf16),
-            jax.ShapeDtypeStruct((4, 2, 16, TOK), bf16),
+            jax.ShapeDtypeStruct((4, 2, TOK, 3 * D), bf16),
             jax.ShapeDtypeStruct((N_CTX, MB, SENT, TOK), bf16),
-            jax.ShapeDtypeStruct((N_CTX, MB, HEAD, TOK), bf16),
             jax.ShapeDtypeStruct((N_CTX, MB, HEAD, TOK), f32),
             jax.ShapeDtypeStruct((N_CTX, MB, 1, TOK), f32),
+            jax.ShapeDtypeStruct((ROWS, D), bf16),
+            jax.ShapeDtypeStruct((ROWS, D), f32),
+            turned, turned, turned, turned,
+            jax.ShapeDtypeStruct((ROWS, D), bf16),
+            jax.ShapeDtypeStruct((ROWS, FF), bf16),
+            jax.ShapeDtypeStruct((ROWS, FF), bf16),
+            jax.ShapeDtypeStruct((N_FSDP, 16, TOK), f32),
+            jax.ShapeDtypeStruct((HEADS, MB, HEAD, TOK), bf16),
         ],
         scratch_shapes=[
-            pltpu.VMEM((2, 4, 2, TOK, 1536), bf16),
+            *(pltpu.VMEM((2, 4, 2, TOK, GROUP_COLS[g]), bf16) for g in range(4)),
             pltpu.VMEM((4, 2, 16, TOK), bf16),
+            pltpu.VMEM((16, D), f32),
             pltpu.VMEM((N_CTX, MB, SENT, TOK), bf16),
             pltpu.VMEM((N_CTX, MB, SENT, TOK), bf16),
             pltpu.VMEM((N_CTX, MB, HEAD, TOK), bf16),
@@ -455,28 +474,32 @@
             pltpu.VMEM((HEAD, PACK), bf16),
             pltpu.VMEM((PACK, TOK), f32),
             pltpu.VMEM((PACK, BLK), f32),
+            pltpu.VMEM((ROWS, D), bf16),
+            pltpu.VMEM((ROWS, D), f32),
+            pltpu.VMEM((ROWS, FF), f32),
+            pltpu.VMEM((ROWS, D), f32),
             sem(4 * N_COPY), sem(4 * N_COPY), sem(7), sem(7), sem(32), sem(32), sem(32), sem(32),
             sem(12), sem(6),
         ],
         compiler_params=pltpu.CompilerParams(
-            collective_id=2, has_side_effects=True, vmem_limit_bytes=48 * 2**20
+            collective_id=2, has_side_effects=True, vmem_limit_bytes=60 * 2**20
         ),
         cost_estimate=pl.CostEstimate(
-            flops=4 * MB * PACK * PACK * HEAD + 2 * ROWS * D * 3 * D, bytes_accessed=32 * 2**20,
+            flops=4 * MB * PACK * PACK * HEAD + 2 * ROWS * D * (5 * D + 4 * FF), bytes_accessed=32 * 2**20,
             transcendentals=MB * PACK * PACK,
         ),
         name="front",
-    )(shard, vec_shard, x, seg_rows)
+    )(shard, vec_shard, x, seg_rows, cot, keep)
 
 
 def back_kernel(
-    left_x, left_o, left_h, left_f, right_o, right_u, right_g, vec, grad_ready, held_in, full, lse,
-    out_attn, out_ffn, out_vec, out_sq, out_q,
+    left_x, left_o, left_h, left_f, right_o, right_u, right_g, vec, grad_ready, held_in, full, lse, w_qkv,
+    out_attn, out_ffn, out_vec, out_sq, out_x,
     peer_left, own_right, peer_right, own_vec, peer_vec,
     w_0, w_1, w_2, s1_0, s1_1, s1_2, s2_0, s2_1, s2_2,
     r1_0, r1_1, r1_2, r2_0, r2_1, r2_2, r3_0, r3_1, r3_2,
     gathered, sq_z, sq_y, sq_x, sq_c,
-    held, grad_held, out_t, landed, right_q, keys, values, keys_t, seg_col, acc_k, acc_v, square_acc,
+    held, grad_held, out_t, landed, right_q, keys, values, keys_t, seg_col, acc_kv, square_acc, w_part,
     swap_send, swap_recv, ring_send, ring_recv, gather_send, gather_recv, sq_send, sq_recv,
     o_send, o_recv, q_send, q_recv, local_sem, out_sem,
 ):
@@ -619,8 +642,7 @@
 
     for m in range(MB):
         load_side(held, m, keys, values, keys_t, None, seg_col)
-        acc_k[...] = jnp.zeros_like(acc_k)
-        acc_v[...] = jnp.zeros_like(acc_v)
+        acc_kv[...] = jnp.zeros_like(acc_kv)
         for copy in pushes[m]:
             copy.wait_recv()
 
@@ -639,6 +661,10 @@
             row_lse = pair(lse, m, j, slice(0, 1))
             delta = jnp.sum(grad_t.astype(f32) * pair(full, m, j, slice(0, HEAD)), axis=0, keepdims=True)
             acc_q = jnp.zeros((HEAD, BLK), f32)
+            none = jnp.zeros((BLK, HEAD), bf16)
+            sides = jnp.concatenate(
+                [jnp.concatenate([query_t.T, none], axis=1), jnp.concatenate([none, grad_t.T], axis=1)], axis=0
+            )
             for k in range(NBLK):
                 at = slice(k * BLK, (k + 1) * BLK)
                 s = dot(keys[at, :], query_t) * SCALE2 - row_lse
@@ -648,8 +674,7 @@
                 dp = dot(values[at, :], grad_t)
                 ds = (p * (dp - delta)).astype(bf16)
                 acc_q = acc_q + dot(keys_t[:, at], ds)
-                acc_k[:, at] += dot_nt(query_t, ds)
-                acc_v[:, at] += dot_nt(grad_t, p.astype(bf16))
+                acc_kv[at, :] += dot(jnp.concatenate([ds, p.astype(bf16)], axis=1), sides)
             acc_q = (acc_q * SCALE).astype(bf16)
             out_t[2 * j, m, :HEAD, :] = acc_q[:, :TOK]
             out_t[2 * j + 1, m, :HEAD, :] = acc_q[:, TOK:]
@@ -658,33 +683,45 @@
         lax.fori_loop(0, NBLK, query_block, 0)
         for s in range(N_CTX):
             at = slice(s * TOK, (s + 1) * TOK)
-            out_t[s, m, HEAD : 2 * HEAD, :] = (acc_k[:, at] * SCALE).astype(bf16)
-            out_t[s, m, 2 * HEAD :, :] = acc_v[:, at].astype(bf16)
+            both = acc_kv[at, :].T
+            out_t[s, m, HEAD : 2 * HEAD, :] = (both[:HEAD] * SCALE).astype(bf16)
+            out_t[s, m, 2 * HEAD :, :] = both[HEAD:].astype(bf16)
         for copy in returns[m]:
             copy.start()
         landed[place, m] = out_t[place, m]
 
+    fetch_w = [
+        pltpu.make_async_copy(w_qkv.at[:, n * COLS : (n + 1) * COLS], w_part.at[n % 2], local_sem.at[4 + n])
+        for n in range(6)
+    ]
     done = [task for tasks in TASKS.values() for task in tasks]
     for phase in (0, 1):
         for b in range(3):
             for p in range(3):
                 if (phase, b, p) not in done:
                     reduce(phase, p, b * COLS, COLS)
+    gives = []
     for m in range(MB):
         for copy in pushes[m]:
             copy.wait_send()
         for copy in returns[m]:
             copy.wait()
+        if m == 0:
+            fetch_w[0].start()
+            fetch_w[1].start()
         for i in range(HEADS // 2):
             for kind in range(3):
                 rows = slice(kind * HEAD, (kind + 1) * HEAD)
                 both = jnp.concatenate([landed[2 * i, m, rows, :], landed[2 * i + 1, m, rows, :]], axis=0)
                 right_q[m * TOK : (m + 1) * TOK, kind * D + i * 128 : kind * D + (i + 1) * 128] = both.T
-    give = send(
-        right_q.at[:, pl.ds(pl.multiple_of(other * WIDTHS[0], 512), WIDTHS[0])], peer_right.at[:, 0 : WIDTHS[0]],
-        (swap_send, swap_recv), 1, to_core,
-    )
-    give.start()
+        rows = slice(m * TOK, (m + 1) * TOK)
+        gives.append(
+            send(
+                right_q.at[rows, pl.ds(pl.multiple_of(other * WIDTHS[0], 512), WIDTHS[0])],
+                peer_right.at[rows, 0 : WIDTHS[0]], (swap_send, swap_recv), (1, 9)[m], to_core,
+            )
+        )
+        gives[m].start()
     sum_q = jnp.sum(right_q[:, :D].astype(f32), axis=0, keepdims=True)
     sum_v = jnp.sum(right_q[:, 2 * D :].astype(f32), axis=0, keepdims=True)
     row = lax.broadcasted_iota(jnp.int32, (16, TOK), 0)
@@ -695,9 +732,8 @@
         own_vec[f // 2, f % 2, 0, 0] = value.astype(bf16)
     give_vec = send(own_vec, peer_vec, (swap_send, swap_recv), 8, to_core)
     give_vec.start()
-    keep_q = pltpu.make_async_copy(right_q, out_q, local_sem.at[4])
-    keep_q.start()
-    give.wait()
+    for copy in gives:
+        copy.wait()
     for p, at, width in blocks(3):
         if width == COLS:
             multiply(p, 3)
@@ -706,6 +742,15 @@
             works[0][:, :, :, :, :, VEC_AT:] = (own_vec[...].astype(f32) + peer_vec[...].astype(f32)).astype(bf16)
         for copy in copies(p, 0, at, width):
             copy.start()
+    for n in range(6):
+        fetch_w[n].wait()
+        part = dot_nt(right_q[:, n * COLS : (n + 1) * COLS], w_part[n % 2])
+        if n == 0:
+            out_x[...] = part
+        else:
+            out_x[...] += part
+        if n < 4:
+            fetch_w[n + 2].start()
     for b in range(3):
         for p, at, width in blocks(b):
             reduce(2, p, at, width)
@@ -798,10 +843,9 @@
         copy.start()
     for copy in locals_:
         copy.wait()
-    keep_q.wait()
-
-
-def back(lefts, rights, vec, grad_ready, held, full, lse):
+
+
+def back(lefts, rights, vec, grad_ready, held, full, lse, w_qkv):
     vmem = pl.BlockSpec(memory_space=pltpu.VMEM)
     hbm = pl.BlockSpec(memory_space=pl.ANY)
     scratch = [
@@ -830,22 +874,22 @@
         pltpu.VMEM((PACK, HEAD), bf16),
         pltpu.VMEM((HEAD, PACK), bf16),
         pltpu.VMEM((PACK, TOK), f32),
-        pltpu.VMEM((HEAD, PACK), f32),
-        pltpu.VMEM((HEAD, PACK), f32),
+        pltpu.VMEM((PACK, 2 * HEAD), f32),
         pltpu.VMEM((8, 128), f32),
+        pltpu.VMEM((2, D, COLS), bf16),
     ]
-    for count in (9, 9, 135, 135, 12, 12, 10, 10, 32, 32, 32, 32, 5, 25):
+    for count in (10, 10, 135, 135, 12, 12, 10, 10, 32, 32, 32, 32, 10, 25):
         scratch.append(pltpu.SemaphoreType.DMA((count,)))
     out = pl.pallas_call(
         back_kernel,
-        in_specs=[vmem] * 4 + [hbm] * 3 + [vmem, vmem, hbm, vmem, vmem],
-        out_specs=[hbm, hbm, hbm, vmem, hbm],
+        in_specs=[vmem] * 4 + [hbm] * 3 + [vmem, vmem, hbm, vmem, vmem, hbm],
+        out_specs=[hbm, hbm, hbm, vmem, vmem],
         out_shape=[
             jax.ShapeDtypeStruct((8, 16, 4 * D), bf16),
             jax.ShapeDtypeStruct((8, 16, 2 * FF), bf16),
             jax.ShapeDtypeStruct((8, 16, 128), bf16),
             jax.ShapeDtypeStruct((8, 128), f32),
-            jax.ShapeDtypeStruct((ROWS, 3 * D), bf16),
+            jax.ShapeDtypeStruct((ROWS, D), f32),
         ],
         scratch_shapes=scratch,
         compiler_params=pltpu.CompilerParams(
@@ -856,7 +900,7 @@
             transcendentals=MB * PACK * PACK,
         ),
         name="back",
-    )(*lefts, *rights, vec, grad_ready, held, full, lse)
+    )(*lefts, *rights, vec, grad_ready, held, full, lse, w_qkv)
     return out[0].reshape(TOK, 4 * D), out[1].reshape(TOK, 2 * FF), out[2][0, :12], jnp.sum(out[3]), out[4]
 
 
@@ -899,23 +943,17 @@
     return value * top / low
 
 
-def dense_kernel(
-    mixed_ref, x_ref, cot_ref, keep_ref, small_ref, w_attn, w_ffn,
+def w_block(ref, n):
+    per = ref.shape[-1] // CHUNK
+    at = (n % per) * CHUNK
+    return ref[n // per, :, :, :, at : at + CHUNK].reshape(D, CHUNK)
+
+
+def dense_part(
+    mixed_ref, x_ref, cot_ref, keep_ref, small_ref, w_out, w_one, w_two, before,
     out_ref, one_ref, x_t, o_t, h_t, f_t, a_low_ref, du_ref, g_ref, vec_ref, ready_ref,
-    w_out, w_one, w_two, mixed, normal_one_ref, slope, total, sem,
+    mixed, normal_one_ref, slope, total,
 ):
-    fetch_out = pltpu.make_async_copy(w_attn.at[:, 3 * D :], w_out, sem.at[0])
-    fetch_out.start()
-    fetch_one, fetch_two = [], []
-    for n in range(N_CHUNK):
-        at = n * CHUNK
-        fetch_one.append(pltpu.make_async_copy(w_ffn.at[:, at : at + CHUNK], w_one.at[n], sem.at[1 + n]))
-        fetch_two.append(
-            pltpu.make_async_copy(w_ffn.at[:, FF + at : FF + at + CHUNK], w_two.at[n], sem.at[1 + N_CHUNK + n])
-        )
-        fetch_one[n].start()
-        fetch_two[n].start()
-
     def row(i):
         return small_ref[i : i + 1, :]
 
@@ -933,26 +971,24 @@
             both = jnp.concatenate([mixed_ref[2 * i, m], mixed_ref[2 * i + 1, m]], axis=0)
             o_t[i * 128 : (i + 1) * 128, tok] = both
             mixed[tok, i * 128 : (i + 1) * 128] = both.T
-    x_t[...] = x_ref[...].T
-    fetch_out.wait()
-    normed_one, normal_one, inverse_one = layer_stats(
-        x_ref[...].astype(f32) + dot(mixed[...], w_out[...]) + row(2), row(4), row(5)
-    )
+    before(0)
+    branch = jnp.concatenate([dot(mixed[...], w_block(w_out, n)) for n in range(2)], axis=1)
+    normed_one, normal_one, inverse_one = layer_stats(x_ref[...].astype(f32) + branch + row(2), row(4), row(5))
     normal_one_ref[...] = normal_one
     normed_low = normed_one.astype(bf16)
     h_t[...] = normed_low.T
     total[...] = normed_one + row(3)
+    before(1)
     for n in range(N_CHUNK):
         cols = slice(n * CHUNK, (n + 1) * CHUNK)
-        fetch_one[n].wait()
         bias = small_ref[8 + n // 2 : 9 + n // 2, (n % 2) * CHUNK : (n % 2 + 1) * CHUNK]
-        u = dot(normed_low, w_one[n]) + bias
+        u = dot(normed_low, w_block(w_one, n)) + bias
         share = 0.5 + 0.5 * erf(u * math.sqrt(0.5))
-        g = (u * share).astype(bf16)
-        g_ref[:, cols] = g
+        g_ref[:, cols] = (u * share).astype(bf16)
         slope[:, cols] = share + u * (jnp.exp(-0.5 * u * u) * (1.0 / math.sqrt(2.0 * math.pi)))
-        fetch_two[n].wait()
-        total[...] += dot_nt(g, w_two[n])
+    before(2)
+    for n in range(N_CHUNK):
+        total[...] += dot_nt(g_ref[:, n * CHUNK : (n + 1) * CHUNK], w_block(w_two, n))
     output, normal_two, inverse_two = layer_stats(total[...], row(6), row(7))
     keep = keep_ref[...]
     out_ref[...] = (output * keep).astype(bf16)
@@ -966,13 +1002,13 @@
     total[...] = grad_two
     for n in range(N_CHUNK):
         cols = slice(n * CHUNK, (n + 1) * CHUNK)
-        du = (dot(f_low, w_two[n]) * slope[:, cols]).astype(bf16)
+        du = (dot(f_low, w_block(w_two, n)) * slope[:, cols]).astype(bf16)
         du_ref[:, cols] = du
         part = sums(du.astype(f32))
         for i in range(CHUNK // TOK):
             f = (n % 2) * (CHUNK // TOK) + i
             vec_ref[f, 8 + n // 2 : 9 + n // 2, :] = part[:, i * TOK : (i + 1) * TOK]
-        total[...] += dot_nt(du, w_one[n])
+        total[...] += dot_nt(du, w_block(w_one, n))
     grad_normed = total[...]
     normal_one = normal_one_ref[...]
     put(4, sums(grad_normed * normal_one))
@@ -982,46 +1018,15 @@
     a_low = grad_one.astype(bf16)
     a_low_ref[...] = a_low
     put(2, sums(a_low.astype(f32)))
-    grad_mixed = dot_nt(a_low, w_out[...]).T.astype(bf16)
+    for n in range(2):
+        part = a_low[:, n * CHUNK : (n + 1) * CHUNK]
+        part = dot_nt(part, w_block(w_out, n))
+        grad_mixed = part if n == 0 else grad_mixed + part
+    grad_mixed = grad_mixed.T.astype(bf16)
     for h in range(HEADS):
         for m in range(MB):
             ready_ref[h, m] = grad_mixed[h * HEAD : (h + 1) * HEAD, m * TOK : (m + 1) * TOK]
-
-
-def dense(mixed_t, x, cot, keep, small, w_attn, w_ffn):
-    vmem = pl.BlockSpec(memory_space=pltpu.VMEM)
-    hbm = pl.BlockSpec(memory_space=pl.ANY)
-    turned = jax.ShapeDtypeStruct((D, ROWS), bf16)
-    return pl.pallas_call(
-        dense_kernel,
-        in_specs=[vmem] * 5 + [hbm, hbm],
-        out_specs=[vmem] * 11,
-        out_shape=[
-            jax.ShapeDtypeStruct((ROWS, D), bf16),
-            jax.ShapeDtypeStruct((ROWS, D), f32),
-            turned, turned, turned, turned,
-            jax.ShapeDtypeStruct((ROWS, D), bf16),
-            jax.ShapeDtypeStruct((ROWS, FF), bf16),
-            jax.ShapeDtypeStruct((ROWS, FF), bf16),
-            jax.ShapeDtypeStruct((N_FSDP, 16, TOK), f32),
-            jax.ShapeDtypeStruct((HEADS, MB, HEAD, TOK), bf16),
-        ],
-        scratch_shapes=[
-            pltpu.VMEM((D, D), bf16),
-            pltpu.VMEM((N_CHUNK, D, CHUNK), bf16),
-            pltpu.VMEM((N_CHUNK, D, CHUNK), bf16),
-            pltpu.VMEM((ROWS, D), bf16),
-            pltpu.VMEM((ROWS, D), f32),
-            pltpu.VMEM((ROWS, FF), f32),
-            pltpu.VMEM((ROWS, D), f32),
-            pltpu.SemaphoreType.DMA((1 + 2 * N_CHUNK,)),
-        ],
-        compiler_params=pltpu.CompilerParams(vmem_limit_bytes=56 * 2**20),
-        cost_estimate=pl.CostEstimate(
-            flops=2 * ROWS * D * (2 * D + 4 * FF), bytes_accessed=32 * 2**20, transcendentals=ROWS * FF
-        ),
-        name="dense",
-    )(mixed_t, x, cot, keep, small, w_attn, w_ffn)
+    x_t[...] = x_ref[...].T
 
 
 def adamw(weight, grad_value, first, second, rate, decay):
@@ -1054,14 +1059,10 @@
 
     seg_rows = jnp.broadcast_to(seg.astype(bf16)[:, None, :], (MB, 16, TOK))
     vec_shard = jnp.pad(vectors.astype(bf16), ((0, 4), (0, 0)))
-    w_attn, ffn_out, vecs, held, mixed_t, mixed_full, lse = front(shard, vec_shard, x, seg_rows)
-    w_attn = w_attn.reshape(D, 4 * D)
-    w_ffn = ffn_out.reshape(D, 2 * FF)
-    small = jnp.transpose(vecs.reshape(N_FSDP, 16, TOK), (1, 0, 2)).reshape(16, D).astype(f32)
-    output, grad_one, x_t, o_t, h_t, f_t, a_low, du, g, vec_rows, grad_ready = dense(
-        mixed_t, x, cot, keep, small, w_attn, w_ffn
-    )
-    total_attn, total_ffn, total_vec, square_sum, grad_qkv = back(
+    (
+        w_qkv, held, mixed_full, lse, output, grad_one, x_t, o_t, h_t, f_t, a_low, du, g, vec_rows, grad_ready,
+    ) = front(shard, vec_shard, x, seg_rows, cot, keep)
+    total_attn, total_ffn, total_vec, square_sum, grad_x = back(
         (x_t, o_t, h_t, f_t),
         (a_low, du, g),
         vec_rows,
@@ -1069,8 +1070,9 @@
         held,
         mixed_full,
         lse,
+        w_qkv.reshape(D, 3 * D),
     )
-    grad_tokens = grad_one + dot_nt(grad_qkv, w_attn[:, : 3 * D])
+    grad_tokens = grad_one + grad_x
     total_attn, total_ffn, total_vec = total_attn.astype(f32), total_ffn.astype(f32), total_vec.astype(f32)
     grad_norm = jnp.sqrt(square_sum)
     factor = jnp.minimum(1.0, CLIP_NORM / (grad_norm + 1e-06))

time: 305 us -> 287 us (0.941)
  local copies, waits for them, and re-layouts: 15 us -> 5.82 us
  matrix products: 5.97 us -> 0 us
  Pallas kernels: 257 us -> 252 us
  other arithmetic: 18 us -> 21.8 us
    unnamed x35 -> x27, local copies, waits for them, and re-layouts: 10.3 us -> 1.91 us
    dot_general x1 -> x0, matrix products: 5.97 us -> none  [dot_nt(): return lax.dot_general(a, b, CONTRACT_COLS, preferred_element_type=f32)]
    pallas_call x2 -> x1, Pallas kernels: 120 us -> 116 us  [front(): pl.pallas_call(front_kernel, in_specs=[hbm, vmem, vmem, vmem, vmem, vmem]...]
where the time goes in v4:
time: 287 us; the launch traced here: 283 us
  Pallas kernels  252 us (88%)
  other arithmetic  21.8 us (8%)
  local copies, waits for them, and re-layouts  5.82 us (2%)
  between operations  3.1 us (1%)
    pallas_call x1, Pallas kernels, back(): pl.pallas_call(back_kernel, in_specs=[vmem] * 4 + [hbm] * 3 + [vmem, vmem...  136 us
    pallas_call x1, Pallas kernels, front(): pl.pallas_call(front_kernel, in_specs=[hbm, vmem, vmem, vmem, vmem, vmem]...  116 us
    convert_element_type x1, other arithmetic, shards(): ffn_new.astype(bf16)  8.81 us

profile of v4, /device:TPU:1, one launch (start us, length us, event | category | flops | bytes accessed | tf_op | source)
XLA Modules:
  0.0 282.9 jit_solution(9717740319627516103)
XLA Ops:
  0.6 0.0 copy-start.1
  0.7 1.8 dynamic-slice_convert_fusion.1
  2.5 0.4 copy-done.1
  2.9 0.0 copy-start.12
  2.9 0.0 copy-start.11
  2.9 0.0 copy-start.8
  3.0 1.3 pad_maximum_fusion.shard
  4.2 0.0 copy-done.12
  4.2 0.2 reduce_window_sum.14
  4.4 0.0 copy-done.11
  4.4 0.1 convert_reduce_fusion
  4.5 0.8 copy.33.keep_ref
  5.3 0.6 broadcast_in_dim.2.seg_ref
  5.9 0.0 copy-done.8
  5.9 0.6 pad.4.vec_shard
  6.5 116.4 %front.1 = (bf16[4,2,128,3072]{3,2,1,0:T(8,128)(2,1)}, bf16[16,2,208,128]{3,2,1,0:T(8,128)(2,1)}, f32[16,2,64,128]{3,2,1,0:T(8,128)}, f32[16,2,1,128]{3,2,1,0:T(...) custom-call(bf16[128,6144]{1,0:T(8,128)(2,1)} %pad_maximum_fusion.sh, ...), custom_call_target="tpu_custom_call" | custom-call | flops 13421772800 | bytes 33554432 | tf_op jit(solution)/shard_map/front/pallas_call | solution.py:447
  122.9 135.8 %back.1 = (bf16[8,16,4096]{2,1,0:T(8,128)(2,1)}, bf16[8,16,8192]{2,1,0:T(8,128)(2,1)}, bf16[8,16,128]{2,1,0:T(8,128)(2,1)}, f32[8,128]{1,0:T(8,128)}, f32[256,1024]{1,0:T(8,128)}) custom-call(bf16[1024,256]{1,0:T(8,128)(2,1)} %get-tuple-element.37.left_x, bf16[1024,256]{1,0:T(8,128)(2,1)} %get-tuple-element.38.left_o, ...), custom_call_target="tpu_custom_call" | custom-call | flops 11811160064 | bytes 16777216 | tf_op jit(solution)/shard_map/back/pallas_call | solution.py:883
  258.7 1.3 reduce_sum.19
  260.8 0.0 copy-start
  260.8 2.2 convert_multiply_fusion
  263.0 0.6 copy-done
  263.6 0.0 copy-start.9
  263.6 0.0 copy-start.10
  263.6 0.0 copy-start.6
  263.6 0.0 copy-start.3
  263.6 8.8 %fusion.7 = (bf16[128,8192]{1,0:T(8,128)(2,1)}, f32[128,8192]{1,0:T(8,128)}, f32[128,8192]{1,0:T(8,128)}, f32[128,8192]{1,0:T(8,128)}) fusion(f32[128,8192]{1,0:T(8,128)S(1)} %copy-done, f32[8,16,8192]{2,1,0:T(8,128)S(1)} %convert_multiply_fusion, f32[128,8192]{1,0:T(8,128)} %param.21, f32[128,8192]{1,0:T(8,128)} %param.22), kind=kLoop, calls=%fused_computation.28 | loop fusion | flops 16777216 | bytes 31457280 | tf_op jit(solution)/shard_map/convert_element_type | solution.py:1097
  272.4 0.0 copy-start.2
  272.4 0.0 copy-done.9
  272.4 0.0 copy-done.10
  272.4 1.5 multiply_subtract_fusion.2
  273.9 0.7 slice_convert_fusion
  274.5 0.5 fusion.6
  275.1 0.0 copy-done.6
  275.1 0.2 convert_multiply_fusion.1
  275.3 0.0 copy-done.3
  275.3 0.0 copy-done.2
  275.3 0.0 copy-start.4
  275.3 0.0 copy-start.5
  275.3 4.1 %fusion.10 = (bf16[128,4096]{1,0:T(8,128)(2,1)}, f32[128,4096]{1,0:T(8,128)}, f32[128,4096]{1,0:T(8,128)}, f32[128,4096]{1,0:T(8,128)}) fusion(f32[128,4096]{1,0:T(8,128)S(1)} %copy-done.1, f32[8,16,4096]{2,1,0:T(8,128)S(1)} %convert_multiply_fusion.1, f32[128,4096]{1,0:T(8,128)S(1)} %copy-done.2, f32[128,4096]{1,0:T(8,128)S(1)} %copy-done.3), kind=kLoop, calls=%fused_computation.29 | loop fusion | flops 8388608 | bytes 15728640 | tf_op jit(solution)/shard_map/convert_element_type | solution.py:1096
  279.5 0.0 copy-start.7
  279.5 0.0 copy-done.4
  279.5 0.0 copy-done.5
  279.5 0.9 add_convert_fusion
  280.4 0.1 copy-done.7
  280.5 0.8 copy.37
  (5 shorter events, 0.1 us)
Async XLA Ops:
  0.6 2.2 copy-start.1
  2.9 1.4 copy-start.12
  2.9 1.5 copy-start.11
  2.9 3.1 %copy-start.8 = (f32[12,128]{1,0:T(8,128)S(1)}, f32[12,128]{1,0:T(8,128)}, u32[]{:S(2)}) copy-start(f32[12,128]{1,0:T(8,128)} %param.23) | copy-start | bytes 18436
  260.8 2.8 copy-start
  263.6 8.8 %copy-start.9 = (f32[12,128]{1,0:T(8,128)S(1)}, f32[12,128]{1,0:T(8,128)}, u32[]{:S(2)}) copy-start(f32[12,128]{1,0:T(8,128)} %param.24) | copy-start | bytes 18436
  263.6 8.8 %copy-start.10 = (f32[12,128]{1,0:T(8,128)S(1)}, f32[12,128]{1,0:T(8,128)}, u32[]{:S(2)}) copy-start(f32[12,128]{1,0:T(8,128)} %param.25) | copy-start | bytes 18436
  263.6 11.5 %copy-start.6 = (bf16[8,16,4096]{2,1,0:T(8,128)(2,1)S(1)}, bf16[8,16,4096]{2,1,0:T(8,128)(2,1)}, u32[]{:S(2)}) copy-start(bf16[8,16,4096]{2,1,0:T(8,128)(2,1)} %get-tuple-element.52) | copy-start | bytes 3145732
  263.6 11.7 %copy-start.3 = (f32[128,4096]{1,0:T(8,128)S(1)}, f32[128,4096]{1,0:T(8,128)}, u32[]{:S(2)}) copy-start(f32[128,4096]{1,0:T(8,128)} %param.19) | copy-start | bytes 6291460
  272.4 2.9 %copy-start.2 = (f32[128,4096]{1,0:T(8,128)S(1)}, f32[128,4096]{1,0:T(8,128)}, u32[]{:S(2)}) copy-start(f32[128,4096]{1,0:T(8,128)} %param.18) | copy-start | bytes 6291460
  275.3 4.2 %copy-start.4 = (f32[256,1024]{1,0:T(8,128)S(1)}, f32[256,1024]{1,0:T(8,128)}, u32[]{:S(2)}) copy-start(f32[256,1024]{1,0:T(8,128)} %get-tuple-element.36) | copy-start | bytes 3145732
  275.3 4.2 %copy-start.5 = (f32[256,1024]{1,0:T(8,128)S(1)}, f32[256,1024]{1,0:T(8,128)}, u32[]{:S(2)}) copy-start(f32[256,1024]{1,0:T(8,128)} %get-tuple-element.50) | copy-start | bytes 3145732
  279.5 1.0 copy-start.7

commit v5 on v4

--- a/solution.py
+++ b/solution.py
@@ -58,20 +58,21 @@
 COLS = 512
 N_BLK = 4
 ORDERS = (("x", "z", "y"), ("z", "y", "x"), ("y", "x", "z"))
-EARLY = ((2, 0), (2, 512), (2, 1024), (2, 1536), (3, 0), (3, 512), (3, 1024), (3, 1536), (1, 0))
-PRODUCT = tuple(
-    tuple(EARLY[b * 3 + p] for b in range(3)) + ((0, p * COLS),) for p in range(3)
-)
-VEC_AT = 2048
-PART_COLS = (2048 + 128, 2048, 2048)
+EARLY = ((0, 0), (1, 0), (2, 0), (0, 1), (1, 1), (2, 1), (0, 2), (1, 2), (2, 2))
+N_EARLY = (3, 3, 3)
+EARLY_PRODUCT = ((2, 0), (2, 512), (2, 1024), (2, 1536), (3, 0), (3, 512), (3, 1024), (3, 1536), (1, 0))
+PRODUCT = {part_block: product for part_block, product in zip(EARLY, EARLY_PRODUCT)}
+PRODUCT.update({(p, N_EARLY[p]): (0, p * COLS) for p in range(3)})
+PART_AT = (0, 2048, 4096, 6144)
+VEC_AT = 3072
 WIDTHS = (1536, 512, 2048, 2048)
 OFFSETS = (0, 1536, 2048, 4096)
 HALF_Z = 3072
 TASKS = {}
-for _n, _at in enumerate((7, 8, 9, 10, 11, 12, 13, 14, 15)):
-    TASKS.setdefault(_at, []).append((0, _n // 3, _n % 3))
-for _n, _at in enumerate(()):
-    TASKS.setdefault(_at, []).append((1, _n // 3, _n % 3))
+for _n, _at in enumerate((2, 2, 2, 5, 5, 5, 8, 8, 8)):
+    TASKS.setdefault(_at, []).append(("relay", *EARLY[_n]))
+for _n, _at in enumerate((7, 7, 7, 10, 10, 10, 13, 13, 13)):
+    TASKS.setdefault(_at, []).append((0, *EARLY[_n]))
 
 
 def coordinate(axis):
@@ -87,7 +88,7 @@
     return {axis: at}, at
 
 
-def pick(ref, axis, at, dims, cols):
+def pick(ref, axis, at, dims):
     index = []
     for d in dims:
         if d == axis:
@@ -98,7 +99,7 @@
             index.append(lax.rem(at, 2))
         else:
             index.append(slice(None))
-    return ref.at[(*index, slice(None), cols)]
+    return ref.at[tuple(index)]
 
 
 def dims_after(order, n):
@@ -496,21 +497,21 @@
     left_x, left_o, left_h, left_f, right_o, right_u, right_g, vec, grad_ready, held_in, full, lse, w_qkv,
     out_attn, out_ffn, out_vec, out_sq, out_x,
     peer_left, own_right, peer_right, own_vec, peer_vec,
-    w_0, w_1, w_2, s1_0, s1_1, s1_2, s2_0, s2_1, s2_2,
-    r1_0, r1_1, r1_2, r2_0, r2_1, r2_2, r3_0, r3_1, r3_2,
+    *rest_refs,
+):
+    stores, rest_refs = rest_refs[:24], rest_refs[24:]
+    (
     gathered, sq_z, sq_y, sq_x, sq_c,
     held, grad_held, out_t, landed, right_q, keys, values, keys_t, seg_col, acc_kv, square_acc, w_part,
     swap_send, swap_recv, ring_send, ring_recv, gather_send, gather_recv, sq_send, sq_recv,
     o_send, o_recv, q_send, q_recv, local_sem, out_sem,
-):
+    ) = rest_refs
     core = lax.axis_index("core")
     other = 1 - core
     place = lax.axis_index(CTX)
     row_place = lax.axis_index("yl") * 4 + lax.axis_index("z")
     lefts = (left_x, left_o, left_h, left_f)
     rights = (None, right_o, right_u, right_g)
-    works, firsts, seconds = (w_0, w_1, w_2), (s1_0, s1_1, s1_2), (s2_0, s2_1, s2_2)
-    recvs = ((r1_0, r1_1, r1_2), (r2_0, r2_1, r2_2), (r3_0, r3_1, r3_2))
     to_core = {"core": other}
 
     fetch = pltpu.make_async_copy(held_in, held, local_sem.at[0])
@@ -555,29 +556,71 @@
     for copy in fetches:
         copy.wait()
 
-    def blocks(b):
-        out = [(p, b * COLS, COLS) for p in range(3)]
-        if b == 3:
-            out.append((0, VEC_AT, 128))
-        return out
+    late = [(p, N_EARLY[p] * COLS, COLS) for p in range(3)] + [(0, VEC_AT, 128)]
+    early = [(p, b * COLS, COLS) for p, b in EARLY]
+
+    def number(p, at, width):
+        return 12 if width != COLS else PART_AT[p] // COLS + at // COLS
+
+    def store(kind, p, at, width):
+        return stores[4 * kind + 3].at[0] if width != COLS else stores[4 * kind + p].at[at // COLS]
 
     def copies(p, phase, at, width):
         order = ORDERS[p]
         axis = order[phase]
-        cols = slice(at, at + width)
-        src = (works, firsts, seconds)[phase][p]
         out = []
         for step in (1, 2, 3):
             to, index = peer(axis, step)
-            chunk = pick(src, axis, index, dims_after(order, phase), cols)
-            land = recvs[phase][p].at[(step - 1, *(slice(None),) * (len(lead(order, phase + 1)) + 1), cols)]
+            chunk = pick(store(phase, p, at, width), axis, index, dims_after(order, phase))
+            land = store(3 + phase, p, at, width).at[step - 1]
             out.append(
-                send(chunk, land, (ring_send, ring_recv), ((p * 3 + phase) * 5 + at // COLS) * 3 + step - 1, to)
+                send(
+                    chunk, land, (ring_send, ring_recv), 39 + 39 * phase + number(p, at, width) * 3 + step - 1, to
+                )
             )
         return out
 
+    def first_copies(p, at, width):
+        order = ORDERS[p]
+        axis = order[0]
+        n = lead(order, 1)[0]
+        halves = (slice(0, n // 2), slice(n // 2, n))
+        (up, up_at), (_, far_at), (down, down_at) = (peer(axis, step) for step in (1, 2, 3))
+        out = []
+        for k, (index, half, slot, to) in enumerate(
+            (
+                (far_at, 0, 2, up), (far_at, 1, 2, down), (up_at, 1, 0, up), (down_at, 0, 1, down),
+                (up_at, 0, 0, up), (down_at, 1, 1, down),
+            )
+        ):
+            chunk = pick(store(0, p, at, width), axis, index, dims_after(order, 0)).at[halves[half]]
+            land = store(3, p, at, width).at[slot, halves[half]]
+            out.append(send(chunk, land, (ring_send, ring_recv), number(p, at, width) * 6 + k, to))
+        return out
+
+    def begin(p, at, width):
+        for copy in first_copies(p, at, width)[:4]:
+            copy.start()
+
+    def relay(p, at, width):
+        order = ORDERS[p]
+        axis = order[0]
+        n = lead(order, 1)[0]
+        all_copies = first_copies(p, at, width)
+        land = store(3, p, at, width)
+        for half, step in ((0, 1), (1, 3)):
+            all_copies[half].wait_recv()
+            own = pick(store(0, p, at, width), axis, peer(axis, step)[1], dims_after(order, 0))
+
+            def add(i, _, own=own):
+                own[i] = (own[i].astype(f32) + land[2, i].astype(f32)).astype(bf16)
+                return 0
+
+            lax.fori_loop(half * (n // 2), (half + 1) * (n // 2), add, 0)
+            all_copies[4 + half].start()
+
     def multiply(p, b):
-        i, col = PRODUCT[p][b]
+        i, col = PRODUCT[(p, b)]
         if i == 0:
             mine = right_q.at[:, pl.ds(pl.multiple_of(core * WIDTHS[0] + col, 512), COLS)]
         else:
@@ -587,31 +630,33 @@
         def rows_block(x, _):
             rows = pl.ds(pl.multiple_of(x * 256, 256), 256)
             value = dot(lefts[i][rows, :], mine[...]) + dot(peer_left[i, rows, :], theirs[...])
-            works[p][x, :, :, :, :, b * COLS : (b + 1) * COLS] = value.astype(bf16).reshape(2, 2, 4, 16, COLS)
+            stores[p][b, x] = value.astype(bf16).reshape(2, 2, 4, 16, COLS)
             return 0
 
         lax.fori_loop(0, 4, rows_block, 0)
 
     def reduce(phase, p, at, width):
-        cols = slice(at, at + width)
         order = ORDERS[p]
         axis = order[phase]
-        src = (works, firsts, seconds)[phase][p]
-        land = recvs[phase][p]
-        for copy in copies(p, phase, at, width):
-            copy.wait()
-        own = pick(src, axis, coordinate(axis), dims_after(order, phase), cols)
-        rest = len(lead(order, phase + 1)) - 1
+        land = store(3 + phase, p, at, width)
+        if phase == 0:
+            all_copies = first_copies(p, at, width)
+            for copy in all_copies[:2]:
+                copy.wait_send()
+            for copy in all_copies[2:]:
+                copy.wait()
+        else:
+            for copy in copies(p, phase, at, width):
+                copy.wait()
+        own = pick(store(phase, p, at, width), axis, coordinate(axis), dims_after(order, phase))
         if phase < 2:
-            dst = (firsts, seconds)[phase][p]
+            dst = store(phase + 1, p, at, width)
 
             def add(n, _):
-                tail = (*(slice(None),) * (rest + 1), cols)
-                inner = (*(slice(None),) * (rest + 1), slice(None))
-                value = own[(n, *inner)].astype(f32)
-                for step in range(3):
-                    value = value + land[(step, n, *tail)].astype(f32)
-                dst[(n, *tail)] = value.astype(bf16)
+                value = own[n].astype(f32)
+                for step in range(3 if phase else 2):
+                    value = value + land[step, n].astype(f32)
+                dst[n] = value.astype(bf16)
                 return 0
 
             lax.fori_loop(0, lead(order, phase + 1)[0], add, 0)
@@ -620,8 +665,8 @@
             return
         value = own[...].astype(f32)
         for step in range(3):
-            value = value + land[step, :, cols].astype(f32)
-        to = p * 2048 + at if width == COLS else 6144
+            value = value + land[step].astype(f32)
+        to = PART_AT[p] + at if width == COLS else 6144
         gathered[core, row_place, :, to : to + width] = value.astype(bf16)
         square = value * value
         if width != COLS:
@@ -631,14 +676,18 @@
             squares = squares + square[:8, c : c + 128] + square[8:, c : c + 128]
         square_acc[...] = squares
 
+    def run_task(phase, p, b):
+        if phase == "relay":
+            relay(p, b * COLS, COLS)
+        else:
+            reduce(phase, p, b * COLS, COLS)
+
     square_acc[...] = jnp.zeros_like(square_acc)
     for copy in swaps:
         copy.wait()
-    for b in range(3):
-        for p, at, width in blocks(b):
-            multiply(p, b)
-            for copy in copies(p, 0, at, width):
-                copy.start()
+    for p, at, width in early:
+        multiply(p, at // COLS)
+        begin(p, at, width)
 
     for m in range(MB):
         load_side(held, m, keys, values, keys_t, None, seg_col)
@@ -652,8 +701,8 @@
 
                     @pl.when(j == at % NBLK)
                     def _(tasks=tasks):
-                        for phase, b, p in tasks:
-                            reduce(phase, p, b * COLS, COLS)
+                        for phase, p, b in tasks:
+                            run_task(phase, p, b)
 
             query_t = pair(held, m, j, slice(0, HEAD))
             seg_row = pair(held, m, j, slice(3 * HEAD, 3 * HEAD + 1)).astype(f32)
@@ -665,16 +714,24 @@
             sides = jnp.concatenate(
                 [jnp.concatenate([query_t.T, none], axis=1), jnp.concatenate([none, grad_t.T], axis=1)], axis=0
             )
-            for k in range(NBLK):
-                at = slice(k * BLK, (k + 1) * BLK)
-                s = dot(keys[at, :], query_t) * SCALE2 - row_lse
-                col = seg_col[at, :]
-                same = jnp.concatenate([col, col], axis=1) == seg_row
-                p = jnp.exp2(jnp.where(same, s, NEG_LARGE))
-                dp = dot(values[at, :], grad_t)
-                ds = (p * (dp - delta)).astype(bf16)
-                acc_q = acc_q + dot(keys_t[:, at], ds)
-                acc_kv[at, :] += dot(jnp.concatenate([ds, p.astype(bf16)], axis=1), sides)
+            block = lambda k: slice(k * BLK, (k + 1) * BLK)
+            ahead = (dot(keys[block(0), :], query_t), dot(values[block(0), :], grad_t))
+            behind = None
+            for k in range(NBLK + 1):
+                if k < NBLK:
+                    at = block(k)
+                    s, dp = ahead
+                    if k + 1 < NBLK:
+                        ahead = (dot(keys[block(k + 1), :], query_t), dot(values[block(k + 1), :], grad_t))
+                if behind is not None:
+                    to, ds, pb = behind
+                    acc_q = acc_q + dot(keys_t[:, to], ds)
+                    acc_kv[to, :] += dot(jnp.concatenate([ds, pb], axis=1), sides)
+                if k < NBLK:
+                    col = seg_col[at, :]
+                    same = jnp.concatenate([col, col], axis=1) == seg_row
+                    p = jnp.exp2(jnp.where(same, s * SCALE2 - row_lse, NEG_LARGE))
+                    behind = (at, (p * (dp - delta)).astype(bf16), p.astype(bf16))
             acc_q = (acc_q * SCALE).astype(bf16)
             out_t[2 * j, m, :HEAD, :] = acc_q[:, :TOK]
             out_t[2 * j + 1, m, :HEAD, :] = acc_q[:, TOK:]
@@ -695,11 +752,10 @@
         for n in range(6)
     ]
     done = [task for tasks in TASKS.values() for task in tasks]
-    for phase in (0, 1):
-        for b in range(3):
-            for p in range(3):
-                if (phase, b, p) not in done:
-                    reduce(phase, p, b * COLS, COLS)
+    for phase in ("relay", 0, 1):
+        for p, b in EARLY:
+            if (phase, p, b) not in done:
+                run_task(phase, p, b)
     gives = []
     for m in range(MB):
         for copy in pushes[m]:
@@ -734,14 +790,13 @@
     give_vec.start()
     for copy in gives:
         copy.wait()
-    for p, at, width in blocks(3):
+    for p, at, width in late:
         if width == COLS:
-            multiply(p, 3)
+            multiply(p, at // COLS)
         else:
             give_vec.wait()
-            works[0][:, :, :, :, :, VEC_AT:] = (own_vec[...].astype(f32) + peer_vec[...].astype(f32)).astype(bf16)
-        for copy in copies(p, 0, at, width):
-            copy.start()
+            stores[3][0] = (own_vec[...].astype(f32) + peer_vec[...].astype(f32)).astype(bf16)
+        begin(p, at, width)
     for n in range(6):
         fetch_w[n].wait()
         part = dot_nt(right_q[:, n * COLS : (n + 1) * COLS], w_part[n % 2])
@@ -751,12 +806,13 @@
             out_x[...] += part
         if n < 4:
             fetch_w[n + 2].start()
-    for b in range(3):
-        for p, at, width in blocks(b):
-            reduce(2, p, at, width)
+    for piece in late:
+        relay(*piece)
+    for piece in early:
+        reduce(2, *piece)
     for phase in range(3):
-        for p, at, width in blocks(3):
-            reduce(phase, p, at, width)
+        for piece in late:
+            reduce(phase, *piece)
     squares = square_acc[...]
     yl, z = lax.axis_index("yl"), lax.axis_index("z")
     z_first, y_first = slice(0, HALF_Z), slice(HALF_Z, 6272)
@@ -827,11 +883,11 @@
     locals_ = []
     for c in range(2):
         for p in range(3):
-            for b in range(4):
-                i, col = PRODUCT[p][b]
+            for b in range(N_EARLY[p] + 1):
+                i, col = PRODUCT[(p, b)]
                 target, base = ((out_attn, 0), (out_attn, 3072), (out_ffn, 0), (out_ffn, FF))[i]
                 base = base + c * WIDTHS[i] + col
-                at = p * 2048 + b * COLS
+                at = PART_AT[p] + b * COLS
                 locals_.append(
                     pltpu.make_async_copy(
                         gathered.at[c, :, :, at : at + COLS], target.at[:, :, base : base + COLS],
@@ -855,10 +911,11 @@
         pltpu.VMEM((4, 2, 2, 4, 16, 128), bf16),
         pltpu.VMEM((4, 2, 2, 4, 16, 128), bf16),
     ]
-    for n in range(3):
-        scratch += [pltpu.VMEM((*lead(ORDERS[p], n), 16, PART_COLS[p]), bf16) for p in range(3)]
-    for n in range(1, 4):
-        scratch += [pltpu.VMEM((3, *lead(ORDERS[p], n), 16, PART_COLS[p]), bf16) for p in range(3)]
+    for kind in range(6):
+        n = kind if kind < 3 else kind - 2
+        for p, count, width in (*((p, N_EARLY[p] + 1, COLS) for p in range(3)), (0, 1, 128)):
+            landing = (3,) if kind >= 3 else ()
+            scratch.append(pltpu.VMEM((count, *landing, *lead(ORDERS[p], n), 16, width), bf16))
     scratch += [
         pltpu.VMEM((2, 8, 16, 6272), bf16),
         pltpu.VMEM((4, 8, 128), f32),
@@ -878,7 +935,7 @@
         pltpu.VMEM((8, 128), f32),
         pltpu.VMEM((2, D, COLS), bf16),
     ]
-    for count in (10, 10, 135, 135, 12, 12, 10, 10, 32, 32, 32, 32, 10, 25):
+    for count in (10, 10, 156, 156, 12, 12, 10, 10, 32, 32, 32, 32, 10, 25):
         scratch.append(pltpu.SemaphoreType.DMA((count,)))
     out = pl.pallas_call(
         back_kernel,

time: 287 us -> 277 us (0.965)
  Pallas kernels: 252 us -> 242 us
    pallas_call x1, Pallas kernels: 136 us -> 126 us  [back(): pl.pallas_call(back_kernel, in_specs=[vmem] * 4 + [hbm] * 3 + [vmem, vmem...]
where the time goes in v5:
time: 277 us; the launch traced here: 273 us
  Pallas kernels  242 us (87%)
  other arithmetic  21.8 us (8%)
  local copies, waits for them, and re-layouts  5.82 us (2%)
  between operations  3.1 us (1%)
    pallas_call x1, Pallas kernels, back(): pl.pallas_call(back_kernel, in_specs=[vmem] * 4 + [hbm] * 3 + [vmem, vmem...  126 us
    pallas_call x1, Pallas kernels, front(): pl.pallas_call(front_kernel, in_specs=[hbm, vmem, vmem, vmem, vmem, vmem]...  116 us
    convert_element_type x1, other arithmetic, shards(): ffn_new.astype(bf16)  8.81 us

profile of v5, /device:TPU:1, one launch (start us, length us, event | category | flops | bytes accessed | tf_op | source)
XLA Modules:
  0.0 272.6 jit_solution(9771802436949615901)
XLA Ops:
  0.6 0.0 copy-start.1
  0.7 1.8 dynamic-slice_convert_fusion.1
  2.5 0.4 copy-done.1
  2.9 0.0 copy-start.12
  2.9 0.0 copy-start.11
  2.9 0.0 copy-start.8
  3.0 1.3 pad_maximum_fusion.shard
  4.2 0.0 copy-done.12
  4.2 0.2 reduce_window_sum.14
  4.4 0.0 copy-done.11
  4.4 0.1 convert_reduce_fusion
  4.5 0.8 copy.33.keep_ref
  5.3 0.6 broadcast_in_dim.2.seg_ref
  5.9 0.0 copy-done.8
  5.9 0.6 pad.4.vec_shard
  6.5 116.4 %front.1 = (bf16[4,2,128,3072]{3,2,1,0:T(8,128)(2,1)}, bf16[16,2,208,128]{3,2,1,0:T(8,128)(2,1)}, f32[16,2,64,128]{3,2,1,0:T(8,128)}, f32[16,2,1,128]{3,2,1,0:T(...) custom-call(bf16[128,6144]{1,0:T(8,128)(2,1)} %pad_maximum_fusion.sh, ...), custom_call_target="tpu_custom_call" | custom-call | flops 13421772800 | bytes 33554432 | tf_op jit(solution)/shard_map/front/pallas_call | solution.py:448
  122.9 125.5 %back.1 = (bf16[8,16,4096]{2,1,0:T(8,128)(2,1)}, bf16[8,16,8192]{2,1,0:T(8,128)(2,1)}, bf16[8,16,128]{2,1,0:T(8,128)(2,1)}, f32[8,128]{1,0:T(8,128)}, f32[256,1024]{1,0:T(8,128)}) custom-call(bf16[1024,256]{1,0:T(8,128)(2,1)} %get-tuple-element.37.left_x, bf16[1024,256]{1,0:T(8,128)(2,1)} %get-tuple-element.38.left_o, ...), custom_call_target="tpu_custom_call" | custom-call | flops 11811160064 | bytes 16777216 | tf_op jit(solution)/shard_map/back/pallas_call | solution.py:940
  248.4 1.3 reduce_sum.19
  250.4 0.0 copy-start
  250.5 2.2 convert_multiply_fusion
  252.7 0.6 copy-done
  253.3 0.0 copy-start.9
  253.3 0.0 copy-start.10
  253.3 0.0 copy-start.6
  253.3 0.0 copy-start.3
  253.3 8.8 %fusion.7 = (bf16[128,8192]{1,0:T(8,128)(2,1)}, f32[128,8192]{1,0:T(8,128)}, f32[128,8192]{1,0:T(8,128)}, f32[128,8192]{1,0:T(8,128)}) fusion(f32[128,8192]{1,0:T(8,128)S(1)} %copy-done, f32[8,16,8192]{2,1,0:T(8,128)S(1)} %convert_multiply_fusion, f32[128,8192]{1,0:T(8,128)} %param.21, f32[128,8192]{1,0:T(8,128)} %param.22), kind=kLoop, calls=%fused_computation.28 | loop fusion | flops 16777216 | bytes 31457280 | tf_op jit(solution)/shard_map/convert_element_type | solution.py:1154
  262.1 0.0 copy-start.2
  262.1 0.0 copy-done.9
  262.1 0.0 copy-done.10
  262.1 1.5 multiply_subtract_fusion.2
  263.6 0.7 slice_convert_fusion
  264.2 0.5 fusion.6
  264.8 0.0 copy-done.6
  264.8 0.2 convert_multiply_fusion.1
  265.0 0.0 copy-done.3
  265.0 0.0 copy-done.2
  265.0 0.0 copy-start.4
  265.0 0.0 copy-start.5
  265.0 4.1 %fusion.10 = (bf16[128,4096]{1,0:T(8,128)(2,1)}, f32[128,4096]{1,0:T(8,128)}, f32[128,4096]{1,0:T(8,128)}, f32[128,4096]{1,0:T(8,128)}) fusion(f32[128,4096]{1,0:T(8,128)S(1)} %copy-done.1, f32[8,16,4096]{2,1,0:T(8,128)S(1)} %convert_multiply_fusion.1, f32[128,4096]{1,0:T(8,128)S(1)} %copy-done.2, f32[128,4096]{1,0:T(8,128)S(1)} %copy-done.3), kind=kLoop, calls=%fused_computation.29 | loop fusion | flops 8388608 | bytes 15728640 | tf_op jit(solution)/shard_map/convert_element_type | solution.py:1153
  269.2 0.0 copy-start.7
  269.2 0.0 copy-done.4
  269.2 0.0 copy-done.5
  269.2 0.9 add_convert_fusion
  270.1 0.1 copy-done.7
  270.2 0.8 copy.37
  (5 shorter events, 0.1 us)
Async XLA Ops:
  0.6 2.2 copy-start.1
  2.9 1.4 copy-start.12
  2.9 1.5 copy-start.11
  2.9 3.1 %copy-start.8 = (f32[12,128]{1,0:T(8,128)S(1)}, f32[12,128]{1,0:T(8,128)}, u32[]{:S(2)}) copy-start(f32[12,128]{1,0:T(8,128)} %param.23) | copy-start | bytes 18436
  250.4 2.8 %copy-start = (f32[128,8192]{1,0:T(8,128)S(1)}, f32[128,8192]{1,0:T(8,128)}, u32[]{:S(2)}) copy-start(f32[128,8192]{1,0:T(8,128)} %param.20) | copy-start | bytes 12582916
  253.3 8.8 %copy-start.9 = (f32[12,128]{1,0:T(8,128)S(1)}, f32[12,128]{1,0:T(8,128)}, u32[]{:S(2)}) copy-start(f32[12,128]{1,0:T(8,128)} %param.24) | copy-start | bytes 18436
  253.3 8.8 %copy-start.10 = (f32[12,128]{1,0:T(8,128)S(1)}, f32[12,128]{1,0:T(8,128)}, u32[]{:S(2)}) copy-start(f32[12,128]{1,0:T(8,128)} %param.25) | copy-start | bytes 18436
  253.3 11.5 %copy-start.6 = (bf16[8,16,4096]{2,1,0:T(8,128)(2,1)S(1)}, bf16[8,16,4096]{2,1,0:T(8,128)(2,1)}, u32[]{:S(2)}) copy-start(bf16[8,16,4096]{2,1,0:T(8,128)(2,1)} %get-tuple-element.52) | copy-start | bytes 3145732
  253.3 11.7 %copy-start.3 = (f32[128,4096]{1,0:T(8,128)S(1)}, f32[128,4096]{1,0:T(8,128)}, u32[]{:S(2)}) copy-start(f32[128,4096]{1,0:T(8,128)} %param.19) | copy-start | bytes 6291460
  262.1 2.9 %copy-start.2 = (f32[128,4096]{1,0:T(8,128)S(1)}, f32[128,4096]{1,0:T(8,128)}, u32[]{:S(2)}) copy-start(f32[128,4096]{1,0:T(8,128)} %param.18) | copy-start | bytes 6291460
  265.0 4.2 %copy-start.4 = (f32[256,1024]{1,0:T(8,128)S(1)}, f32[256,1024]{1,0:T(8,128)}, u32[]{:S(2)}) copy-start(f32[256,1024]{1,0:T(8,128)} %get-tuple-element.36) | copy-start | bytes 3145732
  265.0 4.2 %copy-start.5 = (f32[256,1024]{1,0:T(8,128)S(1)}, f32[256,1024]{1,0:T(8,128)}, u32[]{:S(2)}) copy-start(f32[256,1024]{1,0:T(8,128)} %get-tuple-element.50) | copy-start | bytes 3145732
  269.2 1.0 copy-start.7
